TPU v7x, 512 devices: a whole 4x4x16 slice. The times are simulated.
512 devices in a mesh: dp: 128 (over x_lo, z, y), head: 4 (over x_hi, core).
Axes of the slice: x: 4 (x_hi: 2, x_lo: 2; x = x_hi * 2 + x_lo), y: 4, z: 16, core: 2. Of those that a mesh axis runs over, the one named last changes fastest.
Arguments:
- prompt_kv: bfloat16 [2, 4096, 128], P(None, 'dp', 'head'), may hold values from -6 to 6
- resp_kv: bfloat16 [2, 49152, 128], P(None, 'dp', 'head'), may hold values from -6 to 6
- resp_query: bfloat16 [49152, 512], P('dp', 'head'), may hold values from -240 to 240
- resp_out: bfloat16 [49152, 512], P('dp', 'head'), may hold values from -6 to 6
- resp_dout: bfloat16 [49152, 512], P('dp', 'head'), may hold values from -6 to 6
- resp_lengths: int32 [4, 16], replicated, may hold values from 1 to 1536, 12288 in all within a row
- prompt_owner: int32 [128], replicated, may hold values from 0 to 127, each once
Outputs:
- query_grad: bfloat16 [49152, 512], P('dp', 'head')
- resp_kv_grad: bfloat16 [2, 49152, 128], P(None, 'dp', 'head')
- prompt_kv_grad: bfloat16 [2, 4096, 128], P(None, 'dp', 'head')
Inputs may be any that keep to these rules, and one draw needn't show every extreme that they name: `resp_lengths`: each group's lengths sum to 12288; the longest is 1536. `prompt_owner`: each piece number appears once.
All inputs are finite; a program needn't handle non-finite values.
Results may differ from a plain program's by a relative error of at most 0.018.
Values may be sent and summed in bfloat16 or wider, within the bound.
No kernel may reach another device: no remote copies, remote signals or barrier semaphores. Data moves between devices by JAX's collectives and lax.ppermute only.
A program may use at most 64 MiB of HBM per device.

v0:
```python
import jax
import jax.numpy as jnp
from jax import lax
from jax.sharding import PartitionSpec as P


def shifted(array, axis, by):
    size = lax.axis_size(axis)
    pairs = [(i, i + by) for i in range(size) if 0 <= i + by < size]
    return lax.ppermute(array, axis, pairs)


def response_ids(row_index, lengths, per_group):
    row_group = row_index // per_group
    offset = row_index % per_group
    bounds = jnp.cumsum(lengths, axis=1)
    group_count = lengths.shape[0]
    resp_count = lengths.shape[1]
    chosen = row_group[:, None] == jnp.arange(group_count, dtype=jnp.int32)[None, :]
    passed = offset[:, None, None] >= bounds[None, :, :]
    finished = jnp.sum(jnp.where(chosen[:, :, None] & passed, 1, 0), axis=(1, 2)).astype(jnp.int32)
    resp_index = row_group * resp_count + finished
    return jnp.where(row_index >= 0, resp_index, -1)


def score_block(queries, keys, allowed, factor):
    scores = jnp.einsum("rhd,pd->hrp", queries, keys, preferred_element_type=jnp.float32) * factor
    if allowed is None:
        return scores
    return jnp.where(allowed[None], scores, -jnp.inf)


def grad_block(queries, dout, row_dot, log_total, block_kv, allowed, factor):
    scores = score_block(queries, block_kv[0], allowed, factor)
    probs = jnp.exp(scores - log_total[..., None])
    value_dot = jnp.einsum("rhd,pd->hrp", dout, block_kv[1], preferred_element_type=jnp.float32)
    score_grad = (probs * (value_dot - row_dot[..., None])).astype(jnp.bfloat16)
    rounded = probs.astype(jnp.bfloat16)
    query_part = jnp.einsum(
        "hrp,pd->rhd", score_grad, block_kv[0], preferred_element_type=jnp.float32
    )
    key_terms = jnp.stack(
        [
            jnp.einsum("hrp,rhd->pd", score_grad, queries, preferred_element_type=jnp.float32)
            * factor,
            jnp.einsum("hrp,rhd->pd", rounded, dout, preferred_element_type=jnp.float32),
        ]
    )
    return (query_part, key_terms)


def body(prompt_kv, resp_kv, resp_query, resp_out, resp_dout, resp_lengths, prompt_owner):
    dp_devices = lax.axis_size("dp")
    own_index = lax.axis_index("dp")
    prompt_rows = prompt_kv.shape[1]
    resp_rows = resp_kv.shape[1]
    group_total = resp_lengths.shape[0]
    pieces_per_group = dp_devices // group_total
    reach_count = min(4, pieces_per_group - 1)
    own_group = own_index // pieces_per_group
    prompt_full, resp_full = (
        lax.all_gather(prompt_kv, "head", axis=2, tiled=True),
        lax.all_gather(resp_kv, "head", axis=2, tiled=True),
    )
    head_width = prompt_full.shape[2]
    factor = head_width ** (-0.5)
    every_prompt = lax.all_gather(prompt_full, "dp", axis=1, tiled=True)
    holders = jnp.nonzero(prompt_owner // pieces_per_group == own_group, size=pieces_per_group)[
        0
    ].astype(jnp.int32)
    picked = (
        holders[:, None] * prompt_rows + jnp.arange(prompt_rows, dtype=jnp.int32)[None, :]
    ).reshape(-1)
    group_kv = jnp.take(every_prompt, picked, axis=1)
    sources = [resp_full]
    for distance in range(1, reach_count + 1):
        sources.append(shifted(resp_full, "dp", distance))
    first_row = own_index * resp_rows
    query_rows = first_row + jnp.arange(resp_rows, dtype=jnp.int32)
    per_group = pieces_per_group * resp_rows
    query_ids = response_ids(query_rows, resp_lengths, per_group)
    masks = []
    for distance in range(reach_count + 1):
        key_rows = first_row - distance * resp_rows + jnp.arange(resp_rows, dtype=jnp.int32)
        key_ids = response_ids(key_rows, resp_lengths, per_group)
        masks.append(
            (query_ids[:, None] == key_ids[None, :]) & (key_rows[None, :] <= query_rows[:, None])
        )
    head_count = resp_query.shape[1] // head_width
    queries = resp_query.reshape(resp_rows, head_count, head_width)
    dout = resp_dout.reshape(resp_rows, head_count, head_width)
    saved_out = resp_out.reshape(resp_rows, head_count, head_width)
    prompt_scores = score_block(queries, group_kv[0], None, factor)
    row_max = jnp.max(prompt_scores, -1)
    row_sum = jnp.sum(jnp.exp(prompt_scores - row_max[..., None]), -1)
    for distance in range(reach_count + 1):
        scores = score_block(queries, sources[distance][0], masks[distance], factor)
        new_max = jnp.maximum(row_max, jnp.max(scores, -1))
        row_sum = row_sum * jnp.exp(row_max - new_max) + jnp.sum(
            jnp.exp(scores - new_max[..., None]), -1
        )
        row_max = new_max
    log_total = row_max + jnp.log(row_sum)
    row_dot = jnp.sum(dout.astype(jnp.float32) * saved_out.astype(jnp.float32), -1).T
    query_sums, prompt_terms = grad_block(queries, dout, row_dot, log_total, group_kv, None, factor)
    local_terms = []
    for distance in range(reach_count + 1):
        query_part, key_terms = grad_block(
            queries, dout, row_dot, log_total, sources[distance], masks[distance], factor
        )
        query_sums = query_sums + query_part
        local_terms.append(key_terms)
    query_grad = (
        (query_sums * factor).reshape(resp_rows, head_count * head_width).astype(jnp.bfloat16)
    )
    own_terms = local_terms[0]
    for distance in range(1, reach_count + 1):
        own_terms = own_terms + shifted(
            local_terms[distance].astype(jnp.bfloat16), "dp", -distance
        ).astype(jnp.float32)
    resp_grad = lax.psum_scatter(
        own_terms.astype(jnp.bfloat16), "head", scatter_dimension=2, tiled=True
    )
    narrow = lax.psum_scatter(
        prompt_terms.astype(jnp.bfloat16), "head", scatter_dimension=2, tiled=True
    ).astype(jnp.float32)
    spread = (
        jnp.zeros((2, every_prompt.shape[1], narrow.shape[2]), jnp.float32)
        .at[:, picked]
        .set(narrow)
    )
    prompt_grad = lax.psum_scatter(spread, "dp", scatter_dimension=1, tiled=True)
    return (query_grad, resp_grad, prompt_grad.astype(jnp.bfloat16))


def solution(mesh):
    in_specs = (
        P(None, "dp", "head"),
        P(None, "dp", "head"),
        P("dp", "head"),
        P("dp", "head"),
        P("dp", "head"),
        P(),
        P(),
    )
    out_specs = (P("dp", "head"), P(None, "dp", "head"), P(None, "dp", "head"))
    return jax.shard_map(body, mesh=mesh, in_specs=in_specs, out_specs=out_specs, check_vma=False)
```

profile of v0, /device:TPU:24, one launch (start us, length us, event | category | flops | bytes accessed | tf_op | source)
XLA Modules:
  0.0 1476.1 jit_solution(18095447637753275922)
XLA Ops:
  7.2 7.3 all_gather.11
  14.5 3.8 collective-permute-start.3
  18.4 4.0 collective-permute-start.2
  22.4 4.2 collective-permute-start.1
  26.6 4.1 collective-permute-start
  30.7 0.8 copy.62
  31.5 16.1 %all_gather.9 = bf16[2,32,128]{1,0,2:T(2,128)(2,1)S(1)} all-gather(bf16[2,32,32]{1,0,2:T(2,128)(2,1)S(1)} %copy.62), channel_id=1, replica_groups=mesh['dp'=128,'head'=4] {'head'}, dimensions={2}, use_global_device_ids=true | all-gather | bytes 20480 | tf_op jit(solution)/shard_map/all_gather | solution.py:62
  47.6 0.7 copy.63
  48.6 1.3 fusion.137
  50.3 1.4 scatter_custom_fusion
  52.0 0.7 fusion.133
  52.9 1.3 dynamic-slice.4
  54.2 1.3 dynamic-slice
  56.7 0.9 reduce_window_sum.30
  57.6 1.1 multiply_reduce_fusion
  59.7 0.3 copy-done.8
  60.4 0.4 copy-done.5
  61.1 0.4 copy-done.11
  61.7 565.0 %all-gather.2.cloned.1.call-done = bf16[2,4096,128]{2,0,1:T(2,128)(2,1)} async-done(((bf16[2,32,128]{2,0,1:T(2,128)(2,1)}), bf16[2,4096,128]{2,0,1:T(2,128)(2,1)}) %all-gather.2.cloned.1.call-update) | async-done | bytes 2097168 | tf_op jit(solution)/shard_map/all_gather | solution.py:67
  626.8 8.7 gather_fusion
  635.5 5.2 fusion.69
  640.7 0.7 fusion.138
  641.4 0.4 fusion.143
  644.3 0.4 fusion.43
  645.0 0.4 fusion.6
  645.8 0.4 fusion.44
  648.8 1.3 collective-permute-start.7
  650.1 0.7 pad_maximum_fusion.3
  650.8 5.4 collective-permute-start.6
  656.1 0.7 pad_maximum_fusion.2
  656.8 2.0 collective-permute-start.5
  658.9 0.7 pad_maximum_fusion.1
  659.6 2.3 collective-permute-start.4
  662.2 1.1 copy.70
  663.5 3.8 collective-permute-done.5
  667.3 2.2 collective-permute-done.4
  669.6 1.3 fusion.78
  670.9 0.8 copy.69
  672.5 0.8 copy.72
  673.2 52.3 %all-reduce.7.cloned.1.call-done = (bf16[2,384,128]{1,0,2:T(2,128)(2,1)}, bf16[2,1024,128]{1,0,2:T(2,128)(2,1)}) async-done(((bf16[2,384,128]{1,0,2:T(2,128)(2,1)}, bf16[2,1024,128]{1,0,2:T(2,128)(2,1)}), (bf16[2,384,128]{1,0,2:T(2,128)(2,1)}, bf16[2,1024,128]{1,0,2:T(2,128)(2,1)})) %all-reduce.7.cloned.1.call-update) | async-done | bytes 720912
  725.5 0.8 constant_dynamic-slice_fusion
  726.4 1.0 convert_bitcast_fusion
  727.4 0.6 copy.73
  728.0 0.5 copy.71
  728.5 2.9 broadcast_in_dim.59
  731.4 93.8 %scatter_fusion = f32[2,4096,32]{2,0,1:T(2,128)} fusion(f32[2,4096,32]{2,0,1:T(2,128)} %broadcast_in_dim.59, s32[1024]{0:T(1024)S(1)} %bitcast.348, f32[1024,2,32]{2,1,0:T(2,128)S(1)} %copy.71), kind=kCustom, calls=%fused_computation.2 | custom fusion | bytes 790528 | tf_op jit(solution)/shard_map/scatter | solution.py:130
  825.2 643.4 %all-reduce.8 = bf16[2,4096,32]{2,0,1:T(2,128)(2,1)S(1)} all-reduce(f32[2,4096,32]{2,0,1:T(2,128)} %scatter_fusion), channel_id=4, replica_groups=mesh['dp'=128,'head'=4] {'dp'}, use_global_device_ids=true, to_apply=%region_26.27.clone | all-reduce | flops 262144 | bytes 1572864
  1468.6 0.6 copy.74
  (106 shorter events, 9.7 us)
Async XLA Ops:
  7.2 51.9 %copy-start = (bf16[384,128]{1,0:T(8,128)(2,1)S(1)}, bf16[384,128]{1,0:T(8,128)(2,1)}, u32[]{:S(2)}) copy-start(bf16[384,128]{1,0:T(8,128)(2,1)} %param.9) | copy-start | bytes 294916
  7.2 619.6 %all-gather.2.cloned.1.call-start = ((), (), s32[]{:S(2)}) async-start(), calls=%async_computation | async-start | bytes 2113536 | tf_op jit(solution)/shard_map/all_gather | solution.py:67
  14.5 46.9 %collective-permute-start.3 = (bf16[2,384,128]{1,2,0:T(8,128)(2,1)S(1)}, bf16[2,384,128]{1,2,0:T(8,128)(2,1)S(1)}, u32[]{:S(2)}, u32[]{:S(2)}) collective-permute-start(bf16[2,384,128]{1,2,0:T(8,128)(2,1)S(1)} %all_gather.11), channel_id=1, source_target_pairs={{0,16},{4,20},{8,24},{12,28},{16,32},{20,36},{24,40},{28,44},{32,4... | collective-permute-start | bytes 589832 | tf_op jit(solution)/shard_map/ppermute | solution.py:10
  18.4 42.4 %collective-permute-start.2 = (bf16[2,384,128]{1,2,0:T(8,128)(2,1)S(1)}, bf16[2,384,128]{1,2,0:T(8,128)(2,1)S(1)}, u32[]{:S(2)}, u32[]{:S(2)}) collective-permute-start(bf16[2,384,128]{1,2,0:T(8,128)(2,1)S(1)} %all_gather.11), channel_id=1, source_target_pairs={{0,12},{4,16},{8,20},{12,24},{16,28},{20,32},{24,36},{28,40},{32,4... | collective-permute-start | bytes 589832 | tf_op jit(solution)/shard_map/ppermute | solution.py:10
  22.4 37.7 %collective-permute-start.1 = (bf16[2,384,128]{1,2,0:T(8,128)(2,1)S(1)}, bf16[2,384,128]{1,2,0:T(8,128)(2,1)S(1)}, u32[]{:S(2)}, u32[]{:S(2)}) collective-permute-start(bf16[2,384,128]{1,2,0:T(8,128)(2,1)S(1)} %all_gather.11), channel_id=1, source_target_pairs={{0,8},{4,12},{8,16},{12,20},{16,24},{20,28},{24,32},{28,36},{32,40... | collective-permute-start | bytes 589832 | tf_op jit(solution)/shard_map/ppermute | solution.py:10
  26.6 32.8 %collective-permute-start = (bf16[2,384,128]{1,2,0:T(8,128)(2,1)S(1)}, bf16[2,384,128]{1,2,0:T(8,128)(2,1)S(1)}, u32[]{:S(2)}, u32[]{:S(2)}) collective-permute-start(bf16[2,384,128]{1,2,0:T(8,128)(2,1)S(1)} %all_gather.11), channel_id=1, source_target_pairs={{0,4},{4,8},{8,12},{12,16},{16,20},{20,24},{24,28},{28,32},{32,36}... | collective-permute-start | bytes 589832 | tf_op jit(solution)/shard_map/ppermute | solution.py:10
  48.3 677.2 %all-reduce.7.cloned.1.call-start = ((), (), s32[]{:S(2)}) async-start(), calls=%async_computation.1 | async-start | bytes 1441792
  59.4 0.7 copy-start.8
  60.1 0.7 copy-start.5
  60.8 0.7 copy-start.11
  61.4 579.3 %copy-start.2 = (bf16[2,384,128]{1,2,0:T(8,128)(2,1)}, bf16[2,384,128]{1,2,0:T(8,128)(2,1)S(1)}, u32[]{:S(2)}) copy-start(bf16[2,384,128]{1,2,0:T(8,128)(2,1)S(1)} %collective-permute-done.3) | copy-start | bytes 589828
  642.1 0.9 copy-start.1
  645.4 0.9 copy-start.9
  645.8 1.1 copy-start.6
  646.3 1.1 copy-start.12
  646.9 1.1 copy-start.3
  648.8 14.8 collective-permute-start.7
  650.8 12.8 collective-permute-start.6
  656.8 6.5 copy-start.13
  656.8 10.5 collective-permute-start.5
  659.6 10.0 collective-permute-start.4
  663.3 8.5 copy-start.4
  663.5 8.5 copy-start.10
  670.9 1.3 copy-start.7
Sparse Core Ops, SparseCore 0:
  48.5 578.2 all-gather.1
  671.9 53.5 all-reduce.6
where the time goes:
time: 1490 us; the launch traced here: 1480 us
  blocking collectives  667 us (45%)
  waiting for transfers between devices  623 us (42%)
  local copies, waits for them, and re-layouts  117 us (8%)
  starting transfers between devices  27.2 us (2%)
  other arithmetic  16.9 us (1%)
  between operations  16 us (1%)
    unnamed x1, blocking collectives  643 us
    all_gather x1, waiting for transfers between devices, body(): every_prompt = lax.all_gather(prompt_full, 'dp', axis=1, tiled=True)  565 us
    scatter x1, local copies, waits for them, and re-layouts, body(): spread = jnp.zeros((2, every_prompt.shape[1], narrow.shape[2]), jnp.float...  93.8 us
    unnamed x3, waiting for transfers between devices  52.3 us
  transfers between devices with their start and end apart: 10, of which 4 were waited for; matrix products, arithmetic and copies ran while one was open for 1% of the time, Pallas kernels for 0%

commit v1 on v0

--- a/solution.py
+++ b/solution.py
@@ -8,6 +8,30 @@
     size = lax.axis_size(axis)
     pairs = [(i, i + by) for i in range(size) if 0 <= i + by < size]
     return lax.ppermute(array, axis, pairs)
+
+
+EXCHANGE_BITS = (32, 16, 8, 4, 2, 1, 64)
+
+
+def doubled(array, axis, bits):
+    size = lax.axis_size(axis)
+    for bit in bits:
+        other = lax.ppermute(array, axis, [(i, i ^ bit) for i in range(size)])
+        array = jnp.concatenate([array, other], axis=0)
+    return array
+
+
+def slot_offsets(bits):
+    slots = jnp.arange(1 << len(bits), dtype=jnp.int32)
+    offsets = jnp.zeros_like(slots)
+    for place, bit in enumerate(bits):
+        offsets = offsets + ((slots >> place) & 1) * bit
+    return offsets
+
+
+def head_summed(terms):
+    landed = lax.all_to_all(terms, "head", split_axis=0, concat_axis=0, tiled=True)
+    return jnp.sum(landed.astype(jnp.float32), axis=0)
 
 
 def response_ids(row_index, lengths, per_group):
@@ -58,20 +82,28 @@
     pieces_per_group = dp_devices // group_total
     reach_count = min(4, pieces_per_group - 1)
     own_group = own_index // pieces_per_group
-    prompt_full, resp_full = (
-        lax.all_gather(prompt_kv, "head", axis=2, tiled=True),
-        lax.all_gather(resp_kv, "head", axis=2, tiled=True),
+    resp_full = lax.all_gather(resp_kv, "head", axis=2, tiled=True)
+    head_size = lax.axis_size("head")
+    narrow_width = prompt_kv.shape[2]
+    head_width = resp_full.shape[2]
+    factor = head_width ** (-0.5)
+    pieces = doubled(prompt_kv.reshape(1, -1, 128), "dp", EXCHANGE_BITS)
+    slot_holder = own_index ^ slot_offsets(EXCHANGE_BITS)
+    all_holders = jnp.arange(dp_devices, dtype=jnp.int32)
+    slot_piece = jnp.sum(
+        jnp.where(slot_holder[:, None] == all_holders[None, :], prompt_owner[None, :], 0), axis=1
     )
-    head_width = prompt_full.shape[2]
-    factor = head_width ** (-0.5)
-    every_prompt = lax.all_gather(prompt_full, "dp", axis=1, tiled=True)
-    holders = jnp.nonzero(prompt_owner // pieces_per_group == own_group, size=pieces_per_group)[
-        0
-    ].astype(jnp.int32)
-    picked = (
-        holders[:, None] * prompt_rows + jnp.arange(prompt_rows, dtype=jnp.int32)[None, :]
-    ).reshape(-1)
-    group_kv = jnp.take(every_prompt, picked, axis=1)
+    own_pieces = own_group * pieces_per_group + jnp.arange(pieces_per_group, dtype=jnp.int32)
+    pick = (own_pieces[:, None] == slot_piece[None, :]).astype(jnp.bfloat16)
+    group_pieces = jnp.dot(
+        pick, pieces.reshape(dp_devices, -1), preferred_element_type=jnp.float32
+    ).astype(jnp.bfloat16)
+    gathered = lax.all_gather(group_pieces.reshape(-1, 128), "head", axis=0, tiled=False)
+    group_kv = (
+        gathered.reshape(head_size, pieces_per_group, 2, prompt_rows, narrow_width)
+        .transpose(2, 1, 3, 0, 4)
+        .reshape(2, pieces_per_group * prompt_rows, head_width)
+    )
     sources = [resp_full]
     for distance in range(1, reach_count + 1):
         sources.append(shifted(resp_full, "dp", distance))
@@ -118,19 +150,29 @@
         own_terms = own_terms + shifted(
             local_terms[distance].astype(jnp.bfloat16), "dp", -distance
         ).astype(jnp.float32)
-    resp_grad = lax.psum_scatter(
-        own_terms.astype(jnp.bfloat16), "head", scatter_dimension=2, tiled=True
+    resp_grad = head_summed(
+        own_terms.astype(jnp.bfloat16)
+        .reshape(2, resp_rows, head_size, narrow_width)
+        .transpose(2, 0, 1, 3)
+        .reshape(head_size, -1, 128)
+    ).reshape(2, resp_rows, narrow_width)
+    narrow = head_summed(
+        prompt_terms.astype(jnp.bfloat16)
+        .reshape(2, pieces_per_group, prompt_rows, head_size, narrow_width)
+        .transpose(3, 1, 0, 2, 4)
+        .reshape(head_size, -1, 128)
+    ).astype(jnp.bfloat16)
+    place = (prompt_owner[:, None] == own_pieces[None, :]).astype(jnp.bfloat16)
+    spread = jnp.dot(
+        place, narrow.reshape(pieces_per_group, -1), preferred_element_type=jnp.float32
+    ).astype(jnp.bfloat16)
+    landed = lax.all_to_all(
+        spread.reshape(dp_devices, -1, 128), "dp", split_axis=0, concat_axis=0, tiled=True
     )
-    narrow = lax.psum_scatter(
-        prompt_terms.astype(jnp.bfloat16), "head", scatter_dimension=2, tiled=True
-    ).astype(jnp.float32)
-    spread = (
-        jnp.zeros((2, every_prompt.shape[1], narrow.shape[2]), jnp.float32)
-        .at[:, picked]
-        .set(narrow)
+    prompt_grad = jnp.sum(landed.astype(jnp.float32), axis=0).reshape(
+        2, prompt_rows, narrow_width
     )
-    prompt_grad = lax.psum_scatter(spread, "dp", scatter_dimension=1, tiled=True)
-    return (query_grad, resp_grad, prompt_grad.astype(jnp.bfloat16))
+    return (query_grad, resp_grad.astype(jnp.bfloat16), prompt_grad.astype(jnp.bfloat16))
 
 
 def solution(mesh):

time: 1490 us -> 220 us (0.15)
  the two profiles are of different devices: /device:TPU:24 before, /device:TPU:32 now
where the time goes in v1:
time: 220 us; the launch traced here: 219 us
  starting transfers between devices  86.8 us (39%)
  waiting for transfers between devices  59.9 us (27%)
  local copies, waits for them, and re-layouts  27 us (12%)
  blocking collectives  16.8 us (8%)
  matrix products  16.2 us (7%)
  other arithmetic  10.1 us (5%)
    ppermute x7, starting transfers between devices, doubled(): other = lax.ppermute(array, axis, [(i, i ^ bit) for i in range(size)])  36.7 us
    all_to_all x1, waiting for transfers between devices, body(): lax.all_to_all(spread.reshape(dp_devices, -1, 128), 'dp', split_axis=0, c...  30.2 us
    ppermute x8, starting transfers between devices, shifted(): return lax.ppermute(array, axis, pairs)  27.1 us
    ppermute x7, waiting for transfers between devices, doubled(): other = lax.ppermute(array, axis, [(i, i ^ bit) for i in range(size)])  17.4 us
    all_to_all x1, starting transfers between devices, body(): lax.all_to_all(spread.reshape(dp_devices, -1, 128), 'dp', split_axis=0, c...  15.9 us
    all_to_all x2, waiting for transfers between devices, head_summed(): lax.all_to_all(terms, 'head', split_axis=0, concat_axis=0, tiled=True)  12.3 us
    all_gather x1, blocking collectives, body(): lax.all_gather(group_pieces.reshape(-1, 128), 'head', axis=0, tiled=False)  9.34 us
    all_gather x1, blocking collectives, body(): resp_full = lax.all_gather(resp_kv, 'head', axis=2, tiled=True)  7.45 us
  transfers between devices with their start and end apart: 18, of which 9 were waited for; matrix products, arithmetic and copies ran while one was open for 11% of the time, Pallas kernels for 0%

profile of v1, /device:TPU:32, one launch (start us, length us, event | category | flops | bytes accessed | tf_op | source)
XLA Modules:
  0.0 218.7 jit_solution(4050140115359160846)
XLA Ops:
  0.7 7.5 %all_gather.7 = bf16[2,384,128]{1,2,0:T(8,128)(2,1)S(1)} all-gather(bf16[2,384,32]{1,2,0:T(8,128)(2,1)} %param.8), channel_id=1, replica_groups=mesh['dp'=128,'head'=4] {'head'}, dimensions={2}, use_global_device_ids=true | all-gather | bytes 245760 | tf_op jit(solution)/shard_map/all_gather | solution.py:85
  8.1 3.8 %collective-permute-start.10 = (bf16[2,384,128]{1,2,0:T(8,128)(2,1)S(1)}, bf16[2,384,128]{1,2,0:T(8,128)(2,1)S(1)}, u32[]{:S(2)}, u32[]{:S(2)}) collective-permute-start(bf16[2,384,128]{1,2,0:T(8,128)(2,1)S(1)} %all_gather.7), channel_id=1, source_target_pairs={{0,16},{4,20},{8,24},{12,28},{16,32},{20,36},{24,40},{28,44},{32,4... | collective-permute-start | bytes 589832 | tf_op jit(solution)/shard_map/ppermute | solution.py:10
  11.9 4.9 %collective-permute-start.9 = (bf16[2,384,128]{1,2,0:T(8,128)(2,1)S(1)}, bf16[2,384,128]{1,2,0:T(8,128)(2,1)S(1)}, u32[]{:S(2)}, u32[]{:S(2)}) collective-permute-start(bf16[2,384,128]{1,2,0:T(8,128)(2,1)S(1)} %all_gather.7), channel_id=1, source_target_pairs={{0,12},{4,16},{8,20},{12,24},{16,28},{20,32},{24,36},{28,40},{32,4... | collective-permute-start | bytes 589832 | tf_op jit(solution)/shard_map/ppermute | solution.py:10
  16.9 3.9 %collective-permute-start.8 = (bf16[2,384,128]{1,2,0:T(8,128)(2,1)S(1)}, bf16[2,384,128]{1,2,0:T(8,128)(2,1)S(1)}, u32[]{:S(2)}, u32[]{:S(2)}) collective-permute-start(bf16[2,384,128]{1,2,0:T(8,128)(2,1)S(1)} %all_gather.7), channel_id=1, source_target_pairs={{0,8},{4,12},{8,16},{12,20},{16,24},{20,28},{24,32},{28,36},{32,40... | collective-permute-start | bytes 589832 | tf_op jit(solution)/shard_map/ppermute | solution.py:10
  20.8 2.9 %collective-permute-start.7 = (bf16[2,384,128]{1,2,0:T(8,128)(2,1)S(1)}, bf16[2,384,128]{1,2,0:T(8,128)(2,1)S(1)}, u32[]{:S(2)}, u32[]{:S(2)}) collective-permute-start(bf16[2,384,128]{1,2,0:T(8,128)(2,1)S(1)} %all_gather.7), channel_id=1, source_target_pairs={{0,4},{4,8},{8,12},{12,16},{16,20},{20,24},{24,28},{28,32},{32,36}... | collective-permute-start | bytes 589832 | tf_op jit(solution)/shard_map/ppermute | solution.py:10
  24.5 13.0 %collective-permute-start = (bf16[1,16,128]{2,1,0:T(8,128)(2,1)S(1)}, bf16[1,16,128]{2,1,0:T(8,128)(2,1)S(1)}, u32[]{:S(2)}, u32[]{:S(2)}) collective-permute-start(bf16[1,16,128]{2,1,0:T(8,128)(2,1)S(1)} %reshape.1213), channel_id=1, source_target_pairs={{0,128},{4,132},{8,136},{12,140},{16,144},{20,148},{24,152},{28,15... | collective-permute-start | bytes 12296 | tf_op jit(solution)/shard_map/ppermute | solution.py:19
  39.8 1.1 multiply_reduce_fusion
  42.1 5.7 %collective-permute-start.1 = (bf16[2,16,128]{2,1,0:T(8,128)(2,1)S(1)}, bf16[2,16,128]{2,1,0:T(8,128)(2,1)S(1)}, u32[]{:S(2)}, u32[]{:S(2)}) collective-permute-start(bf16[2,16,128]{2,1,0:T(8,128)(2,1)S(1)} %pad_maximum_fusion.6), channel_id=1, source_target_pairs={{0,64},{4,68},{8,72},{12,76},{16,80},{20,84},{24,88},{28,92},{32,9... | collective-permute-start | bytes 24584 | tf_op jit(solution)/shard_map/ppermute | solution.py:19
  47.8 3.7 %collective-permute-done.1 = bf16[2,16,128]{2,1,0:T(8,128)(2,1)S(1)} collective-permute-done((bf16[2,16,128]{2,1,0:T(8,128)(2,1)S(1)}, bf16[2,16,128]{2,1,0:T(8,128)(2,1)S(1)}, u32[]{:S(2)}, u32[]{:S(2)}) %collective-permute-start.1) | collective-permute-done | bytes 8224 | tf_op jit(solution)/shard_map/ppermute | solution.py:19
  51.5 3.4 %collective-permute-start.2 = (bf16[4,16,128]{2,1,0:T(8,128)(2,1)S(1)}, bf16[4,16,128]{2,1,0:T(8,128)(2,1)S(1)}, u32[]{:S(2)}, u32[]{:S(2)}) collective-permute-start(bf16[4,16,128]{2,1,0:T(8,128)(2,1)S(1)} %pad_maximum_fusion.5), channel_id=1, source_target_pairs={{0,32},{4,36},{8,40},{12,44},{16,48},{20,52},{24,56},{28,60},{32,0... | collective-permute-start | bytes 49160 | tf_op jit(solution)/shard_map/ppermute | solution.py:19
  54.9 3.1 %collective-permute-done.2 = bf16[4,16,128]{2,1,0:T(8,128)(2,1)S(1)} collective-permute-done((bf16[4,16,128]{2,1,0:T(8,128)(2,1)S(1)}, bf16[4,16,128]{2,1,0:T(8,128)(2,1)S(1)}, u32[]{:S(2)}, u32[]{:S(2)}) %collective-permute-start.2) | collective-permute-done | bytes 16416 | tf_op jit(solution)/shard_map/ppermute | solution.py:19
  58.0 2.9 %collective-permute-start.3 = (bf16[8,16,128]{2,1,0:T(8,128)(2,1)S(1)}, bf16[8,16,128]{2,1,0:T(8,128)(2,1)S(1)}, u32[]{:S(2)}, u32[]{:S(2)}) collective-permute-start(bf16[8,16,128]{2,1,0:T(8,128)(2,1)S(1)} %pad_maximum_fusion.4), channel_id=1, source_target_pairs={{0,16},{4,20},{8,24},{12,28},{16,0},{20,4},{24,8},{28,12},{32,48},... | collective-permute-start | bytes 98312 | tf_op jit(solution)/shard_map/ppermute | solution.py:19
  61.0 2.9 %collective-permute-done.3 = bf16[8,16,128]{2,1,0:T(8,128)(2,1)S(1)} collective-permute-done((bf16[8,16,128]{2,1,0:T(8,128)(2,1)S(1)}, bf16[8,16,128]{2,1,0:T(8,128)(2,1)S(1)}, u32[]{:S(2)}, u32[]{:S(2)}) %collective-permute-start.3) | collective-permute-done | bytes 32800 | tf_op jit(solution)/shard_map/ppermute | solution.py:19
  63.9 3.9 %collective-permute-start.4 = (bf16[16,16,128]{2,1,0:T(8,128)(2,1)S(1)}, bf16[16,16,128]{2,1,0:T(8,128)(2,1)S(1)}, u32[]{:S(2)}, u32[]{:S(2)}) collective-permute-start(bf16[16,16,128]{2,1,0:T(8,128)(2,1)S(1)} %get-tuple-element.34), channel_id=1, source_target_pairs={{0,8},{4,12},{8,0},{12,4},{16,24},{20,28},{24,16},{28,20},{32,40},... | collective-permute-start | bytes 196616 | tf_op jit(solution)/shard_map/ppermute | solution.py:19
  67.9 3.7 %collective-permute-done.4 = bf16[16,16,128]{2,1,0:T(8,128)(2,1)S(1)} collective-permute-done((bf16[16,16,128]{2,1,0:T(8,128)(2,1)S(1)}, bf16[16,16,128]{2,1,0:T(8,128)(2,1)S(1)}, u32[]{:S(2)}, u32[]{:S(2)}) %collective-permute-start.4) | collective-permute-done | bytes 65568 | tf_op jit(solution)/shard_map/ppermute | solution.py:19
  71.6 4.4 %collective-permute-start.5 = (bf16[32,16,128]{2,1,0:T(8,128)(2,1)S(1)}, bf16[32,16,128]{2,1,0:T(8,128)(2,1)S(1)}, u32[]{:S(2)}, u32[]{:S(2)}) collective-permute-start(bf16[32,16,128]{2,1,0:T(8,128)(2,1)S(1)} %get-tuple-element.31), channel_id=1, source_target_pairs={{0,4},{4,0},{8,12},{12,8},{16,20},{20,16},{24,28},{28,24},{32,36},... | collective-permute-start | bytes 393224 | tf_op jit(solution)/shard_map/ppermute | solution.py:19
  76.4 1.1 fusion.150
  77.5 1.4 collective-permute-done.5
  79.0 3.4 %collective-permute-start.6 = (bf16[64,16,128]{2,1,0:T(8,128)(2,1)S(1)}, bf16[64,16,128]{2,1,0:T(8,128)(2,1)S(1)}, u32[]{:S(2)}, u32[]{:S(2)}) collective-permute-start(bf16[64,16,128]{2,1,0:T(8,128)(2,1)S(1)} %constant_dynamic-update-slice_fusion.11), channel_id=1, source_target_pairs={{0,256},{4,260},{8,264},{12,268},{16,272},{20,276},{24,280},{28,28... | collective-permute-start | bytes 786440 | tf_op jit(solution)/shard_map/ppermute | solution.py:19
  82.4 1.1 fusion.149
  83.5 1.1 fusion.148
  84.7 2.5 %collective-permute-done.6 = bf16[64,16,128]{2,1,0:T(8,128)(2,1)S(1)} collective-permute-done((bf16[64,16,128]{2,1,0:T(8,128)(2,1)S(1)}, bf16[64,16,128]{2,1,0:T(8,128)(2,1)S(1)}, u32[]{:S(2)}, u32[]{:S(2)}) %collective-permute-start.6) | collective-permute-done | bytes 262176 | tf_op jit(solution)/shard_map/ppermute | solution.py:19
  87.8 9.3 %all_gather.6 = bf16[4,512,128]{2,1,0:T(8,128)(2,1)} all-gather(bf16[1,512,128]{2,1,0:T(8,128)(2,1)S(1)} %all_gather_reshape.3), channel_id=1, replica_groups=mesh['dp'=128,'head'=4] {'head'}, dimensions={0}, use_global_device_ids=true | all-gather | bytes 655360 | tf_op jit(solution)/shard_map/all_gather | solution.py:101
  97.1 2.6 %reshape.1214 = bf16[4,32,2,32,32]{4,3,2,1,0:T(8,128)(2,1)S(1)} reshape(bf16[4,512,128]{2,1,0:T(8,128)(2,1)} %all_gather.6) | data formatting | bytes 1048576 | tf_op jit(solution)/shard_map/reshape | solution.py:103
  99.8 1.8 fusion.147
  101.6 2.6 %copy.87 = bf16[1,32,32,4,32]{2,1,4,3,0:T(8,128)(2,1)S(1)} copy(bf16[1,32,32,4,32]{4,2,0,1,3:T(8,128)(2,1)} %get-tuple-element.29) | data formatting | bytes 524288 | tf_op jit(solution)/shard_map/slice | solution.py:64
  104.2 1.1 squeeze.48
  108.0 0.9 fusion.60
  108.9 0.9 fusion.61
  109.9 1.1 fusion.5
  111.0 3.3 %copy.88 = bf16[1,32,32,4,32]{2,1,4,3,0:T(8,128)(2,1)} copy(bf16[1,32,32,4,32]{4,2,0,1,3:T(8,128)(2,1)} %get-tuple-element.28) | data formatting | bytes 524288 | tf_op jit(solution)/shard_map/slice | solution.py:60
  114.3 2.9 %squeeze.54 = bf16[1024,128]{0,1:T(8,128)(2,1)} reshape(bf16[1,32,32,4,32]{2,1,4,3,0:T(8,128)(2,1)} %copy.88) | data formatting | bytes 524288 | tf_op jit(solution)/shard_map/squeeze | solution.py:60
  117.2 1.2 fusion.40
  118.5 1.2 fusion.41
  123.3 2.8 %collective-permute-start.14 = (bf16[2,384,128]{1,2,0:T(8,128)(2,1)}, bf16[2,384,128]{1,2,0:T(8,128)(2,1)}, u32[]{:S(2)}, u32[]{:S(2)}) collective-permute-start(bf16[2,384,128]{1,2,0:T(8,128)(2,1)} %pad_maximum_fusion.3), channel_id=1, source_target_pairs={{16,0},{20,4},{24,8},{28,12},{32,16},{36,20},{40,24},{44,28},{48,3... | collective-permute-start | bytes 589832 | tf_op jit(solution)/shard_map/ppermute | solution.py:10
  126.9 2.7 %collective-permute-start.13 = (bf16[2,384,128]{1,2,0:T(8,128)(2,1)}, bf16[2,384,128]{1,2,0:T(8,128)(2,1)}, u32[]{:S(2)}, u32[]{:S(2)}) collective-permute-start(bf16[2,384,128]{1,2,0:T(8,128)(2,1)} %pad_maximum_fusion.2), channel_id=1, source_target_pairs={{12,0},{16,4},{20,8},{24,12},{28,16},{32,20},{36,24},{40,28},{44,3... | collective-permute-start | bytes 589832 | tf_op jit(solution)/shard_map/ppermute | solution.py:10
  130.3 1.9 collective-permute-start.12
  133.0 4.1 %collective-permute-start.11 = (bf16[2,384,128]{1,2,0:T(8,128)(2,1)}, bf16[2,384,128]{1,2,0:T(8,128)(2,1)}, u32[]{:S(2)}, u32[]{:S(2)}) collective-permute-start(bf16[2,384,128]{1,2,0:T(8,128)(2,1)} %pad_maximum_fusion), channel_id=1, source_target_pairs={{4,0},{8,4},{12,8},{16,12},{20,16},{24,20},{28,24},{32,28},{36,32}... | collective-permute-start | bytes 589832 | tf_op jit(solution)/shard_map/ppermute | solution.py:10
  140.9 1.7 reshape.1230
  142.7 3.7 %all-to-all-start.1 = ((bf16[4,512,128]{2,1,0:T(8,128)(2,1)}), bf16[4,512,128]{2,1,0:T(8,128)(2,1)S(1)}, u32[]{:S(2)}, u32[]{:S(2)}) async-start(bf16[4,512,128]{2,1,0:T(8,128)(2,1)} %reshape.1230), calls=%async_computation.1 | async-start | bytes 1048576 | tf_op jit(solution)/shard_map/all_to_all | solution.py:33
  147.0 1.3 fusion.74
  148.8 1.1 reshape.1227
  149.8 6.9 %all-to-all-done.1 = bf16[4,512,128]{2,1,0:T(8,128)(2,1)S(1)} async-done(((bf16[4,512,128]{2,1,0:T(8,128)(2,1)}), bf16[4,512,128]{2,1,0:T(8,128)(2,1)S(1)}, u32[]{:S(2)}, u32[]{:S(2)}) %all-to-all-start.1) | async-done | bytes 524320 | tf_op jit(solution)/shard_map/all_to_all | solution.py:33
  156.8 3.4 %all-to-all-start = ((bf16[4,192,128]{2,1,0:T(8,128)(2,1)}), bf16[4,192,128]{2,1,0:T(8,128)(2,1)S(1)}, u32[]{:S(2)}, u32[]{:S(2)}) async-start(bf16[4,192,128]{2,1,0:T(8,128)(2,1)} %reshape.1227), calls=%async_computation | async-start | bytes 393216 | tf_op jit(solution)/shard_map/all_to_all | solution.py:33
  161.6 5.3 %all-to-all-done = bf16[4,192,128]{2,1,0:T(8,128)(2,1)S(1)} async-done(((bf16[4,192,128]{2,1,0:T(8,128)(2,1)}), bf16[4,192,128]{2,1,0:T(8,128)(2,1)S(1)}, u32[]{:S(2)}, u32[]{:S(2)}) %all-to-all-start) | async-done | bytes 196640 | tf_op jit(solution)/shard_map/all_to_all | solution.py:33
  167.6 15.9 %all-to-all-start.2 = ((bf16[128,16,128]{2,1,0:T(8,128)(2,1)}), bf16[128,16,128]{2,1,0:T(8,128)(2,1)S(1)}, u32[]{:S(2)}, u32[]{:S(2)}) async-start(bf16[128,16,128]{2,1,0:T(8,128)(2,1)} %bitcast.389), calls=%async_computation.2 | async-start | bytes 1048576 | tf_op jit(solution)/shard_map/all_to_all | solution.py:169
  183.5 1.2 convolution_bitcast_fusion.6
  187.6 30.2 %all-to-all-done.2 = bf16[128,16,128]{2,1,0:T(8,128)(2,1)S(1)} async-done(((bf16[128,16,128]{2,1,0:T(8,128)(2,1)}), bf16[128,16,128]{2,1,0:T(8,128)(2,1)S(1)}, u32[]{:S(2)}, u32[]{:S(2)}) %all-to-all-start.2) | async-done | bytes 524320 | tf_op jit(solution)/shard_map/all_to_all | solution.py:169
  (188 shorter events, 23.8 us)
Async XLA Ops:
  0.6 40.2 %copy-start = (bf16[384,128]{1,0:T(8,128)(2,1)S(1)}, bf16[384,128]{1,0:T(8,128)(2,1)}, u32[]{:S(2)}) copy-start(bf16[384,128]{1,0:T(8,128)(2,1)} %param.9) | copy-start | bytes 294916
  0.6 40.6 %copy-start.39 = (bf16[2,32,32]{2,1,0:T(8,128)(2,1)S(1)}, bf16[2,32,32]{2,1,0:T(8,128)(2,1)}, u32[]{:S(2)}) copy-start(bf16[2,32,32]{2,1,0:T(8,128)(2,1)} %param.7) | copy-start | bytes 12292
  0.7 40.6 %copy-start.1 = (bf16[384,128]{1,0:T(8,128)(2,1)S(1)}, bf16[384,128]{1,0:T(8,128)(2,1)}, u32[]{:S(2)}) copy-start(bf16[384,128]{1,0:T(8,128)(2,1)} %param.11) | copy-start | bytes 294916
  8.1 68.2 %copy-start.21 = (bf16[2,384,128]{1,2,0:T(8,128)(2,1)}, bf16[2,384,128]{1,2,0:T(8,128)(2,1)S(1)}, u32[]{:S(2)}) copy-start(bf16[2,384,128]{1,2,0:T(8,128)(2,1)S(1)} %all_gather.7) | copy-start | bytes 589828
  8.1 75.4 %collective-permute-start.10 = (bf16[2,384,128]{1,2,0:T(8,128)(2,1)S(1)}, bf16[2,384,128]{1,2,0:T(8,128)(2,1)S(1)}, u32[]{:S(2)}, u32[]{:S(2)}) collective-permute-start(bf16[2,384,128]{1,2,0:T(8,128)(2,1)S(1)} %all_gather.7), channel_id=1, source_target_pairs={{0,16},{4,20},{8,24},{12,28},{16,32},{20,36},{24,40},{28,44},{32,4... | collective-permute-start | bytes 589832 | tf_op jit(solution)/shard_map/ppermute | solution.py:10
  11.9 70.4 %collective-permute-start.9 = (bf16[2,384,128]{1,2,0:T(8,128)(2,1)S(1)}, bf16[2,384,128]{1,2,0:T(8,128)(2,1)S(1)}, u32[]{:S(2)}, u32[]{:S(2)}) collective-permute-start(bf16[2,384,128]{1,2,0:T(8,128)(2,1)S(1)} %all_gather.7), channel_id=1, source_target_pairs={{0,12},{4,16},{8,20},{12,24},{16,28},{20,32},{24,36},{28,40},{32,4... | collective-permute-start | bytes 589832 | tf_op jit(solution)/shard_map/ppermute | solution.py:10
  16.9 59.5 %collective-permute-start.8 = (bf16[2,384,128]{1,2,0:T(8,128)(2,1)S(1)}, bf16[2,384,128]{1,2,0:T(8,128)(2,1)S(1)}, u32[]{:S(2)}, u32[]{:S(2)}) collective-permute-start(bf16[2,384,128]{1,2,0:T(8,128)(2,1)S(1)} %all_gather.7), channel_id=1, source_target_pairs={{0,8},{4,12},{8,16},{12,20},{16,24},{20,28},{24,32},{28,36},{32,40... | collective-permute-start | bytes 589832 | tf_op jit(solution)/shard_map/ppermute | solution.py:10
  20.8 55.2 %collective-permute-start.7 = (bf16[2,384,128]{1,2,0:T(8,128)(2,1)S(1)}, bf16[2,384,128]{1,2,0:T(8,128)(2,1)S(1)}, u32[]{:S(2)}, u32[]{:S(2)}) collective-permute-start(bf16[2,384,128]{1,2,0:T(8,128)(2,1)S(1)} %all_gather.7), channel_id=1, source_target_pairs={{0,4},{4,8},{8,12},{12,16},{16,20},{20,24},{24,28},{28,32},{32,36}... | collective-permute-start | bytes 589832 | tf_op jit(solution)/shard_map/ppermute | solution.py:10
  24.5 17.6 %collective-permute-start = (bf16[1,16,128]{2,1,0:T(8,128)(2,1)S(1)}, bf16[1,16,128]{2,1,0:T(8,128)(2,1)S(1)}, u32[]{:S(2)}, u32[]{:S(2)}) collective-permute-start(bf16[1,16,128]{2,1,0:T(8,128)(2,1)S(1)} %reshape.1213), channel_id=1, source_target_pairs={{0,128},{4,132},{8,136},{12,140},{16,144},{20,148},{24,152},{28,15... | collective-permute-start | bytes 12296 | tf_op jit(solution)/shard_map/ppermute | solution.py:19
  41.2 76.0 %copy-start.2 = (f32[1,384,384]{1,2,0:T(8,128)}, f32[1,384,384]{1,2,0:T(8,128)S(1)}, u32[]{:S(2)}) copy-start(f32[1,384,384]{1,2,0:T(8,128)S(1)} %get-tuple-element.58) | copy-start | bytes 1769476
  42.1 9.4 %collective-permute-start.1 = (bf16[2,16,128]{2,1,0:T(8,128)(2,1)S(1)}, bf16[2,16,128]{2,1,0:T(8,128)(2,1)S(1)}, u32[]{:S(2)}, u32[]{:S(2)}) collective-permute-start(bf16[2,16,128]{2,1,0:T(8,128)(2,1)S(1)} %pad_maximum_fusion.6), channel_id=1, source_target_pairs={{0,64},{4,68},{8,72},{12,76},{16,80},{20,84},{24,88},{28,92},{32,9... | collective-permute-start | bytes 24584 | tf_op jit(solution)/shard_map/ppermute | solution.py:19
  51.5 6.5 %collective-permute-start.2 = (bf16[4,16,128]{2,1,0:T(8,128)(2,1)S(1)}, bf16[4,16,128]{2,1,0:T(8,128)(2,1)S(1)}, u32[]{:S(2)}, u32[]{:S(2)}) collective-permute-start(bf16[4,16,128]{2,1,0:T(8,128)(2,1)S(1)} %pad_maximum_fusion.5), channel_id=1, source_target_pairs={{0,32},{4,36},{8,40},{12,44},{16,48},{20,52},{24,56},{28,60},{32,0... | collective-permute-start | bytes 49160 | tf_op jit(solution)/shard_map/ppermute | solution.py:19
  58.0 5.8 %collective-permute-start.3 = (bf16[8,16,128]{2,1,0:T(8,128)(2,1)S(1)}, bf16[8,16,128]{2,1,0:T(8,128)(2,1)S(1)}, u32[]{:S(2)}, u32[]{:S(2)}) collective-permute-start(bf16[8,16,128]{2,1,0:T(8,128)(2,1)S(1)} %pad_maximum_fusion.4), channel_id=1, source_target_pairs={{0,16},{4,20},{8,24},{12,28},{16,0},{20,4},{24,8},{28,12},{32,48},... | collective-permute-start | bytes 98312 | tf_op jit(solution)/shard_map/ppermute | solution.py:19
  63.9 7.7 %collective-permute-start.4 = (bf16[16,16,128]{2,1,0:T(8,128)(2,1)S(1)}, bf16[16,16,128]{2,1,0:T(8,128)(2,1)S(1)}, u32[]{:S(2)}, u32[]{:S(2)}) collective-permute-start(bf16[16,16,128]{2,1,0:T(8,128)(2,1)S(1)} %get-tuple-element.34), channel_id=1, source_target_pairs={{0,8},{4,12},{8,0},{12,4},{16,24},{20,28},{24,16},{28,20},{32,40},... | collective-permute-start | bytes 196616 | tf_op jit(solution)/shard_map/ppermute | solution.py:19
  71.6 7.4 %collective-permute-start.5 = (bf16[32,16,128]{2,1,0:T(8,128)(2,1)S(1)}, bf16[32,16,128]{2,1,0:T(8,128)(2,1)S(1)}, u32[]{:S(2)}, u32[]{:S(2)}) collective-permute-start(bf16[32,16,128]{2,1,0:T(8,128)(2,1)S(1)} %get-tuple-element.31), channel_id=1, source_target_pairs={{0,4},{4,0},{8,12},{12,8},{16,20},{20,16},{24,28},{28,24},{32,36},... | collective-permute-start | bytes 393224 | tf_op jit(solution)/shard_map/ppermute | solution.py:19
  76.0 7.5 %copy-start.34 = (bf16[2,384,128]{1,2,0:T(8,128)(2,1)}, bf16[2,384,128]{1,2,0:T(8,128)(2,1)S(1)}, u32[]{:S(2)}) copy-start(bf16[2,384,128]{1,2,0:T(8,128)(2,1)S(1)} %collective-permute-done.7) | copy-start | bytes 589828
  76.4 2.6 %copy-start.28 = (bf16[2,384,128]{1,2,0:T(8,128)(2,1)}, bf16[2,384,128]{1,2,0:T(8,128)(2,1)S(1)}, u32[]{:S(2)}) copy-start(bf16[2,384,128]{1,2,0:T(8,128)(2,1)S(1)} %collective-permute-done.8) | copy-start | bytes 589828
  79.0 8.3 %collective-permute-start.6 = (bf16[64,16,128]{2,1,0:T(8,128)(2,1)S(1)}, bf16[64,16,128]{2,1,0:T(8,128)(2,1)S(1)}, u32[]{:S(2)}, u32[]{:S(2)}) collective-permute-start(bf16[64,16,128]{2,1,0:T(8,128)(2,1)S(1)} %constant_dynamic-update-slice_fusion.11), channel_id=1, source_target_pairs={{0,256},{4,260},{8,264},{12,268},{16,272},{20,276},{24,280},{28,28... | collective-permute-start | bytes 786440 | tf_op jit(solution)/shard_map/ppermute | solution.py:19
  82.4 4.9 %copy-start.36 = (bf16[2,384,128]{1,2,0:T(8,128)(2,1)}, bf16[2,384,128]{1,2,0:T(8,128)(2,1)S(1)}, u32[]{:S(2)}) copy-start(bf16[2,384,128]{1,2,0:T(8,128)(2,1)S(1)} %collective-permute-done.9) | copy-start | bytes 589828
  83.5 3.7 %copy-start.31 = (bf16[2,384,128]{1,2,0:T(8,128)(2,1)}, bf16[2,384,128]{1,2,0:T(8,128)(2,1)S(1)}, u32[]{:S(2)}) copy-start(bf16[2,384,128]{1,2,0:T(8,128)(2,1)S(1)} %collective-permute-done.10) | copy-start | bytes 589828
  105.8 1.3 copy-start.4
  117.2 3.5 %copy-start.5 = (f32[1,384,384]{1,2,0:T(8,128)S(1)}, f32[1,384,384]{1,2,0:T(8,128)}, u32[]{:S(2)}) copy-start(f32[1,384,384]{1,2,0:T(8,128)} %get-tuple-element.52) | copy-start | bytes 1769476
  117.2 3.5 %copy-start.29 = (bf16[2,384,128]{1,2,0:T(8,128)(2,1)S(1)}, bf16[2,384,128]{1,2,0:T(8,128)(2,1)}, u32[]{:S(2)}) copy-start(bf16[2,384,128]{1,2,0:T(8,128)(2,1)} %copy-done.28) | copy-start | bytes 589828
  118.5 2.9 %copy-start.7 = (f32[1,384,384]{1,2,0:T(8,128)S(1)}, f32[1,384,384]{1,2,0:T(8,128)}, u32[]{:S(2)}) copy-start(f32[1,384,384]{1,2,0:T(8,128)} %get-tuple-element.50) | copy-start | bytes 1769476
  118.5 2.9 %copy-start.37 = (bf16[2,384,128]{1,2,0:T(8,128)(2,1)S(1)}, bf16[2,384,128]{1,2,0:T(8,128)(2,1)}, u32[]{:S(2)}) copy-start(bf16[2,384,128]{1,2,0:T(8,128)(2,1)} %copy-done.36) | copy-start | bytes 589828
  120.8 1.2 copy-start.9
  121.1 1.3 copy-start.16
  121.4 4.8 %copy-start.26 = (bf16[1,384,128]{1,2,0:T(8,128)(2,1)S(1)}, bf16[1,384,128]{1,2,0:T(8,128)(2,1)}, u32[]{:S(2)}) copy-start(bf16[1,384,128]{1,2,0:T(8,128)(2,1)} %fusion.60) | copy-start | bytes 294916
  121.7 8.6 %copy-start.12 = (bf16[384,384]{0,1:T(8,128)(2,1)}, bf16[384,384]{0,1:T(8,128)(2,1)S(1)}, u32[]{:S(2)}) copy-start(bf16[384,384]{0,1:T(8,128)(2,1)S(1)} %fusion.43) | copy-start | bytes 884740
  122.0 15.1 %copy-start.20 = (bf16[1024,128]{0,1:T(8,128)(2,1)S(1)}, bf16[1024,128]{0,1:T(8,128)(2,1)}, u32[]{:S(2)}) copy-start(bf16[1024,128]{0,1:T(8,128)(2,1)} %squeeze.54) | copy-start | bytes 786436
  122.3 10.6 %copy-start.14 = (bf16[384,384]{0,1:T(8,128)(2,1)}, bf16[384,384]{0,1:T(8,128)(2,1)S(1)}, u32[]{:S(2)}) copy-start(bf16[384,384]{0,1:T(8,128)(2,1)S(1)} %fusion.44) | copy-start | bytes 884740
  123.3 23.7 %collective-permute-start.14 = (bf16[2,384,128]{1,2,0:T(8,128)(2,1)}, bf16[2,384,128]{1,2,0:T(8,128)(2,1)}, u32[]{:S(2)}, u32[]{:S(2)}) collective-permute-start(bf16[2,384,128]{1,2,0:T(8,128)(2,1)} %pad_maximum_fusion.3), channel_id=1, source_target_pairs={{16,0},{20,4},{24,8},{28,12},{32,16},{36,20},{40,24},{44,28},{48,3... | collective-permute-start | bytes 589832 | tf_op jit(solution)/shard_map/ppermute | solution.py:10
  126.9 20.1 %collective-permute-start.13 = (bf16[2,384,128]{1,2,0:T(8,128)(2,1)}, bf16[2,384,128]{1,2,0:T(8,128)(2,1)}, u32[]{:S(2)}, u32[]{:S(2)}) collective-permute-start(bf16[2,384,128]{1,2,0:T(8,128)(2,1)} %pad_maximum_fusion.2), channel_id=1, source_target_pairs={{12,0},{16,4},{20,8},{24,12},{28,16},{32,20},{36,24},{40,28},{44,3... | collective-permute-start | bytes 589832 | tf_op jit(solution)/shard_map/ppermute | solution.py:10
  130.3 16.7 %collective-permute-start.12 = (bf16[2,384,128]{1,2,0:T(8,128)(2,1)}, bf16[2,384,128]{1,2,0:T(8,128)(2,1)}, u32[]{:S(2)}, u32[]{:S(2)}) collective-permute-start(bf16[2,384,128]{1,2,0:T(8,128)(2,1)} %pad_maximum_fusion.1), channel_id=1, source_target_pairs={{8,0},{12,4},{16,8},{20,12},{24,16},{28,20},{32,24},{36,28},{40,32... | collective-permute-start | bytes 589832 | tf_op jit(solution)/shard_map/ppermute | solution.py:10
  133.0 14.1 %collective-permute-start.11 = (bf16[2,384,128]{1,2,0:T(8,128)(2,1)}, bf16[2,384,128]{1,2,0:T(8,128)(2,1)}, u32[]{:S(2)}, u32[]{:S(2)}) collective-permute-start(bf16[2,384,128]{1,2,0:T(8,128)(2,1)} %pad_maximum_fusion), channel_id=1, source_target_pairs={{4,0},{8,4},{12,8},{16,12},{20,16},{24,20},{28,24},{32,28},{36,32}... | collective-permute-start | bytes 589832 | tf_op jit(solution)/shard_map/ppermute | solution.py:10
  142.7 4.0 %copy-start.3 = (f32[1,384,384]{1,2,0:T(8,128)S(1)}, f32[1,384,384]{1,2,0:T(8,128)}, u32[]{:S(2)}) copy-start(f32[1,384,384]{1,2,0:T(8,128)} %copy-done.2) | copy-start | bytes 1769476
  142.7 14.1 %all-to-all-start.1 = ((bf16[4,512,128]{2,1,0:T(8,128)(2,1)}), bf16[4,512,128]{2,1,0:T(8,128)(2,1)S(1)}, u32[]{:S(2)}, u32[]{:S(2)}) async-start(bf16[4,512,128]{2,1,0:T(8,128)(2,1)} %reshape.1230), calls=%async_computation.1 | async-start | bytes 1048576 | tf_op jit(solution)/shard_map/all_to_all | solution.py:33
  148.4 11.9 %copy-start.40 = (s32[128]{0:T(128)S(1)}, s32[128]{0:T(128)}, u32[]{:S(2)}) copy-start(s32[128]{0:T(128)} %param.13) | copy-start | bytes 1540
  156.8 10.2 %all-to-all-start = ((bf16[4,192,128]{2,1,0:T(8,128)(2,1)}), bf16[4,192,128]{2,1,0:T(8,128)(2,1)S(1)}, u32[]{:S(2)}, u32[]{:S(2)}) async-start(bf16[4,192,128]{2,1,0:T(8,128)(2,1)} %reshape.1227), calls=%async_computation | async-start | bytes 393216 | tf_op jit(solution)/shard_map/all_to_all | solution.py:33
  160.2 23.3 %copy-start.13 = (bf16[384,384]{0,1:T(8,128)(2,1)S(1)}, bf16[384,384]{0,1:T(8,128)(2,1)}, u32[]{:S(2)}) copy-start(bf16[384,384]{0,1:T(8,128)(2,1)} %copy-done.12) | copy-start | bytes 884740
  160.3 24.4 %copy-start.15 = (bf16[384,384]{0,1:T(8,128)(2,1)S(1)}, bf16[384,384]{0,1:T(8,128)(2,1)}, u32[]{:S(2)}) copy-start(bf16[384,384]{0,1:T(8,128)(2,1)} %copy-done.14) | copy-start | bytes 884740
  160.3 24.4 %copy-start.33 = (bf16[2,384,128]{1,2,0:T(8,128)(2,1)S(1)}, bf16[2,384,128]{1,2,0:T(8,128)(2,1)}, u32[]{:S(2)}) copy-start(bf16[2,384,128]{1,2,0:T(8,128)(2,1)} %copy-done.31) | copy-start | bytes 589828
  160.7 24.3 %copy-start.19 = (bf16[1024,128]{0,1:T(8,128)(2,1)S(1)}, bf16[1024,128]{0,1:T(8,128)(2,1)}, u32[]{:S(2)}) copy-start(bf16[1024,128]{0,1:T(8,128)(2,1)} %copy-done.18) | copy-start | bytes 786436
  166.9 18.3 %copy-start.22 = (bf16[2,384,128]{1,2,0:T(8,128)(2,1)S(1)}, bf16[2,384,128]{1,2,0:T(8,128)(2,1)}, u32[]{:S(2)}) copy-start(bf16[2,384,128]{1,2,0:T(8,128)(2,1)} %copy-done.21) | copy-start | bytes 589828
  167.6 50.3 %all-to-all-start.2 = ((bf16[128,16,128]{2,1,0:T(8,128)(2,1)}), bf16[128,16,128]{2,1,0:T(8,128)(2,1)S(1)}, u32[]{:S(2)}, u32[]{:S(2)}) async-start(bf16[128,16,128]{2,1,0:T(8,128)(2,1)} %bitcast.389), calls=%async_computation.2 | async-start | bytes 1048576 | tf_op jit(solution)/shard_map/all_to_all | solution.py:169
  183.5 2.0 copy-start.11
  183.5 2.0 copy-start.35
  185.3 1.5 copy-start.24
  (11 other events, 11.2 us)

commit v2 on v0

v2 whole, which is shorter than its diff:
```python
import jax
import jax.numpy as jnp
import numpy as np
from jax import lax
from jax.experimental import pallas as pl
from jax.experimental.pallas import tpu as pltpu
from jax.sharding import Mesh
from jax.sharding import PartitionSpec as P

XLO, Z, Y, HEADS = 2, 16, 4, 4
DP = XLO * Z * Y
WIDTH = 128
PART = WIDTH // HEADS
PIECES = 32
PROWS = 32
TILE = 2 * PROWS * PART // WIDTH
RROWS = 384
HOPS = 4
PROMPT = PIECES * PROWS
PACKED = 2 * RROWS * PART // WIDTH
QUARTER = PROMPT // HEADS
FACTOR = WIDTH**-0.5
LOG2E = 1.4426950408889634
VMEM = pl.BlockSpec(memory_space=pltpu.VMEM)
SMEM = pl.BlockSpec(memory_space=pltpu.SMEM)
PARAMS = pltpu.CompilerParams(vmem_limit_bytes=32 * 1024 * 1024)


def swap_matrix():
    shape = (HEADS * WIDTH, HEADS * WIDTH)
    row = lax.broadcasted_iota(jnp.int32, shape, 0)
    col = lax.broadcasted_iota(jnp.int32, shape, 1)
    target = ((row >> 5) & 3) * WIDTH + (row >> 7) * PART + (row & 31)
    return jnp.where(target == col, 1.0, 0.0).astype(jnp.bfloat16)


def swapped(rows, swap):
    return jnp.dot(rows, swap, preferred_element_type=jnp.float32)


def select_kernel(slots, pieces, picked):
    for piece in range(PIECES):
        picked[piece] = pieces[slots[piece]]


def place_kernel(slots, landed, spread, own):
    spread[...] = jnp.zeros_like(spread)
    total = landed[0].astype(jnp.float32)
    for head in range(1, HEADS):
        total = total + landed[head].astype(jnp.float32)
    rounded = total[: PIECES * TILE].astype(jnp.bfloat16)
    for piece in range(PIECES):
        spread[slots[piece]] = rounded[piece * TILE : (piece + 1) * TILE]
    own[...] = total[PIECES * TILE :]


def attention_kernel(
    place, q, o, do, start, prompt, near0, near1, near2, near3, near4, dq, close, far, exps, keys, values
):
    swap = swap_matrix()
    columns = swapped(jnp.concatenate([prompt[c] for c in range(HEADS)], axis=1), swap)
    for quarter in range(HEADS):
        part = columns[:, quarter * WIDTH : (quarter + 1) * WIDTH].reshape(PIECES, 2, TILE // 2, WIDTH)
        rows = slice(quarter * QUARTER, (quarter + 1) * QUARTER)
        keys[rows] = part[:, 0].reshape(QUARTER, WIDTH).astype(jnp.bfloat16)
        values[rows] = part[:, 1].reshape(QUARTER, WIDTH).astype(jnp.bfloat16)
    for distance, near in enumerate((near0, near1, near2, near3, near4)):
        rows = slice(PROMPT + distance * RROWS, PROMPT + (distance + 1) * RROWS)
        keys[rows] = near[0].T
        values[rows] = near[1].T
    chunks = [(i * QUARTER, QUARTER, None) for i in range(HEADS)]
    chunks += [(PROMPT + d * RROWS, RROWS, d) for d in range(HOPS + 1)]
    queries, dout = q[...], do[...]
    queries_t, dout_t = queries.T, dout.T
    products = dout.astype(jnp.float32) * o[...].astype(jnp.float32)
    delta = jnp.sum(products.T, axis=0, keepdims=True)
    first = start[...]
    peak = jnp.full((1, RROWS), -jnp.inf, jnp.float32)
    for begin, count, distance in chunks:
        rows = slice(begin, begin + count)
        scores = jnp.dot(keys[rows], queries_t, preferred_element_type=jnp.float32) * (FACTOR * LOG2E)
        if distance is not None:
            at = lax.broadcasted_iota(jnp.int32, (count, RROWS), 0) - distance * RROWS
            allowed = at >= first
            if distance == 0:
                allowed &= at <= lax.broadcasted_iota(jnp.int32, (count, RROWS), 1)
            scores = jnp.where(allowed, scores, -jnp.inf)
        peak = jnp.maximum(peak, jnp.max(scores, axis=0, keepdims=True))
        exps[rows] = scores
    total = jnp.zeros((1, RROWS), jnp.float32)
    for begin, count, _ in chunks:
        rows = slice(begin, begin + count)
        raised = jnp.exp2(exps[rows] - peak)
        total = total + jnp.sum(raised, axis=0, keepdims=True)
        exps[rows] = raised
    scale = 1.0 / total
    dq_t = jnp.zeros((WIDTH, RROWS), jnp.float32)
    prompt_sums = []
    for begin, count, distance in chunks:
        rows = slice(begin, begin + count)
        probs = exps[rows] * scale
        value_dot = jnp.dot(values[rows], dout_t, preferred_element_type=jnp.float32)
        score_grad = (probs * (value_dot - delta)).astype(jnp.bfloat16)
        dk = jnp.dot(score_grad, queries, preferred_element_type=jnp.float32) * FACTOR
        dv = jnp.dot(probs.astype(jnp.bfloat16), dout, preferred_element_type=jnp.float32)
        dq_t = dq_t + lax.dot_general(
            keys[rows], score_grad, (((0,), (0,)), ((), ())), preferred_element_type=jnp.float32
        )
        if distance is None:
            pair = jnp.stack(
                [dk.reshape(PIECES, TILE // 2, WIDTH), dv.reshape(PIECES, TILE // 2, WIDTH)], axis=1
            )
            prompt_sums.append(pair.reshape(PIECES * TILE, WIDTH).astype(jnp.bfloat16))
            continue
        dk, dv = dk.astype(jnp.bfloat16), dv.astype(jnp.bfloat16)
        half = RROWS // 2
        wide = jnp.concatenate([dk[:half], dk[half:], dv[:half], dv[half:]], axis=1)
        split = swapped(wide, swap).astype(jnp.bfloat16)
        for head in range(HEADS):
            block = split[:, head * WIDTH : (head + 1) * WIDTH]
            if distance == 0:
                close[head, PIECES * TILE :] = block
            else:
                far[(place[0] + HOPS - distance) & (Y - 1), head] = block
    split = swapped(jnp.concatenate(prompt_sums, axis=1), swap).astype(jnp.bfloat16)
    for head in range(HEADS):
        close[head, : PIECES * TILE] = split[:, head * WIDTH : (head + 1) * WIDTH]
    dq[...] = (dq_t.T * FACTOR).astype(jnp.bfloat16)


def attention(place, q, o, do, start, prompt, near):
    half = jnp.bfloat16
    keys_total = PROMPT + (HOPS + 1) * RROWS
    return pl.pallas_call(
        attention_kernel,
        out_shape=(
            jax.ShapeDtypeStruct((RROWS, WIDTH), half),
            jax.ShapeDtypeStruct((HEADS, PIECES * TILE + PACKED, WIDTH), half),
            jax.ShapeDtypeStruct((Y, HEADS, PACKED, WIDTH), half),
        ),
        in_specs=[SMEM] + [VMEM] * (5 + HOPS + 1),
        out_specs=(VMEM, VMEM, VMEM),
        scratch_shapes=[
            pltpu.VMEM((keys_total, RROWS), jnp.float32),
            pltpu.VMEM((keys_total, WIDTH), half),
            pltpu.VMEM((keys_total, WIDTH), half),
        ],
        compiler_params=PARAMS,
        cost_estimate=pl.CostEstimate(
            flops=12 * keys_total * RROWS * WIDTH, bytes_accessed=6_000_000, transcendentals=keys_total * RROWS
        ),
        name="attention",
    )(place, q, o, do, start, prompt, *near)


def select(slots, pieces):
    return pl.pallas_call(
        select_kernel,
        out_shape=jax.ShapeDtypeStruct((PIECES, TILE, WIDTH), jnp.bfloat16),
        in_specs=[SMEM, VMEM],
        out_specs=VMEM,
        compiler_params=PARAMS,
        name="select",
    )(slots, pieces)


def place_pieces(slots, landed):
    return pl.pallas_call(
        place_kernel,
        out_shape=(
            jax.ShapeDtypeStruct((DP, TILE, WIDTH), jnp.bfloat16),
            jax.ShapeDtypeStruct((PACKED, WIDTH), jnp.float32),
        ),
        in_specs=[SMEM, VMEM],
        out_specs=(VMEM, VMEM),
        compiler_params=PARAMS,
        name="place",
    )(slots, landed)


def exchanged(blocks, axes):
    return lax.all_to_all(blocks, axes, split_axis=0, concat_axis=0, tiled=True)


def given_to_all(block, axes):
    count = lax.axis_size(axes)
    return exchanged(jnp.broadcast_to(block[None], (count,) + block.shape), axes)


def shifted(array, by):
    pairs = [(i, i + by) for i in range(DP) if 0 <= i + by < DP]
    return lax.ppermute(array, ("xlo", "z", "y"), pairs)


def body(prompt_kv, resp_kv, resp_query, resp_out, resp_dout, resp_lengths, prompt_owner):
    half = jnp.bfloat16
    xlo, z, y = lax.axis_index("xlo"), lax.axis_index("z"), lax.axis_index("y")
    own_index = (xlo * Z + z) * Y + y
    own_group = own_index // PIECES

    along_z = given_to_all(prompt_kv.reshape(TILE, WIDTH), "z")
    resp_full = lax.all_gather(resp_kv.transpose(0, 2, 1), "head", axis=1, tiled=True)
    near = [resp_full] + [shifted(resp_full, d) for d in range(1, HOPS + 1)]
    pieces = given_to_all(along_z.reshape(Z * TILE, WIDTH), ("xlo", "y")).reshape(DP, TILE, WIDTH)

    holder = jnp.arange(DP, dtype=jnp.int32)
    slot = ((holder // (Z * Y)) * Y + holder % Y) * Z + (holder // Y) % Z
    own_pieces = own_group * PIECES + jnp.arange(PIECES, dtype=jnp.int32)
    slots = jnp.sum(
        jnp.where(own_pieces[:, None] == prompt_owner[None, :], slot[None, :], 0), axis=1
    ).astype(jnp.int32)
    picked = select(slots, pieces).reshape(PIECES * TILE, WIDTH)
    prompt = lax.all_gather(picked, "head", axis=0, tiled=False)

    offset = (own_index % PIECES) * RROWS + jnp.arange(RROWS, dtype=jnp.int32)
    lengths = jnp.sum(
        jnp.where(jnp.arange(resp_lengths.shape[0])[:, None] == own_group, resp_lengths, 0), axis=0
    )
    count = lengths.shape[0]
    earlier = jnp.arange(count)[None, :] <= jnp.arange(count)[:, None]
    bounds = jnp.sum(jnp.where(earlier, lengths[None, :], 0), axis=1)
    begun = jnp.max(jnp.where(bounds[:, None] <= offset[None, :], bounds[:, None], 0), axis=0)
    start = (begun - (own_index % PIECES) * RROWS).astype(jnp.int32)[None, :]

    place = jnp.reshape(y, (1,)).astype(jnp.int32)
    query_grad, close, far = attention(
        place, resp_query, resp_out, resp_dout, start, prompt, near
    )

    landed = exchanged(close, "head")
    far_landed = exchanged(far.reshape(Y * HEADS, PACKED, WIDTH), ("y", "head"))
    spread, own_sum = place_pieces(slots, landed)
    by_column = exchanged(spread.reshape(XLO * Y, Z * TILE, WIDTH), ("xlo", "y"))
    column_sum = jnp.sum(by_column.astype(jnp.float32), axis=0).astype(half)
    by_z = exchanged(column_sum.reshape(Z, TILE, WIDTH), "z")
    prompt_grad = jnp.sum(by_z.astype(jnp.float32), axis=0).astype(half)

    sender_sums = far_landed.reshape(Y, HEADS, PACKED, WIDTH).astype(jnp.float32)
    after = (jnp.arange(Y) > y)[:, None, None, None]
    same_plane = jnp.sum(jnp.where(after, sender_sums, 0.0), axis=(0, 1))
    plane_before = jnp.sum(jnp.where(after, 0.0, sender_sums), axis=(0, 1)).astype(half)
    from_plane_after = shifted(plane_before, -Y).astype(jnp.float32)
    resp_total = (own_sum + same_plane + from_plane_after).astype(half)
    resp_grad = resp_total.reshape(PACKED, HEADS, PART).transpose(1, 0, 2).reshape(2, RROWS, PART)
    return query_grad, resp_grad, prompt_grad.reshape(2, PROWS, PART)


def solution(mesh):
    fine = Mesh(np.asarray(mesh.devices).reshape(XLO, Z, Y, HEADS), ("xlo", "z", "y", "head"))
    dp = ("xlo", "z", "y")
    in_specs = (
        P(None, dp, "head"),
        P(None, dp, "head"),
        P(dp, "head"),
        P(dp, "head"),
        P(dp, "head"),
        P(),
        P(),
    )
    out_specs = (P(dp, "head"), P(None, dp, "head"), P(None, dp, "head"))
    return jax.shard_map(body, mesh=fine, in_specs=in_specs, out_specs=out_specs, check_vma=False)
```

time: 1490 us -> 146 us (0.10)
  blocking collectives: 667 us -> 31.9 us
  waiting for transfers between devices: 623 us -> 46.7 us
  local copies, waits for them, and re-layouts: 117 us -> 4.09 us
  starting transfers between devices: 27.2 us -> 50 us
  between operations: 16 us -> 0.86 us
    unnamed x1 -> x0, blocking collectives: 643 us -> none
    all_gather x1 -> x0, waiting for transfers between devices: 565 us -> none  [body(): every_prompt = lax.all_gather(prompt_full, 'dp', axis=1, tiled=True)]
    scatter x1 -> x0, local copies, waits for them, and re-layouts: 93.8 us -> none  [body(): spread = jnp.zeros((2, every_prompt.shape[1], narrow.shape[2]), jnp.float...]
    unnamed x3 -> x0, waiting for transfers between devices: 52.3 us -> none
    all_to_all x0 -> x5, waiting for transfers between devices: none -> 46.7 us  [exchanged(): return lax.all_to_all(blocks, axes, split_axis=0, concat_axis=0, tiled=True)]
    all_to_all x0 -> x5, starting transfers between devices: none -> 33.8 us  [exchanged(): return lax.all_to_all(blocks, axes, split_axis=0, concat_axis=0, tiled=True)]
    all_to_all x0 -> x1, blocking collectives: none -> 15.9 us  [exchanged(): return lax.all_to_all(blocks, axes, split_axis=0, concat_axis=0, tiled=True)]
  transfers between devices with their start and end apart: 10 -> 10, of which waited for: 4 -> 5; matrix products, arithmetic and copies ran while one was open for 1% -> 4% of each run, Pallas kernels for 0% -> 1%
where the time goes in v2:
time: 146 us; the launch traced here: 144 us
  starting transfers between devices  50 us (34%)
  waiting for transfers between devices  46.7 us (32%)
  blocking collectives  31.9 us (22%)
  Pallas kernels  8.32 us (6%)
  local copies, waits for them, and re-layouts  4.09 us (3%)
  other arithmetic  2.27 us (2%)
    all_to_all x5, waiting for transfers between devices, exchanged(): return lax.all_to_all(blocks, axes, split_axis=0, concat_axis=0, tiled=True)  46.7 us
    all_to_all x5, starting transfers between devices, exchanged(): return lax.all_to_all(blocks, axes, split_axis=0, concat_axis=0, tiled=True)  33.8 us
    ppermute x5, starting transfers between devices, shifted(): return lax.ppermute(array, ('xlo', 'z', 'y'), pairs)  16.2 us
    all_to_all x1, blocking collectives, exchanged(): return lax.all_to_all(blocks, axes, split_axis=0, concat_axis=0, tiled=True)  15.9 us
    all_gather x1, blocking collectives, body(): prompt = lax.all_gather(picked, 'head', axis=0, tiled=False)  8.7 us
    all_gather x1, blocking collectives, body(): lax.all_gather(resp_kv.transpose(0, 2, 1), 'head', axis=1, tiled=True)  7.32 us
    pallas_call x1, Pallas kernels, attention(): pl.pallas_call(attention_kernel, out_shape=(jax.ShapeDtypeStruct((RROWS,...  6.3 us
  transfers between devices with their start and end apart: 10, of which 5 were waited for; matrix products, arithmetic and copies ran while one was open for 4% of the time, Pallas kernels for 1%

profile of v2, /device:TPU:24, one launch (start us, length us, event | category | flops | bytes accessed | tf_op | source)
XLA Modules:
  0.0 144.2 jit_solution(9481285611672576027)
XLA Ops:
  0.6 7.3 %all_gather.7.near0 = bf16[2,128,384]{2,1,0:T(8,128)(2,1)S(1)} all-gather(bf16[2,32,384]{2,1,0:T(8,128)(2,1)} %bitcast.17), channel_id=1, replica_groups=mesh['xlo'=2,'z'=16,'y'=4,'head'=4] {'head'}, dimensions={1}, use_global_device_ids=true | all-gather | bytes 245760 | tf_op jit(solution)/shard_map/all_gather | solution.py:202
  8.0 3.5 %collective-permute-start = (bf16[2,128,384]{2,1,0:T(8,128)(2,1)S(1)}, bf16[2,128,384]{2,1,0:T(8,128)(2,1)S(1)}, u32[]{:S(2)}, u32[]{:S(2)}) collective-permute-start(bf16[2,128,384]{2,1,0:T(8,128)(2,1)S(1)} %all_gather.7.near0), channel_id=1, source_target_pairs={{0,4},{4,8},{8,12},{12,16},{16,20},{20,24},{24,28},{28,32},{32,36}... | collective-permute-start | bytes 589832 | tf_op jit(solution)/shard_map/ppermute | solution.py:192
  11.4 4.5 %collective-permute-start.1 = (bf16[2,128,384]{2,1,0:T(8,128)(2,1)S(1)}, bf16[2,128,384]{2,1,0:T(8,128)(2,1)S(1)}, u32[]{:S(2)}, u32[]{:S(2)}) collective-permute-start(bf16[2,128,384]{2,1,0:T(8,128)(2,1)S(1)} %all_gather.7.near0), channel_id=1, source_target_pairs={{0,8},{4,12},{8,16},{12,20},{16,24},{20,28},{24,32},{28,36},{32,40... | collective-permute-start | bytes 589832 | tf_op jit(solution)/shard_map/ppermute | solution.py:192
  15.9 3.1 %collective-permute-start.2 = (bf16[2,128,384]{2,1,0:T(8,128)(2,1)S(1)}, bf16[2,128,384]{2,1,0:T(8,128)(2,1)S(1)}, u32[]{:S(2)}, u32[]{:S(2)}) collective-permute-start(bf16[2,128,384]{2,1,0:T(8,128)(2,1)S(1)} %all_gather.7.near0), channel_id=1, source_target_pairs={{0,12},{4,16},{8,20},{12,24},{16,28},{20,32},{24,36},{28,40},{32,4... | collective-permute-start | bytes 589832 | tf_op jit(solution)/shard_map/ppermute | solution.py:192
  19.1 3.8 %collective-permute-start.3 = (bf16[2,128,384]{2,1,0:T(8,128)(2,1)S(1)}, bf16[2,128,384]{2,1,0:T(8,128)(2,1)S(1)}, u32[]{:S(2)}, u32[]{:S(2)}) collective-permute-start(bf16[2,128,384]{2,1,0:T(8,128)(2,1)S(1)} %all_gather.7.near0), channel_id=1, source_target_pairs={{0,16},{4,20},{8,24},{12,28},{16,32},{20,36},{24,40},{28,44},{32,4... | collective-permute-start | bytes 589832 | tf_op jit(solution)/shard_map/ppermute | solution.py:192
  22.9 0.8 broadcast_in_dim.103
  23.7 0.6 broadcast_in_dim.104
  24.3 12.5 %all-to-all-start = ((bf16[16,16,128]{2,1,0:T(8,128)(2,1)}), bf16[16,16,128]{2,1,0:T(8,128)(2,1)S(1)}, u32[]{:S(2)}, u32[]{:S(2)}) async-start(bf16[16,16,128]{2,1,0:T(8,128)(2,1)} %broadcast_in_dim.104), calls=%async_computation | async-start | bytes 131072 | tf_op jit(solution)/shard_map/all_to_all | solution.py:182
  36.9 0.8 select_reduce_fusion.3
  37.7 0.1 select_reduce_fusion.2
  37.8 0.1 select_reduce_fusion
  37.9 11.9 %all-to-all-done = bf16[16,16,128]{2,1,0:T(8,128)(2,1)S(1)} async-done(((bf16[16,16,128]{2,1,0:T(8,128)(2,1)}), bf16[16,16,128]{2,1,0:T(8,128)(2,1)S(1)}, u32[]{:S(2)}, u32[]{:S(2)}) %all-to-all-start) | async-done | bytes 65568 | tf_op jit(solution)/shard_map/all_to_all | solution.py:182
  49.7 0.0 copy-start.3
  49.7 0.9 broadcast_in_dim.106
  50.6 6.3 %all-to-all-start.1 = ((bf16[8,256,128]{2,1,0:T(8,128)(2,1)}), bf16[8,256,128]{2,1,0:T(8,128)(2,1)S(1)}, u32[]{:S(2)}, u32[]{:S(2)}) async-start(bf16[8,256,128]{2,1,0:T(8,128)(2,1)} %broadcast_in_dim.106), calls=%async_computation.1 | async-start | bytes 1048576 | tf_op jit(solution)/shard_map/all_to_all | solution.py:182
  56.9 0.0 copy-start
  57.0 0.0 copy-done.3
  57.0 0.2 select_reduce_fusion.1.slots
  57.2 5.8 %all-to-all-done.1 = bf16[8,256,128]{2,1,0:T(8,128)(2,1)S(1)} async-done(((bf16[8,256,128]{2,1,0:T(8,128)(2,1)}), bf16[8,256,128]{2,1,0:T(8,128)(2,1)S(1)}, u32[]{:S(2)}, u32[]{:S(2)}) %all-to-all-start.1) | async-done | bytes 524320 | tf_op jit(solution)/shard_map/all_to_all | solution.py:182
  63.0 0.6 select.33
  63.6 8.7 %all_gather.6.prompt = bf16[4,512,128]{2,1,0:T(8,128)(2,1)S(1)} all-gather(bf16[1,512,128]{2,1,0:T(8,128)(2,1)S(1)} %bitcast.14), channel_id=1, replica_groups=mesh['xlo'=2,'z'=16,'y'=4,'head'=4] {'head'}, dimensions={0}, use_global_device_ids=true | all-gather | bytes 655360 | tf_op jit(solution)/shard_map/all_gather | solution.py:213
  72.3 0.0 collective-permute-done.near1
  72.3 0.0 collective-permute-done.1.near2
  72.3 0.0 collective-permute-done.2.near3
  72.3 0.0 collective-permute-done.3.near4
  72.3 0.0 copy-done
  72.3 0.0 copy-done.1
  72.3 0.0 copy-done.2
  72.4 6.3 %attention.1 = (bf16[384,128]{1,0:T(8,128)(2,1)}, bf16[4,704,128]{2,1,0:T(8,128)(2,1)S(1)}, bf16[4,4,192,128]{3,2,1,0:T(8,128)(2,1)}) custom-call(s32[1]{0:T(128)} %bitcast.place, bf16[384,128]{1,0:T(8,128)(2,1)S(1)} %copy-done, bf16[384,128]{1,0:T(8,128)(2,1)S(1)} %copy-done.1, bf16[384,128]{1,0:T(8,128)(2,1)S(1)} %copy-done.2, s32[1,384]{1,0:T(1,128)S(1)} %sub.30.start, ...), custom_call_target="tpu_custom_call" | custom-call | flops 1736441856 | bytes 6000000 | tf_op jit(solution)/shard_map/attention/pallas_call | solution.py:134
  78.6 15.9 %all_to_all.30.landed = bf16[4,704,128]{2,1,0:T(8,128)(2,1)S(1)} all-to-all(bf16[4,704,128]{2,1,0:T(8,128)(2,1)S(1)} %get-tuple-element.9), channel_id=1, replica_groups=mesh['xlo'=2,'z'=16,'y'=4,'head'=4] {'head'}, dimensions={0} | all-to-all | bytes 1441792 | tf_op jit(solution)/shard_map/all_to_all | solution.py:182
  94.5 5.7 %all-to-all-start.3 = ((bf16[16,192,128]{2,1,0:T(8,128)(2,1)}), bf16[16,192,128]{2,1,0:T(8,128)(2,1)S(1)}, u32[]{:S(2)}, u32[]{:S(2)}) async-start(bf16[16,192,128]{2,1,0:T(8,128)(2,1)} %bitcast.5), calls=%async_computation.3 | async-start | bytes 1572864 | tf_op jit(solution)/shard_map/all_to_all | solution.py:182
  100.2 1.5 %place.1 = (bf16[128,16,128]{2,1,0:T(8,128)(2,1)}, f32[192,128]{1,0:T(8,128)S(1)}) custom-call(s32[32]{0:T(128)S(1)} %select_reduce_fusion.1.slots, bf16[4,704,128]{2,1,0:T(8,128)(2,1)S(1)} %all_to_all.30.landed), custom_call_target="tpu_custom_call" | custom-call | tf_op jit(solution)/shard_map/place/pallas_call | solution.py:168
  101.7 11.4 %all-to-all-done.3 = bf16[16,192,128]{2,1,0:T(8,128)(2,1)S(1)} async-done(((bf16[16,192,128]{2,1,0:T(8,128)(2,1)}), bf16[16,192,128]{2,1,0:T(8,128)(2,1)S(1)}, u32[]{:S(2)}, u32[]{:S(2)}) %all-to-all-start.3) | async-done | bytes 786464 | tf_op jit(solution)/shard_map/all_to_all | solution.py:182
  113.1 5.8 %all-to-all-start.4 = ((bf16[8,256,128]{2,1,0:T(8,128)(2,1)}), bf16[8,256,128]{2,1,0:T(8,128)(2,1)S(1)}, u32[]{:S(2)}, u32[]{:S(2)}) async-start(bf16[8,256,128]{2,1,0:T(8,128)(2,1)} %bitcast.8), calls=%async_computation.4 | async-start | bytes 1048576 | tf_op jit(solution)/shard_map/all_to_all | solution.py:182
  118.9 0.1 broadcast_in_dim.107
  119.0 0.1 broadcast_in_dim.108
  119.1 0.4 fusion
  119.4 1.3 collective-permute-start.4
  120.7 5.7 %all-to-all-done.4 = bf16[8,256,128]{2,1,0:T(8,128)(2,1)S(1)} async-done(((bf16[8,256,128]{2,1,0:T(8,128)(2,1)}), bf16[8,256,128]{2,1,0:T(8,128)(2,1)S(1)}, u32[]{:S(2)}, u32[]{:S(2)}) %all-to-all-start.4) | async-done | bytes 524320 | tf_op jit(solution)/shard_map/all_to_all | solution.py:182
  126.5 0.7 reduce_sum.74
  127.1 3.5 %all-to-all-start.5 = ((bf16[16,16,128]{2,1,0:T(8,128)(2,1)}), bf16[16,16,128]{2,1,0:T(8,128)(2,1)S(1)}, u32[]{:S(2)}, u32[]{:S(2)}) async-start(bf16[16,16,128]{2,1,0:T(8,128)(2,1)} %bitcast.9), calls=%async_computation.5 | async-start | bytes 131072 | tf_op jit(solution)/shard_map/all_to_all | solution.py:182
  130.7 0.0 collective-permute-done.4
  130.7 0.1 copy.16
  130.8 0.1 copy.17
  130.9 0.1 reshape.111
  131.0 0.6 copy.18
  131.6 11.8 %all-to-all-done.5 = bf16[16,16,128]{2,1,0:T(8,128)(2,1)S(1)} async-done(((bf16[16,16,128]{2,1,0:T(8,128)(2,1)}), bf16[16,16,128]{2,1,0:T(8,128)(2,1)S(1)}, u32[]{:S(2)}, u32[]{:S(2)}) %all-to-all-start.5) | async-done | bytes 65568 | tf_op jit(solution)/shard_map/all_to_all | solution.py:182
  143.5 0.7 reshape.114
  (11 shorter events, 0.1 us)
Async XLA Ops:
  8.0 64.4 %collective-permute-start = (bf16[2,128,384]{2,1,0:T(8,128)(2,1)S(1)}, bf16[2,128,384]{2,1,0:T(8,128)(2,1)S(1)}, u32[]{:S(2)}, u32[]{:S(2)}) collective-permute-start(bf16[2,128,384]{2,1,0:T(8,128)(2,1)S(1)} %all_gather.7.near0), channel_id=1, source_target_pairs={{0,4},{4,8},{8,12},{12,16},{16,20},{20,24},{24,28},{28,32},{32,36}... | collective-permute-start | bytes 589832 | tf_op jit(solution)/shard_map/ppermute | solution.py:192
  11.4 60.9 %collective-permute-start.1 = (bf16[2,128,384]{2,1,0:T(8,128)(2,1)S(1)}, bf16[2,128,384]{2,1,0:T(8,128)(2,1)S(1)}, u32[]{:S(2)}, u32[]{:S(2)}) collective-permute-start(bf16[2,128,384]{2,1,0:T(8,128)(2,1)S(1)} %all_gather.7.near0), channel_id=1, source_target_pairs={{0,8},{4,12},{8,16},{12,20},{16,24},{20,28},{24,32},{28,36},{32,40... | collective-permute-start | bytes 589832 | tf_op jit(solution)/shard_map/ppermute | solution.py:192
  15.9 56.4 %collective-permute-start.2 = (bf16[2,128,384]{2,1,0:T(8,128)(2,1)S(1)}, bf16[2,128,384]{2,1,0:T(8,128)(2,1)S(1)}, u32[]{:S(2)}, u32[]{:S(2)}) collective-permute-start(bf16[2,128,384]{2,1,0:T(8,128)(2,1)S(1)} %all_gather.7.near0), channel_id=1, source_target_pairs={{0,12},{4,16},{8,20},{12,24},{16,28},{20,32},{24,36},{28,40},{32,4... | collective-permute-start | bytes 589832 | tf_op jit(solution)/shard_map/ppermute | solution.py:192
  19.1 53.3 %collective-permute-start.3 = (bf16[2,128,384]{2,1,0:T(8,128)(2,1)S(1)}, bf16[2,128,384]{2,1,0:T(8,128)(2,1)S(1)}, u32[]{:S(2)}, u32[]{:S(2)}) collective-permute-start(bf16[2,128,384]{2,1,0:T(8,128)(2,1)S(1)} %all_gather.7.near0), channel_id=1, source_target_pairs={{0,16},{4,20},{8,24},{12,28},{16,32},{20,36},{24,40},{28,44},{32,4... | collective-permute-start | bytes 589832 | tf_op jit(solution)/shard_map/ppermute | solution.py:192
  24.3 25.4 %all-to-all-start = ((bf16[16,16,128]{2,1,0:T(8,128)(2,1)}), bf16[16,16,128]{2,1,0:T(8,128)(2,1)S(1)}, u32[]{:S(2)}, u32[]{:S(2)}) async-start(bf16[16,16,128]{2,1,0:T(8,128)(2,1)} %broadcast_in_dim.104), calls=%async_computation | async-start | bytes 131072 | tf_op jit(solution)/shard_map/all_to_all | solution.py:182
  49.7 7.3 %copy-start.3 = (s32[128]{0:T(128)S(1)}, s32[128]{0:T(128)}, u32[]{:S(2)}) copy-start(s32[128]{0:T(128)} %param.13) | copy-start | bytes 1540
  50.6 12.4 %all-to-all-start.1 = ((bf16[8,256,128]{2,1,0:T(8,128)(2,1)}), bf16[8,256,128]{2,1,0:T(8,128)(2,1)S(1)}, u32[]{:S(2)}, u32[]{:S(2)}) async-start(bf16[8,256,128]{2,1,0:T(8,128)(2,1)} %broadcast_in_dim.106), calls=%async_computation.1 | async-start | bytes 1048576 | tf_op jit(solution)/shard_map/all_to_all | solution.py:182
  56.9 15.4 %copy-start = (bf16[384,128]{1,0:T(8,128)(2,1)S(1)}, bf16[384,128]{1,0:T(8,128)(2,1)}, u32[]{:S(2)}) copy-start(bf16[384,128]{1,0:T(8,128)(2,1)} %q.1) | copy-start | bytes 294916
  56.9 15.4 %copy-start.1 = (bf16[384,128]{1,0:T(8,128)(2,1)S(1)}, bf16[384,128]{1,0:T(8,128)(2,1)}, u32[]{:S(2)}) copy-start(bf16[384,128]{1,0:T(8,128)(2,1)} %o.1) | copy-start | bytes 294916
  56.9 15.4 %copy-start.2 = (bf16[384,128]{1,0:T(8,128)(2,1)S(1)}, bf16[384,128]{1,0:T(8,128)(2,1)}, u32[]{:S(2)}) copy-start(bf16[384,128]{1,0:T(8,128)(2,1)} %do.1) | copy-start | bytes 294916
  94.5 18.6 %all-to-all-start.3 = ((bf16[16,192,128]{2,1,0:T(8,128)(2,1)}), bf16[16,192,128]{2,1,0:T(8,128)(2,1)S(1)}, u32[]{:S(2)}, u32[]{:S(2)}) async-start(bf16[16,192,128]{2,1,0:T(8,128)(2,1)} %bitcast.5), calls=%async_computation.3 | async-start | bytes 1572864 | tf_op jit(solution)/shard_map/all_to_all | solution.py:182
  113.1 13.4 %all-to-all-start.4 = ((bf16[8,256,128]{2,1,0:T(8,128)(2,1)}), bf16[8,256,128]{2,1,0:T(8,128)(2,1)S(1)}, u32[]{:S(2)}, u32[]{:S(2)}) async-start(bf16[8,256,128]{2,1,0:T(8,128)(2,1)} %bitcast.8), calls=%async_computation.4 | async-start | bytes 1048576 | tf_op jit(solution)/shard_map/all_to_all | solution.py:182
  119.4 11.2 %collective-permute-start.4 = (bf16[192,128]{1,0:T(8,128)(2,1)S(1)}, bf16[192,128]{1,0:T(8,128)(2,1)S(1)}, u32[]{:S(2)}, u32[]{:S(2)}) collective-permute-start(bf16[192,128]{1,0:T(8,128)(2,1)S(1)} %get-tuple-element.23), channel_id=1, source_target_pairs={{16,0},{20,4},{24,8},{28,12},{32,16},{36,20},{40,24},{44,28},{48,3... | collective-permute-start | bytes 147464 | tf_op jit(solution)/shard_map/ppermute | solution.py:192
  127.1 16.3 %all-to-all-start.5 = ((bf16[16,16,128]{2,1,0:T(8,128)(2,1)}), bf16[16,16,128]{2,1,0:T(8,128)(2,1)S(1)}, u32[]{:S(2)}, u32[]{:S(2)}) async-start(bf16[16,16,128]{2,1,0:T(8,128)(2,1)} %bitcast.9), calls=%async_computation.5 | async-start | bytes 131072 | tf_op jit(solution)/shard_map/all_to_all | solution.py:182

commit v3 on v2

v3 whole, which is shorter than its diff:
```python
import jax
import jax.numpy as jnp
import numpy as np
from jax import lax
from jax.experimental import pallas as pl
from jax.experimental.pallas import tpu as pltpu
from jax.sharding import Mesh
from jax.sharding import PartitionSpec as P

XLO, Z, Y, HEADS = 2, 16, 4, 4
PLANES = XLO * Z
DP = PLANES * Y
WIDTH = 128
PART = WIDTH // HEADS
PIECES = 32
PROWS = 32
TILE = 2 * PROWS * PART // WIDTH
RROWS = 384
HOPS = 4
PROMPT = PIECES * PROWS
QUARTER = PROMPT // HEADS
FACTOR = WIDTH**-0.5
LOG2E = 1.4426950408889634
VMEM = pl.BlockSpec(memory_space=pltpu.VMEM)
SMEM = pl.BlockSpec(memory_space=pltpu.SMEM)
PARAMS = pltpu.CompilerParams(vmem_limit_bytes=32 * 1024 * 1024)


def swap_matrix():
    shape = (HEADS * WIDTH, HEADS * WIDTH)
    row = lax.broadcasted_iota(jnp.int32, shape, 0)
    col = lax.broadcasted_iota(jnp.int32, shape, 1)
    target = ((row >> 5) & 3) * WIDTH + (row >> 7) * PART + (row & 31)
    return jnp.where(target == col, 1.0, 0.0).astype(jnp.bfloat16)


def swapped(rows, swap):
    return jnp.dot(rows, swap, preferred_element_type=jnp.float32)


def fan_kernel(place, shares, own, other1, other2, other3, fanned, near):
    for column in range(Y):
        fanned[column] = shares[...]
    for step, part in enumerate((own, other1, other2, other3)):
        near[place[0] ^ step] = part[...]


def select_kernel(slots, pieces, picked):
    for piece in range(PIECES):
        picked[piece * TILE : (piece + 1) * TILE] = pieces[slots[piece]]


def place_kernel(slots, landed, spread):
    spread[...] = jnp.zeros_like(spread)
    total = landed[0].astype(jnp.float32)
    for head in range(1, HEADS):
        total = total + landed[head].astype(jnp.float32)
    rounded = total.astype(jnp.bfloat16)
    for piece in range(PIECES):
        spread[slots[piece]] = rounded[piece * TILE : (piece + 1) * TILE]


def column_kernel(landed, total):
    held = landed[0].astype(jnp.float32)
    for column in range(1, Y):
        held = held + landed[column].astype(jnp.float32)
    total[...] = held.astype(total.dtype)


def combine_kernel(place, own, far1, far2, far3, far4, mine, out1, out2, out3, slots):
    total = own[...]
    for far in (far1, far2, far3, far4):
        total = total + far[...].astype(jnp.float32)
    turned = [total[kind].T.astype(jnp.bfloat16) for kind in range(2)]
    for head in range(HEADS):
        for kind in range(2):
            slots[head, kind * PART : (kind + 1) * PART] = turned[kind][head * PART : (head + 1) * PART]
    for step, out in enumerate((mine, out1, out2, out3)):
        out[...] = slots[place[0] ^ step]


def attention_kernel(
    q, o, do, start, gathered, near0, near1, near2, near3, near4, dq, close, own, far1, far2, far3, far4, exps, keys, values
):
    swap = swap_matrix()
    packed = jnp.concatenate([gathered[c, : PIECES * TILE] for c in range(HEADS)], axis=1)
    columns = swapped(packed, swap)
    for quarter in range(HEADS):
        part = columns[:, quarter * WIDTH : (quarter + 1) * WIDTH].reshape(PIECES, 2, TILE // 2, WIDTH)
        rows = slice(quarter * QUARTER, (quarter + 1) * QUARTER)
        keys[rows] = part[:, 0].reshape(QUARTER, WIDTH).astype(jnp.bfloat16)
        values[rows] = part[:, 1].reshape(QUARTER, WIDTH).astype(jnp.bfloat16)
    for distance, near in enumerate((near0, near1, near2, near3, near4)):
        rows = slice(PROMPT + distance * RROWS, PROMPT + (distance + 1) * RROWS)
        for held, shift in ((keys, 0), (values, PART)):
            turned = [near[c, shift : shift + PART] for c in range(HEADS)]
            held[rows] = jnp.concatenate(turned, axis=0).T
    chunks = [(i * QUARTER, QUARTER, None) for i in range(HEADS)]
    chunks += [(PROMPT + d * RROWS, RROWS, d) for d in range(HOPS + 1)]
    queries, dout = q[...], do[...]
    queries_t, dout_t = queries.T, dout.T
    products = dout.astype(jnp.float32) * o[...].astype(jnp.float32)
    delta = jnp.sum(products.T, axis=0, keepdims=True)
    first = start[...]
    peak = jnp.full((1, RROWS), -jnp.inf, jnp.float32)
    for begin, count, distance in chunks:
        rows = slice(begin, begin + count)
        scores = jnp.dot(keys[rows], queries_t, preferred_element_type=jnp.float32) * (FACTOR * LOG2E)
        if distance is not None:
            at = lax.broadcasted_iota(jnp.int32, (count, RROWS), 0) - distance * RROWS
            allowed = at >= first
            if distance == 0:
                allowed &= at <= lax.broadcasted_iota(jnp.int32, (count, RROWS), 1)
            scores = jnp.where(allowed, scores, -jnp.inf)
        peak = jnp.maximum(peak, jnp.max(scores, axis=0, keepdims=True))
        exps[rows] = scores
    total = jnp.zeros((1, RROWS), jnp.float32)
    for begin, count, _ in chunks:
        rows = slice(begin, begin + count)
        raised = jnp.exp2(exps[rows] - peak)
        total = total + jnp.sum(raised, axis=0, keepdims=True)
        exps[rows] = raised
    scale = 1.0 / total
    dq_t = jnp.zeros((WIDTH, RROWS), jnp.float32)
    prompt_sums = []
    for begin, count, distance in chunks:
        rows = slice(begin, begin + count)
        probs = exps[rows] * scale
        value_dot = jnp.dot(values[rows], dout_t, preferred_element_type=jnp.float32)
        score_grad = (probs * (value_dot - delta)).astype(jnp.bfloat16)
        dk = jnp.dot(score_grad, queries, preferred_element_type=jnp.float32) * FACTOR
        dv = jnp.dot(probs.astype(jnp.bfloat16), dout, preferred_element_type=jnp.float32)
        dq_t = dq_t + lax.dot_general(
            keys[rows], score_grad, (((0,), (0,)), ((), ())), preferred_element_type=jnp.float32
        )
        if distance is None:
            pair = jnp.stack(
                [dk.reshape(PIECES, TILE // 2, WIDTH), dv.reshape(PIECES, TILE // 2, WIDTH)], axis=1
            )
            prompt_sums.append(pair.reshape(PIECES * TILE, WIDTH).astype(jnp.bfloat16))
            continue
        out = (own, far1, far2, far3, far4)[distance]
        out[0] = dk.astype(out.dtype)
        out[1] = dv.astype(out.dtype)
    split = swapped(jnp.concatenate(prompt_sums, axis=1), swap).astype(jnp.bfloat16)
    for head in range(HEADS):
        close[head] = split[:, head * WIDTH : (head + 1) * WIDTH]
    dq[...] = (dq_t.T * FACTOR).astype(jnp.bfloat16)


def local_call(kernel, name, shapes, operands, scratch=(), cost=None):
    scalars = sum(operand.ndim == 1 for operand in operands)
    arrays = len(operands) - scalars
    return pl.pallas_call(
        kernel,
        out_shape=[jax.ShapeDtypeStruct(shape, dtype) for shape, dtype in shapes],
        in_specs=[SMEM] * scalars + [VMEM] * arrays,
        out_specs=[VMEM] * len(shapes),
        scratch_shapes=scratch,
        compiler_params=PARAMS,
        cost_estimate=cost,
        name=name,
    )(*operands)


def attention(q, o, do, start, gathered, near):
    half = jnp.bfloat16
    total = PROMPT + (HOPS + 1) * RROWS
    block = (2, RROWS, WIDTH)
    shapes = [((RROWS, WIDTH), half), ((HEADS, PIECES * TILE, WIDTH), half), (block, jnp.float32)]
    return local_call(
        attention_kernel,
        "attention",
        shapes + [(block, half)] * HOPS,
        (q, o, do, start, gathered, *near),
        [
            pltpu.VMEM((total, RROWS), jnp.float32),
            pltpu.VMEM((total, WIDTH), half),
            pltpu.VMEM((total, WIDTH), half),
        ],
        pl.CostEstimate(
            flops=12 * total * RROWS * WIDTH, bytes_accessed=6_000_000, transcendentals=total * RROWS
        ),
    )


def exchanged(blocks, axes):
    return lax.all_to_all(blocks, axes, split_axis=0, concat_axis=0, tiled=True)


def given_to_all(block, axes):
    count = lax.axis_size(axes)
    return exchanged(jnp.broadcast_to(block[None], (count,) + block.shape), axes)


def shifted(array, by):
    pairs = [(i, i + by) for i in range(DP) if 0 <= i + by < DP]
    return lax.ppermute(array, ("xlo", "z", "y"), pairs)


def swapped_heads(array, step):
    return lax.ppermute(array, "head", [(i, i ^ step) for i in range(HEADS)])


def body(prompt_kv, resp_kv, resp_query, resp_out, resp_dout, resp_lengths, prompt_owner):
    half = jnp.bfloat16
    xlo, z, y = lax.axis_index("xlo"), lax.axis_index("z"), lax.axis_index("y")
    own_index = (xlo * Z + z) * Y + y
    own_group = own_index // PIECES

    head = lax.axis_index("head")
    place = head.reshape(1).astype(jnp.int32)
    own = resp_kv.transpose(0, 2, 1).reshape(2 * PART, RROWS)
    along_planes = given_to_all(prompt_kv.reshape(TILE, WIDTH), ("xlo", "z")).reshape(PLANES * TILE, WIDTH)
    fanned, near = local_call(
        fan_kernel,
        "fan",
        [((Y, PLANES * TILE, WIDTH), half), ((HEADS, 2 * PART, RROWS), half)],
        (place, along_planes, own, *[swapped_heads(own, step) for step in range(1, HEADS)]),
    )
    pieces = exchanged(fanned, "y").reshape(DP, TILE, WIDTH)
    near = [near] + [shifted(near, distance) for distance in range(1, HOPS + 1)]

    holder = jnp.arange(DP, dtype=jnp.int32)
    slot = (holder % Y) * PLANES + holder // Y
    own_pieces = own_group * PIECES + jnp.arange(PIECES, dtype=jnp.int32)
    owned = own_pieces[:, None] == prompt_owner[None, :]
    slots = jnp.sum(jnp.where(owned, slot[None, :], 0), axis=1).astype(jnp.int32)
    picked = local_call(select_kernel, "select", [((PIECES * TILE, WIDTH), half)], (slots, pieces))[0]
    gathered = lax.all_gather(picked, "head", axis=0, tiled=False)

    offset = (own_index % PIECES) * RROWS + jnp.arange(RROWS, dtype=jnp.int32)
    lengths = jnp.sum(
        jnp.where(jnp.arange(resp_lengths.shape[0])[:, None] == own_group, resp_lengths, 0), axis=0
    )
    count = lengths.shape[0]
    earlier = jnp.arange(count)[None, :] <= jnp.arange(count)[:, None]
    bounds = jnp.sum(jnp.where(earlier, lengths[None, :], 0), axis=1)
    begun = jnp.max(jnp.where(bounds[:, None] <= offset[None, :], bounds[:, None], 0), axis=0)
    start = (begun - (own_index % PIECES) * RROWS).astype(jnp.int32)[None, :]

    query_grad, close, own_terms, *fars = attention(
        resp_query, resp_out, resp_dout, start, gathered, near
    )

    landed = exchanged(close, "head")
    spread = local_call(place_kernel, "place", [((DP, TILE, WIDTH), half)], (slots, landed))[0]
    by_column = exchanged(spread.reshape(Y, PLANES * TILE, WIDTH), "y")
    column_sum = local_call(column_kernel, "column", [((PLANES * TILE, WIDTH), half)], (by_column,))[0]
    by_plane = exchanged(column_sum.reshape(PLANES, TILE, WIDTH), ("xlo", "z"))
    prompt_grad = jnp.sum(by_plane.astype(jnp.float32), axis=0).astype(half)

    fars = [shifted(far, -distance) for distance, far in enumerate(fars, 1)]
    cut = (2 * PART, RROWS)
    mine, *others = local_call(
        combine_kernel,
        "combine",
        [(cut, half)] * HEADS,
        (place, own_terms, *fars),
        [pltpu.VMEM((HEADS,) + cut, half)],
    )
    resp_total = mine.astype(jnp.float32)
    for step, other in enumerate(others, 1):
        resp_total = resp_total + swapped_heads(other, step).astype(jnp.float32)
    resp_grad = resp_total.astype(half).reshape(2, PART, RROWS).transpose(0, 2, 1)
    return query_grad, resp_grad, prompt_grad.reshape(2, PROWS, PART)


def solution(mesh):
    fine = Mesh(np.asarray(mesh.devices).reshape(XLO, Z, Y, HEADS), ("xlo", "z", "y", "head"))
    dp = ("xlo", "z", "y")
    in_specs = (
        P(None, dp, "head"),
        P(None, dp, "head"),
        P(dp, "head"),
        P(dp, "head"),
        P(dp, "head"),
        P(),
        P(),
    )
    out_specs = (P(dp, "head"), P(None, dp, "head"), P(None, dp, "head"))
    return jax.shard_map(body, mesh=fine, in_specs=in_specs, out_specs=out_specs, check_vma=False)
```

time: 146 us -> 156 us (1.068)
  the two profiles are of different devices: /device:TPU:24 before, /device:TPU:65 now
where the time goes in v3:
time: 156 us; the launch traced here: 155 us
  starting transfers between devices  70.8 us (45%)
  blocking collectives  36 us (23%)
  waiting for transfers between devices  33.7 us (22%)
  Pallas kernels  8.77 us (6%)
  local copies, waits for them, and re-layouts  3.49 us (2%)
    all_to_all x3, starting transfers between devices, exchanged(): return lax.all_to_all(blocks, axes, split_axis=0, concat_axis=0, tiled=True)  28.6 us
    all_to_all x2, blocking collectives, exchanged(): return lax.all_to_all(blocks, axes, split_axis=0, concat_axis=0, tiled=True)  24.5 us
    ppermute x8, starting transfers between devices, shifted(): return lax.ppermute(array, ('xlo', 'z', 'y'), pairs)  22.4 us
    ppermute x6, starting transfers between devices, swapped_heads(): return lax.ppermute(array, 'head', [(i, i ^ step) for i in range(HEADS)])  19.8 us
    ppermute x8, waiting for transfers between devices, shifted(): return lax.ppermute(array, ('xlo', 'z', 'y'), pairs)  16.1 us
    all_to_all x3, waiting for transfers between devices, exchanged(): return lax.all_to_all(blocks, axes, split_axis=0, concat_axis=0, tiled=True)  12.7 us
    all_gather x1, blocking collectives, body(): gathered = lax.all_gather(picked, 'head', axis=0, tiled=False)  11.6 us
    pallas_call x6, Pallas kernels, local_call(): pl.pallas_call(kernel, out_shape=[jax.ShapeDtypeStruct(shape, dtype) for...  8.77 us
  transfers between devices with their start and end apart: 17, of which 5 were waited for; matrix products, arithmetic and copies ran while one was open for 2% of the time, Pallas kernels for 1%

profile of v3, /device:TPU:65, one launch (start us, length us, event | category | flops | bytes accessed | tf_op | source)
XLA Modules:
  0.0 155.0 jit_solution(15976954356525340287)
XLA Ops:
  0.6 5.2 %collective-permute-start.2 = (bf16[64,384]{1,0:T(8,128)(2,1)}, bf16[64,384]{1,0:T(8,128)(2,1)S(1)}, u32[]{:S(2)}, u32[]{:S(2)}) collective-permute-start(bf16[64,384]{1,0:T(8,128)(2,1)} %bitcast.16), channel_id=1, source_target_pairs={{0,3},{1,2},{2,1},{3,0},{4,7},{5,6},{6,5},{7,4},{8,11},{9,10},{10,... | collective-permute-start | bytes 147464 | tf_op jit(solution)/shard_map/ppermute | solution.py:202
  5.9 2.1 %collective-permute-start.1 = (bf16[64,384]{1,0:T(8,128)(2,1)}, bf16[64,384]{1,0:T(8,128)(2,1)S(1)}, u32[]{:S(2)}, u32[]{:S(2)}) collective-permute-start(bf16[64,384]{1,0:T(8,128)(2,1)} %bitcast.17), channel_id=1, source_target_pairs={{0,2},{1,3},{2,0},{3,1},{4,6},{5,7},{6,4},{7,5},{8,10},{9,11},{10,... | collective-permute-start | bytes 147464 | tf_op jit(solution)/shard_map/ppermute | solution.py:202
  8.0 2.1 %collective-permute-start = (bf16[64,384]{1,0:T(8,128)(2,1)}, bf16[64,384]{1,0:T(8,128)(2,1)S(1)}, u32[]{:S(2)}, u32[]{:S(2)}) collective-permute-start(bf16[64,384]{1,0:T(8,128)(2,1)} %bitcast.18), channel_id=1, source_target_pairs={{0,1},{1,0},{2,3},{3,2},{4,5},{5,4},{6,7},{7,6},{8,9},{9,8},{10,11... | collective-permute-start | bytes 147464 | tf_op jit(solution)/shard_map/ppermute | solution.py:202
  10.1 0.8 broadcast_in_dim.71
  10.9 0.7 broadcast_in_dim.72
  11.6 15.2 %all-to-all-start = ((bf16[32,16,128]{2,1,0:T(8,128)(2,1)}), bf16[32,16,128]{2,1,0:T(8,128)(2,1)S(1)}, u32[]{:S(2)}, u32[]{:S(2)}) async-start(bf16[32,16,128]{2,1,0:T(8,128)(2,1)} %broadcast_in_dim.72), calls=%async_computation | async-start | bytes 262144 | tf_op jit(solution)/shard_map/all_to_all | solution.py:188
  26.8 0.0 copy-start
  26.8 0.0 copy-start.4
  26.9 0.7 copy-done.4
  27.5 0.1 select_reduce_fusion.3
  27.6 0.1 select_reduce_fusion.2
  27.7 0.1 select_reduce_fusion
  27.8 0.0 collective-permute-done.1.other2
  27.8 12.6 %all-to-all-done = bf16[32,16,128]{2,1,0:T(8,128)(2,1)S(1)} async-done(((bf16[32,16,128]{2,1,0:T(8,128)(2,1)}), bf16[32,16,128]{2,1,0:T(8,128)(2,1)S(1)}, u32[]{:S(2)}, u32[]{:S(2)}) %all-to-all-start) | async-done | bytes 131104 | tf_op jit(solution)/shard_map/all_to_all | solution.py:188
  40.5 0.9 fan.1
  41.4 4.2 %all-to-all-start.1 = ((bf16[4,512,128]{2,1,0:T(8,128)(2,1)}), bf16[4,512,128]{2,1,0:T(8,128)(2,1)S(1)}, u32[]{:S(2)}, u32[]{:S(2)}) async-start(bf16[4,512,128]{2,1,0:T(8,128)(2,1)} %get-tuple-element.16), calls=%async_computation.1 | async-start | bytes 1048576 | tf_op jit(solution)/shard_map/all_to_all | solution.py:188
  45.6 0.6 copy-done.5
  46.2 0.2 select_reduce_fusion.1.slots
  46.4 3.1 %collective-permute-start.6 = (bf16[4,64,384]{2,1,0:T(8,128)(2,1)S(1)}, bf16[4,64,384]{2,1,0:T(8,128)(2,1)S(1)}, u32[]{:S(2)}, u32[]{:S(2)}) collective-permute-start(bf16[4,64,384]{2,1,0:T(8,128)(2,1)S(1)} %get-tuple-element.17.near0), channel_id=1, source_target_pairs={{0,16},{4,20},{8,24},{12,28},{16,32},{20,36},{24,40},{28,44},{32,4... | collective-permute-start | bytes 589832 | tf_op jit(solution)/shard_map/ppermute | solution.py:198
  49.5 4.6 %collective-permute-start.5 = (bf16[4,64,384]{2,1,0:T(8,128)(2,1)S(1)}, bf16[4,64,384]{2,1,0:T(8,128)(2,1)S(1)}, u32[]{:S(2)}, u32[]{:S(2)}) collective-permute-start(bf16[4,64,384]{2,1,0:T(8,128)(2,1)S(1)} %get-tuple-element.17.near0), channel_id=1, source_target_pairs={{0,12},{4,16},{8,20},{12,24},{16,28},{20,32},{24,36},{28,40},{32,4... | collective-permute-start | bytes 589832 | tf_op jit(solution)/shard_map/ppermute | solution.py:198
  54.1 2.2 %collective-permute-start.4 = (bf16[4,64,384]{2,1,0:T(8,128)(2,1)S(1)}, bf16[4,64,384]{2,1,0:T(8,128)(2,1)S(1)}, u32[]{:S(2)}, u32[]{:S(2)}) collective-permute-start(bf16[4,64,384]{2,1,0:T(8,128)(2,1)S(1)} %get-tuple-element.17.near0), channel_id=1, source_target_pairs={{0,8},{4,12},{8,16},{12,20},{16,24},{20,28},{24,32},{28,36},{32,40... | collective-permute-start | bytes 589832 | tf_op jit(solution)/shard_map/ppermute | solution.py:198
  56.3 2.5 %collective-permute-start.3 = (bf16[4,64,384]{2,1,0:T(8,128)(2,1)S(1)}, bf16[4,64,384]{2,1,0:T(8,128)(2,1)S(1)}, u32[]{:S(2)}, u32[]{:S(2)}) collective-permute-start(bf16[4,64,384]{2,1,0:T(8,128)(2,1)S(1)} %get-tuple-element.17.near0), channel_id=1, source_target_pairs={{0,4},{4,8},{8,12},{12,16},{16,20},{20,24},{24,28},{28,32},{32,36}... | collective-permute-start | bytes 589832 | tf_op jit(solution)/shard_map/ppermute | solution.py:198
  58.8 0.0 all-to-all-done.1
  58.8 0.6 select.17
  59.4 0.0 copy-start.1
  59.4 0.0 copy-start.2
  59.4 0.0 copy-start.3
  59.4 11.6 %all-gather = bf16[2048,128]{1,0:T(8,128)(2,1)S(1)} all-gather(bf16[512,128]{1,0:T(8,128)(2,1)S(1)} %select.17), channel_id=2, replica_groups=mesh['xlo'=2,'z'=16,'y'=4,'head'=4] {'head'}, dimensions={0}, use_global_device_ids=true | all-gather | bytes 655360 | tf_op jit(solution)/shard_map/all_gather | solution.py:230
  71.1 5.7 %attention.1 = (bf16[384,128]{1,0:T(8,128)(2,1)}, bf16[4,512,128]{2,1,0:T(8,128)(2,1)S(1)}, f32[2,384,128]{2,1,0:T(8,128)S(1)}, bf16[2,384,128]{2,1,0:T(8,128)(2...) custom-call(bf16[384,128]{1,0:T(8,128)(2,1)S(1)} %copy-done.1, ...), custom_call_target="tpu_custom_call" | custom-call | flops 1736441856 | bytes 6000000 | tf_op jit(solution)/shard_map/attention/pallas_call | solution.py:154
  76.8 14.0 %all_to_all.25.landed = bf16[4,512,128]{2,1,0:T(8,128)(2,1)S(1)} all-to-all(bf16[4,512,128]{2,1,0:T(8,128)(2,1)S(1)} %get-tuple-element.28), channel_id=1, replica_groups=mesh['xlo'=2,'z'=16,'y'=4,'head'=4] {'head'}, dimensions={0} | all-to-all | bytes 1048576 | tf_op jit(solution)/shard_map/all_to_all | solution.py:188
  90.8 0.7 place.1
  91.5 10.5 %all_to_all.26.landed = bf16[4,512,128]{2,1,0:T(8,128)(2,1)S(1)} all-to-all(bf16[4,512,128]{2,1,0:T(8,128)(2,1)S(1)} %bitcast.13), channel_id=1, replica_groups=mesh['xlo'=2,'z'=16,'y'=4,'head'=4] {'y'}, dimensions={0} | all-to-all | bytes 1048576 | tf_op jit(solution)/shard_map/all_to_all | solution.py:188
  101.9 0.7 column.1
  102.7 9.2 %all-to-all-start.4 = ((bf16[32,16,128]{2,1,0:T(8,128)(2,1)}), bf16[32,16,128]{2,1,0:T(8,128)(2,1)S(1)}, u32[]{:S(2)}, u32[]{:S(2)}) async-start(bf16[32,16,128]{2,1,0:T(8,128)(2,1)} %bitcast.10), calls=%async_computation.4 | async-start | bytes 262144 | tf_op jit(solution)/shard_map/all_to_all | solution.py:188
  111.9 2.8 %collective-permute-start.7 = (bf16[2,384,128]{2,1,0:T(8,128)(2,1)S(1)}, bf16[2,384,128]{2,1,0:T(8,128)(2,1)S(1)}, u32[]{:S(2)}, u32[]{:S(2)}) collective-permute-start(bf16[2,384,128]{2,1,0:T(8,128)(2,1)S(1)} %get-tuple-element.20), channel_id=1, source_target_pairs={{4,0},{8,4},{12,8},{16,12},{20,16},{24,20},{28,24},{32,28},{36,32}... | collective-permute-start | bytes 589832 | tf_op jit(solution)/shard_map/ppermute | solution.py:198
  114.7 3.1 %collective-permute-start.8 = (bf16[2,384,128]{2,1,0:T(8,128)(2,1)S(1)}, bf16[2,384,128]{2,1,0:T(8,128)(2,1)S(1)}, u32[]{:S(2)}, u32[]{:S(2)}) collective-permute-start(bf16[2,384,128]{2,1,0:T(8,128)(2,1)S(1)} %get-tuple-element.21), channel_id=1, source_target_pairs={{8,0},{12,4},{16,8},{20,12},{24,16},{28,20},{32,24},{36,28},{40,32... | collective-permute-start | bytes 589832 | tf_op jit(solution)/shard_map/ppermute | solution.py:198
  117.8 1.9 %collective-permute-start.9 = (bf16[2,384,128]{2,1,0:T(8,128)(2,1)S(1)}, bf16[2,384,128]{2,1,0:T(8,128)(2,1)S(1)}, u32[]{:S(2)}, u32[]{:S(2)}) collective-permute-start(bf16[2,384,128]{2,1,0:T(8,128)(2,1)S(1)} %get-tuple-element.22), channel_id=1, source_target_pairs={{12,0},{16,4},{20,8},{24,12},{28,16},{32,20},{36,24},{40,28},{44,3... | collective-permute-start | bytes 589832 | tf_op jit(solution)/shard_map/ppermute | solution.py:198
  119.7 2.3 %collective-permute-start.10 = (bf16[2,384,128]{2,1,0:T(8,128)(2,1)S(1)}, bf16[2,384,128]{2,1,0:T(8,128)(2,1)S(1)}, u32[]{:S(2)}, u32[]{:S(2)}) collective-permute-start(bf16[2,384,128]{2,1,0:T(8,128)(2,1)S(1)} %get-tuple-element.23), channel_id=1, source_target_pairs={{16,0},{20,4},{24,8},{28,12},{32,16},{36,20},{40,24},{44,28},{48,3... | collective-permute-start | bytes 589832 | tf_op jit(solution)/shard_map/ppermute | solution.py:198
  122.0 4.8 %collective-permute-done.8.far2 = bf16[2,384,128]{2,1,0:T(8,128)(2,1)S(1)} collective-permute-done((bf16[2,384,128]{2,1,0:T(8,128)(2,1)S(1)}, bf16[2,384,128]{2,1,0:T(8,128)(2,1)S(1)}, u32[]{:S(2)}, u32[]{:S(2)}) %collective-permute-start.8) | collective-permute-done | bytes 196640 | tf_op jit(solution)/shard_map/ppermute | solution.py:198
  126.8 4.9 %collective-permute-done.9.far3 = bf16[2,384,128]{2,1,0:T(8,128)(2,1)S(1)} collective-permute-done((bf16[2,384,128]{2,1,0:T(8,128)(2,1)S(1)}, bf16[2,384,128]{2,1,0:T(8,128)(2,1)S(1)}, u32[]{:S(2)}, u32[]{:S(2)}) %collective-permute-start.9) | collective-permute-done | bytes 196640 | tf_op jit(solution)/shard_map/ppermute | solution.py:198
  131.8 6.4 %collective-permute-done.10.far4 = bf16[2,384,128]{2,1,0:T(8,128)(2,1)S(1)} collective-permute-done((bf16[2,384,128]{2,1,0:T(8,128)(2,1)S(1)}, bf16[2,384,128]{2,1,0:T(8,128)(2,1)S(1)}, u32[]{:S(2)}, u32[]{:S(2)}) %collective-permute-start.10) | collective-permute-done | bytes 196640 | tf_op jit(solution)/shard_map/ppermute | solution.py:198
  138.1 0.2 combine.1
  138.3 3.4 %collective-permute-start.11 = (bf16[64,384]{1,0:T(8,128)(2,1)S(1)}, bf16[64,384]{1,0:T(8,128)(2,1)S(1)}, u32[]{:S(2)}, u32[]{:S(2)}) collective-permute-start(bf16[64,384]{1,0:T(8,128)(2,1)S(1)} %get-tuple-element.25), channel_id=1, source_target_pairs={{0,1},{1,0},{2,3},{3,2},{4,5},{5,4},{6,7},{7,6},{8,9},{9,8},{10,11... | collective-permute-start | bytes 147464 | tf_op jit(solution)/shard_map/ppermute | solution.py:202
  141.7 4.9 %collective-permute-start.12 = (bf16[64,384]{1,0:T(8,128)(2,1)S(1)}, bf16[64,384]{1,0:T(8,128)(2,1)S(1)}, u32[]{:S(2)}, u32[]{:S(2)}) collective-permute-start(bf16[64,384]{1,0:T(8,128)(2,1)S(1)} %get-tuple-element.26), channel_id=1, source_target_pairs={{0,2},{1,3},{2,0},{3,1},{4,6},{5,7},{6,4},{7,5},{8,10},{9,11},{10,... | collective-permute-start | bytes 147464 | tf_op jit(solution)/shard_map/ppermute | solution.py:202
  146.6 2.1 %collective-permute-start.13 = (bf16[64,384]{1,0:T(8,128)(2,1)S(1)}, bf16[64,384]{1,0:T(8,128)(2,1)S(1)}, u32[]{:S(2)}, u32[]{:S(2)}) collective-permute-start(bf16[64,384]{1,0:T(8,128)(2,1)S(1)} %get-tuple-element.27), channel_id=1, source_target_pairs={{0,3},{1,2},{2,1},{3,0},{4,7},{5,6},{6,5},{7,4},{8,11},{9,10},{10,... | collective-permute-start | bytes 147464 | tf_op jit(solution)/shard_map/ppermute | solution.py:202
  148.7 4.9 %collective-permute-done.13 = bf16[64,384]{1,0:T(8,128)(2,1)S(1)} collective-permute-done((bf16[64,384]{1,0:T(8,128)(2,1)S(1)}, bf16[64,384]{1,0:T(8,128)(2,1)S(1)}, u32[]{:S(2)}, u32[]{:S(2)}) %collective-permute-start.13) | collective-permute-done | bytes 49184 | tf_op jit(solution)/shard_map/ppermute | solution.py:202
  153.6 0.6 add_convert_fusion
  154.3 0.7 reshape.85
  (22 shorter events, 0.1 us)
Async XLA Ops:
  0.6 27.2 %collective-permute-start.2 = (bf16[64,384]{1,0:T(8,128)(2,1)}, bf16[64,384]{1,0:T(8,128)(2,1)S(1)}, u32[]{:S(2)}, u32[]{:S(2)}) collective-permute-start(bf16[64,384]{1,0:T(8,128)(2,1)} %bitcast.16), channel_id=1, source_target_pairs={{0,3},{1,2},{2,1},{3,0},{4,7},{5,6},{6,5},{7,4},{8,11},{9,10},{10,... | collective-permute-start | bytes 147464 | tf_op jit(solution)/shard_map/ppermute | solution.py:202
  5.9 22.0 %collective-permute-start.1 = (bf16[64,384]{1,0:T(8,128)(2,1)}, bf16[64,384]{1,0:T(8,128)(2,1)S(1)}, u32[]{:S(2)}, u32[]{:S(2)}) collective-permute-start(bf16[64,384]{1,0:T(8,128)(2,1)} %bitcast.17), channel_id=1, source_target_pairs={{0,2},{1,3},{2,0},{3,1},{4,6},{5,7},{6,4},{7,5},{8,10},{9,11},{10,... | collective-permute-start | bytes 147464 | tf_op jit(solution)/shard_map/ppermute | solution.py:202
  8.0 19.8 %collective-permute-start = (bf16[64,384]{1,0:T(8,128)(2,1)}, bf16[64,384]{1,0:T(8,128)(2,1)S(1)}, u32[]{:S(2)}, u32[]{:S(2)}) collective-permute-start(bf16[64,384]{1,0:T(8,128)(2,1)} %bitcast.18), channel_id=1, source_target_pairs={{0,1},{1,0},{2,3},{3,2},{4,5},{5,4},{6,7},{7,6},{8,9},{9,8},{10,11... | collective-permute-start | bytes 147464 | tf_op jit(solution)/shard_map/ppermute | solution.py:202
  11.6 28.9 %all-to-all-start = ((bf16[32,16,128]{2,1,0:T(8,128)(2,1)}), bf16[32,16,128]{2,1,0:T(8,128)(2,1)S(1)}, u32[]{:S(2)}, u32[]{:S(2)}) async-start(bf16[32,16,128]{2,1,0:T(8,128)(2,1)} %broadcast_in_dim.72), calls=%async_computation | async-start | bytes 262144 | tf_op jit(solution)/shard_map/all_to_all | solution.py:188
  26.8 13.7 %copy-start = (bf16[2,384,32]{1,2,0:T(8,128)(2,1)S(1)}, bf16[2,384,32]{1,2,0:T(8,128)(2,1)}, u32[]{:S(2)}) copy-start(bf16[2,384,32]{1,2,0:T(8,128)(2,1)} %param.8) | copy-start | bytes 147460
  26.8 0.7 copy-start.4
  41.4 17.4 %all-to-all-start.1 = ((bf16[4,512,128]{2,1,0:T(8,128)(2,1)}), bf16[4,512,128]{2,1,0:T(8,128)(2,1)S(1)}, u32[]{:S(2)}, u32[]{:S(2)}) async-start(bf16[4,512,128]{2,1,0:T(8,128)(2,1)} %get-tuple-element.16), calls=%async_computation.1 | async-start | bytes 1048576 | tf_op jit(solution)/shard_map/all_to_all | solution.py:188
  45.6 0.7 copy-start.5
  46.4 24.6 %collective-permute-start.6 = (bf16[4,64,384]{2,1,0:T(8,128)(2,1)S(1)}, bf16[4,64,384]{2,1,0:T(8,128)(2,1)S(1)}, u32[]{:S(2)}, u32[]{:S(2)}) collective-permute-start(bf16[4,64,384]{2,1,0:T(8,128)(2,1)S(1)} %get-tuple-element.17.near0), channel_id=1, source_target_pairs={{0,16},{4,20},{8,24},{12,28},{16,32},{20,36},{24,40},{28,44},{32,4... | collective-permute-start | bytes 589832 | tf_op jit(solution)/shard_map/ppermute | solution.py:198
  49.5 21.5 %collective-permute-start.5 = (bf16[4,64,384]{2,1,0:T(8,128)(2,1)S(1)}, bf16[4,64,384]{2,1,0:T(8,128)(2,1)S(1)}, u32[]{:S(2)}, u32[]{:S(2)}) collective-permute-start(bf16[4,64,384]{2,1,0:T(8,128)(2,1)S(1)} %get-tuple-element.17.near0), channel_id=1, source_target_pairs={{0,12},{4,16},{8,20},{12,24},{16,28},{20,32},{24,36},{28,40},{32,4... | collective-permute-start | bytes 589832 | tf_op jit(solution)/shard_map/ppermute | solution.py:198
  54.1 16.9 %collective-permute-start.4 = (bf16[4,64,384]{2,1,0:T(8,128)(2,1)S(1)}, bf16[4,64,384]{2,1,0:T(8,128)(2,1)S(1)}, u32[]{:S(2)}, u32[]{:S(2)}) collective-permute-start(bf16[4,64,384]{2,1,0:T(8,128)(2,1)S(1)} %get-tuple-element.17.near0), channel_id=1, source_target_pairs={{0,8},{4,12},{8,16},{12,20},{16,24},{20,28},{24,32},{28,36},{32,40... | collective-permute-start | bytes 589832 | tf_op jit(solution)/shard_map/ppermute | solution.py:198
  56.3 14.7 %collective-permute-start.3 = (bf16[4,64,384]{2,1,0:T(8,128)(2,1)S(1)}, bf16[4,64,384]{2,1,0:T(8,128)(2,1)S(1)}, u32[]{:S(2)}, u32[]{:S(2)}) collective-permute-start(bf16[4,64,384]{2,1,0:T(8,128)(2,1)S(1)} %get-tuple-element.17.near0), channel_id=1, source_target_pairs={{0,4},{4,8},{8,12},{12,16},{16,20},{20,24},{24,28},{28,32},{32,36}... | collective-permute-start | bytes 589832 | tf_op jit(solution)/shard_map/ppermute | solution.py:198
  59.4 11.6 %copy-start.1 = (bf16[384,128]{1,0:T(8,128)(2,1)S(1)}, bf16[384,128]{1,0:T(8,128)(2,1)}, u32[]{:S(2)}) copy-start(bf16[384,128]{1,0:T(8,128)(2,1)} %q.1) | copy-start | bytes 294916
  59.4 11.6 %copy-start.2 = (bf16[384,128]{1,0:T(8,128)(2,1)S(1)}, bf16[384,128]{1,0:T(8,128)(2,1)}, u32[]{:S(2)}) copy-start(bf16[384,128]{1,0:T(8,128)(2,1)} %o.1) | copy-start | bytes 294916
  59.4 11.6 %copy-start.3 = (bf16[384,128]{1,0:T(8,128)(2,1)S(1)}, bf16[384,128]{1,0:T(8,128)(2,1)}, u32[]{:S(2)}) copy-start(bf16[384,128]{1,0:T(8,128)(2,1)} %do.1) | copy-start | bytes 294916
  102.7 51.6 %all-to-all-start.4 = ((bf16[32,16,128]{2,1,0:T(8,128)(2,1)}), bf16[32,16,128]{2,1,0:T(8,128)(2,1)S(1)}, u32[]{:S(2)}, u32[]{:S(2)}) async-start(bf16[32,16,128]{2,1,0:T(8,128)(2,1)} %bitcast.10), calls=%async_computation.4 | async-start | bytes 262144 | tf_op jit(solution)/shard_map/all_to_all | solution.py:188
  111.9 10.1 %collective-permute-start.7 = (bf16[2,384,128]{2,1,0:T(8,128)(2,1)S(1)}, bf16[2,384,128]{2,1,0:T(8,128)(2,1)S(1)}, u32[]{:S(2)}, u32[]{:S(2)}) collective-permute-start(bf16[2,384,128]{2,1,0:T(8,128)(2,1)S(1)} %get-tuple-element.20), channel_id=1, source_target_pairs={{4,0},{8,4},{12,8},{16,12},{20,16},{24,20},{28,24},{32,28},{36,32}... | collective-permute-start | bytes 589832 | tf_op jit(solution)/shard_map/ppermute | solution.py:198
  114.7 12.1 %collective-permute-start.8 = (bf16[2,384,128]{2,1,0:T(8,128)(2,1)S(1)}, bf16[2,384,128]{2,1,0:T(8,128)(2,1)S(1)}, u32[]{:S(2)}, u32[]{:S(2)}) collective-permute-start(bf16[2,384,128]{2,1,0:T(8,128)(2,1)S(1)} %get-tuple-element.21), channel_id=1, source_target_pairs={{8,0},{12,4},{16,8},{20,12},{24,16},{28,20},{32,24},{36,28},{40,32... | collective-permute-start | bytes 589832 | tf_op jit(solution)/shard_map/ppermute | solution.py:198
  117.8 14.0 %collective-permute-start.9 = (bf16[2,384,128]{2,1,0:T(8,128)(2,1)S(1)}, bf16[2,384,128]{2,1,0:T(8,128)(2,1)S(1)}, u32[]{:S(2)}, u32[]{:S(2)}) collective-permute-start(bf16[2,384,128]{2,1,0:T(8,128)(2,1)S(1)} %get-tuple-element.22), channel_id=1, source_target_pairs={{12,0},{16,4},{20,8},{24,12},{28,16},{32,20},{36,24},{40,28},{44,3... | collective-permute-start | bytes 589832 | tf_op jit(solution)/shard_map/ppermute | solution.py:198
  119.7 18.4 %collective-permute-start.10 = (bf16[2,384,128]{2,1,0:T(8,128)(2,1)S(1)}, bf16[2,384,128]{2,1,0:T(8,128)(2,1)S(1)}, u32[]{:S(2)}, u32[]{:S(2)}) collective-permute-start(bf16[2,384,128]{2,1,0:T(8,128)(2,1)S(1)} %get-tuple-element.23), channel_id=1, source_target_pairs={{16,0},{20,4},{24,8},{28,12},{32,16},{36,20},{40,24},{44,28},{48,3... | collective-permute-start | bytes 589832 | tf_op jit(solution)/shard_map/ppermute | solution.py:198
  138.3 10.4 %collective-permute-start.11 = (bf16[64,384]{1,0:T(8,128)(2,1)S(1)}, bf16[64,384]{1,0:T(8,128)(2,1)S(1)}, u32[]{:S(2)}, u32[]{:S(2)}) collective-permute-start(bf16[64,384]{1,0:T(8,128)(2,1)S(1)} %get-tuple-element.25), channel_id=1, source_target_pairs={{0,1},{1,0},{2,3},{3,2},{4,5},{5,4},{6,7},{7,6},{8,9},{9,8},{10,11... | collective-permute-start | bytes 147464 | tf_op jit(solution)/shard_map/ppermute | solution.py:202
  141.7 7.0 %collective-permute-start.12 = (bf16[64,384]{1,0:T(8,128)(2,1)S(1)}, bf16[64,384]{1,0:T(8,128)(2,1)S(1)}, u32[]{:S(2)}, u32[]{:S(2)}) collective-permute-start(bf16[64,384]{1,0:T(8,128)(2,1)S(1)} %get-tuple-element.26), channel_id=1, source_target_pairs={{0,2},{1,3},{2,0},{3,1},{4,6},{5,7},{6,4},{7,5},{8,10},{9,11},{10,... | collective-permute-start | bytes 147464 | tf_op jit(solution)/shard_map/ppermute | solution.py:202
  146.6 7.0 %collective-permute-start.13 = (bf16[64,384]{1,0:T(8,128)(2,1)S(1)}, bf16[64,384]{1,0:T(8,128)(2,1)S(1)}, u32[]{:S(2)}, u32[]{:S(2)}) collective-permute-start(bf16[64,384]{1,0:T(8,128)(2,1)S(1)} %get-tuple-element.27), channel_id=1, source_target_pairs={{0,3},{1,2},{2,1},{3,0},{4,7},{5,6},{6,5},{7,4},{8,11},{9,10},{10,... | collective-permute-start | bytes 147464 | tf_op jit(solution)/shard_map/ppermute | solution.py:202

commit v4 on v3

--- a/solution.py
+++ b/solution.py
@@ -8,8 +8,7 @@
 from jax.sharding import PartitionSpec as P
 
 XLO, Z, Y, HEADS = 2, 16, 4, 4
-PLANES = XLO * Z
-DP = PLANES * Y
+DP = XLO * Z * Y
 WIDTH = 128
 PART = WIDTH // HEADS
 PIECES = 32
@@ -38,11 +37,10 @@
     return jnp.dot(rows, swap, preferred_element_type=jnp.float32)
 
 
-def fan_kernel(place, shares, own, other1, other2, other3, fanned, near):
-    for column in range(Y):
+def fan_kernel(shares, own, fanned, near):
+    for column in range(XLO * Y):
         fanned[column] = shares[...]
-    for step, part in enumerate((own, other1, other2, other3)):
-        near[place[0] ^ step] = part[...]
+    near[...] = own[...]
 
 
 def select_kernel(slots, pieces, picked):
@@ -50,7 +48,7 @@
         picked[piece * TILE : (piece + 1) * TILE] = pieces[slots[piece]]
 
 
-def place_kernel(slots, landed, spread):
+def place_kernel(slots, landed, own, far2, far4, spread, partial):
     spread[...] = jnp.zeros_like(spread)
     total = landed[0].astype(jnp.float32)
     for head in range(1, HEADS):
@@ -58,19 +56,15 @@
     rounded = total.astype(jnp.bfloat16)
     for piece in range(PIECES):
         spread[slots[piece]] = rounded[piece * TILE : (piece + 1) * TILE]
-
-
-def column_kernel(landed, total):
+    partial[...] = own[...] + far2[...].astype(jnp.float32) + far4[...].astype(jnp.float32)
+
+
+def column_kernel(place, landed, partial, far1, far3, column, mine, out1, out2, out3, slots):
     held = landed[0].astype(jnp.float32)
-    for column in range(1, Y):
-        held = held + landed[column].astype(jnp.float32)
-    total[...] = held.astype(total.dtype)
-
-
-def combine_kernel(place, own, far1, far2, far3, far4, mine, out1, out2, out3, slots):
-    total = own[...]
-    for far in (far1, far2, far3, far4):
-        total = total + far[...].astype(jnp.float32)
+    for sender in range(1, XLO * Y):
+        held = held + landed[sender].astype(jnp.float32)
+    column[...] = held
+    total = partial[...] + far1[...].astype(jnp.float32) + far3[...].astype(jnp.float32)
     turned = [total[kind].T.astype(jnp.bfloat16) for kind in range(2)]
     for head in range(HEADS):
         for kind in range(2):
@@ -92,9 +86,8 @@
         values[rows] = part[:, 1].reshape(QUARTER, WIDTH).astype(jnp.bfloat16)
     for distance, near in enumerate((near0, near1, near2, near3, near4)):
         rows = slice(PROMPT + distance * RROWS, PROMPT + (distance + 1) * RROWS)
-        for held, shift in ((keys, 0), (values, PART)):
-            turned = [near[c, shift : shift + PART] for c in range(HEADS)]
-            held[rows] = jnp.concatenate(turned, axis=0).T
+        keys[rows] = near[0].T
+        values[rows] = near[1].T
     chunks = [(i * QUARTER, QUARTER, None) for i in range(HEADS)]
     chunks += [(PROMPT + d * RROWS, RROWS, d) for d in range(HOPS + 1)]
     queries, dout = q[...], do[...]
@@ -210,19 +203,19 @@
 
     head = lax.axis_index("head")
     place = head.reshape(1).astype(jnp.int32)
-    own = resp_kv.transpose(0, 2, 1).reshape(2 * PART, RROWS)
-    along_planes = given_to_all(prompt_kv.reshape(TILE, WIDTH), ("xlo", "z")).reshape(PLANES * TILE, WIDTH)
+    own = lax.all_gather(resp_kv.transpose(0, 2, 1), "head", axis=1, tiled=True)
+    along_z = given_to_all(prompt_kv.reshape(TILE, WIDTH), "z").reshape(Z * TILE, WIDTH)
     fanned, near = local_call(
         fan_kernel,
         "fan",
-        [((Y, PLANES * TILE, WIDTH), half), ((HEADS, 2 * PART, RROWS), half)],
-        (place, along_planes, own, *[swapped_heads(own, step) for step in range(1, HEADS)]),
-    )
-    pieces = exchanged(fanned, "y").reshape(DP, TILE, WIDTH)
+        [((XLO * Y, Z * TILE, WIDTH), half), ((2, WIDTH, RROWS), half)],
+        (along_z, own),
+    )
+    pieces = exchanged(fanned, ("xlo", "y")).reshape(DP, TILE, WIDTH)
     near = [near] + [shifted(near, distance) for distance in range(1, HOPS + 1)]
 
     holder = jnp.arange(DP, dtype=jnp.int32)
-    slot = (holder % Y) * PLANES + holder // Y
+    slot = ((holder // (Z * Y)) * Y + holder % Y) * Z + (holder // Y) % Z
     own_pieces = own_group * PIECES + jnp.arange(PIECES, dtype=jnp.int32)
     owned = own_pieces[:, None] == prompt_owner[None, :]
     slots = jnp.sum(jnp.where(owned, slot[None, :], 0), axis=1).astype(jnp.int32)
@@ -244,21 +237,25 @@
     )
 
     landed = exchanged(close, "head")
-    spread = local_call(place_kernel, "place", [((DP, TILE, WIDTH), half)], (slots, landed))[0]
-    by_column = exchanged(spread.reshape(Y, PLANES * TILE, WIDTH), "y")
-    column_sum = local_call(column_kernel, "column", [((PLANES * TILE, WIDTH), half)], (by_column,))[0]
-    by_plane = exchanged(column_sum.reshape(PLANES, TILE, WIDTH), ("xlo", "z"))
-    prompt_grad = jnp.sum(by_plane.astype(jnp.float32), axis=0).astype(half)
-
     fars = [shifted(far, -distance) for distance, far in enumerate(fars, 1)]
+    spread, partial = local_call(
+        place_kernel,
+        "place",
+        [((DP, TILE, WIDTH), half), ((2, RROWS, WIDTH), jnp.float32)],
+        (slots, landed, own_terms, fars[1], fars[3]),
+    )
+    by_column = exchanged(spread.reshape(XLO * Y, Z * TILE, WIDTH), ("xlo", "y"))
     cut = (2 * PART, RROWS)
-    mine, *others = local_call(
-        combine_kernel,
-        "combine",
-        [(cut, half)] * HEADS,
-        (place, own_terms, *fars),
+    column_sum, mine, *others = local_call(
+        column_kernel,
+        "column",
+        [((Z * TILE, WIDTH), jnp.float32)] + [(cut, half)] * HEADS,
+        (place, by_column, partial, fars[0], fars[2]),
         [pltpu.VMEM((HEADS,) + cut, half)],
     )
+    by_z = exchanged(column_sum.reshape(Z, TILE, WIDTH), "z")
+    prompt_grad = jnp.sum(by_z, axis=0).astype(half)
+
     resp_total = mine.astype(jnp.float32)
     for step, other in enumerate(others, 1):
         resp_total = resp_total + swapped_heads(other, step).astype(jnp.float32)

time: 156 us -> 132 us (0.85)
  the two profiles are of different devices: /device:TPU:65 before, /device:TPU:1 now
where the time goes in v4:
time: 132 us; the launch traced here: 131 us
  starting transfers between devices  63.6 us (48%)
  waiting for transfers between devices  32.2 us (24%)
  blocking collectives  19.9 us (15%)
  Pallas kernels  9.71 us (7%)
  local copies, waits for them, and re-layouts  3.46 us (3%)
    all_to_all x5, starting transfers between devices, exchanged(): return lax.all_to_all(blocks, axes, split_axis=0, concat_axis=0, tiled=True)  34.5 us
    ppermute x8, waiting for transfers between devices, shifted(): return lax.ppermute(array, ('xlo', 'z', 'y'), pairs)  24.8 us
    ppermute x8, starting transfers between devices, shifted(): return lax.ppermute(array, ('xlo', 'z', 'y'), pairs)  17.6 us
    all_gather x1, blocking collectives, body(): gathered = lax.all_gather(picked, 'head', axis=0, tiled=False)  12 us
    ppermute x3, starting transfers between devices, swapped_heads(): return lax.ppermute(array, 'head', [(i, i ^ step) for i in range(HEADS)])  11.4 us
    pallas_call x5, Pallas kernels, local_call(): pl.pallas_call(kernel, out_shape=[jax.ShapeDtypeStruct(shape, dtype) for...  9.71 us
    all_gather x1, blocking collectives, body(): own = lax.all_gather(resp_kv.transpose(0, 2, 1), 'head', axis=1, tiled=True)  7.89 us
    ppermute x3, waiting for transfers between devices, swapped_heads(): return lax.ppermute(array, 'head', [(i, i ^ step) for i in range(HEADS)])  4.77 us
  transfers between devices with their start and end apart: 16, of which 6 were waited for; matrix products, arithmetic and copies ran while one was open for 1% of the time, Pallas kernels for 0%

profile of v4, /device:TPU:1, one launch (start us, length us, event | category | flops | bytes accessed | tf_op | source)
XLA Modules:
  0.0 131.0 jit_solution(7291998291887608407)
XLA Ops:
  0.6 0.8 broadcast_in_dim.71
  1.4 0.6 broadcast_in_dim.72
  2.1 15.7 %all-to-all-start = ((bf16[16,16,128]{2,1,0:T(8,128)(2,1)}), bf16[16,16,128]{2,1,0:T(8,128)(2,1)S(1)}, u32[]{:S(2)}, u32[]{:S(2)}) async-start(bf16[16,16,128]{2,1,0:T(8,128)(2,1)} %broadcast_in_dim.72), calls=%async_computation | async-start | bytes 131072 | tf_op jit(solution)/shard_map/all_to_all | solution.py:181
  17.8 0.0 copy-start.3
  17.9 0.0 copy-start.4
  17.9 0.7 copy-done.4
  18.6 0.1 select_reduce_fusion.3
  18.7 7.9 %all_gather.9.own = bf16[2,128,384]{2,1,0:T(8,128)(2,1)S(1)} all-gather(bf16[2,32,384]{2,1,0:T(8,128)(2,1)S(1)} %bitcast.13), channel_id=1, replica_groups=mesh['xlo'=2,'z'=16,'y'=4,'head'=4] {'head'}, dimensions={1}, use_global_device_ids=true | all-gather | bytes 245760 | tf_op jit(solution)/shard_map/all_gather | solution.py:206
  26.6 0.1 select_reduce_fusion.2
  26.7 0.1 select_reduce_fusion
  26.8 2.6 %all-to-all-done = bf16[16,16,128]{2,1,0:T(8,128)(2,1)S(1)} async-done(((bf16[16,16,128]{2,1,0:T(8,128)(2,1)}), bf16[16,16,128]{2,1,0:T(8,128)(2,1)S(1)}, u32[]{:S(2)}, u32[]{:S(2)}) %all-to-all-start) | async-done | bytes 65568 | tf_op jit(solution)/shard_map/all_to_all | solution.py:181
  29.4 0.9 fan.1
  30.3 5.1 %all-to-all-start.1 = ((bf16[8,256,128]{2,1,0:T(8,128)(2,1)}), bf16[8,256,128]{2,1,0:T(8,128)(2,1)S(1)}, u32[]{:S(2)}, u32[]{:S(2)}) async-start(bf16[8,256,128]{2,1,0:T(8,128)(2,1)} %get-tuple-element.19), calls=%async_computation.1 | async-start | bytes 1048576 | tf_op jit(solution)/shard_map/all_to_all | solution.py:181
  35.4 0.0 copy-start.5
  35.5 0.6 copy-done.5
  36.1 0.2 select_reduce_fusion.1.slots
  36.3 3.0 %collective-permute-start.3 = (bf16[2,128,384]{2,1,0:T(8,128)(2,1)S(1)}, bf16[2,128,384]{2,1,0:T(8,128)(2,1)S(1)}, u32[]{:S(2)}, u32[]{:S(2)}) collective-permute-start(bf16[2,128,384]{2,1,0:T(8,128)(2,1)S(1)} %get-tuple-element.20.near0), channel_id=1, source_target_pairs={{0,16},{4,20},{8,24},{12,28},{16,32},{20,36},{24,40},{28,44},{32,4... | collective-permute-start | bytes 589832 | tf_op jit(solution)/shard_map/ppermute | solution.py:191
  39.2 4.6 %collective-permute-start.2 = (bf16[2,128,384]{2,1,0:T(8,128)(2,1)S(1)}, bf16[2,128,384]{2,1,0:T(8,128)(2,1)S(1)}, u32[]{:S(2)}, u32[]{:S(2)}) collective-permute-start(bf16[2,128,384]{2,1,0:T(8,128)(2,1)S(1)} %get-tuple-element.20.near0), channel_id=1, source_target_pairs={{0,12},{4,16},{8,20},{12,24},{16,28},{20,32},{24,36},{28,40},{32,4... | collective-permute-start | bytes 589832 | tf_op jit(solution)/shard_map/ppermute | solution.py:191
  43.8 2.5 %collective-permute-start.1 = (bf16[2,128,384]{2,1,0:T(8,128)(2,1)S(1)}, bf16[2,128,384]{2,1,0:T(8,128)(2,1)S(1)}, u32[]{:S(2)}, u32[]{:S(2)}) collective-permute-start(bf16[2,128,384]{2,1,0:T(8,128)(2,1)S(1)} %get-tuple-element.20.near0), channel_id=1, source_target_pairs={{0,8},{4,12},{8,16},{12,20},{16,24},{20,28},{24,32},{28,36},{32,40... | collective-permute-start | bytes 589832 | tf_op jit(solution)/shard_map/ppermute | solution.py:191
  46.3 2.5 %collective-permute-start = (bf16[2,128,384]{2,1,0:T(8,128)(2,1)S(1)}, bf16[2,128,384]{2,1,0:T(8,128)(2,1)S(1)}, u32[]{:S(2)}, u32[]{:S(2)}) collective-permute-start(bf16[2,128,384]{2,1,0:T(8,128)(2,1)S(1)} %get-tuple-element.20.near0), channel_id=1, source_target_pairs={{0,4},{4,8},{8,12},{12,16},{16,20},{20,24},{24,28},{28,32},{32,36}... | collective-permute-start | bytes 589832 | tf_op jit(solution)/shard_map/ppermute | solution.py:191
  48.8 0.6 select.33
  49.4 0.0 copy-start
  49.4 0.0 copy-start.1
  49.4 0.0 copy-start.2
  49.4 12.0 %all-gather = bf16[2048,128]{1,0:T(8,128)(2,1)S(1)} all-gather(bf16[512,128]{1,0:T(8,128)(2,1)S(1)} %select.33), channel_id=2, replica_groups=mesh['xlo'=2,'z'=16,'y'=4,'head'=4] {'head'}, dimensions={0}, use_global_device_ids=true | all-gather | bytes 655360 | tf_op jit(solution)/shard_map/all_gather | solution.py:223
  61.4 0.0 collective-permute-done.3.near4
  61.4 0.0 collective-permute-done.2.near3
  61.5 6.0 %attention.1 = (bf16[384,128]{1,0:T(8,128)(2,1)}, bf16[4,512,128]{2,1,0:T(8,128)(2,1)}, f32[2,384,128]{2,1,0:T(8,128)S(1)}, bf16[2,384,128]{2,1,0:T(8,128)(2,1)S...) custom-call(bf16[384,128]{1,0:T(8,128)(2,1)S(1)} %copy-done, ...), custom_call_target="tpu_custom_call" | custom-call | flops 1736441856 | bytes 6000000 | tf_op jit(solution)/shard_map/attention/pallas_call | solution.py:147
  67.4 3.8 %all-to-all-start.2 = ((bf16[4,512,128]{2,1,0:T(8,128)(2,1)}), bf16[4,512,128]{2,1,0:T(8,128)(2,1)S(1)}, u32[]{:S(2)}, u32[]{:S(2)}) async-start(bf16[4,512,128]{2,1,0:T(8,128)(2,1)} %get-tuple-element.22), calls=%async_computation.2 | async-start | bytes 1048576 | tf_op jit(solution)/shard_map/all_to_all | solution.py:181
  71.2 1.3 collective-permute-start.4
  72.5 1.3 collective-permute-start.5
  73.8 8.4 %collective-permute-done.4.far2 = bf16[2,384,128]{2,1,0:T(8,128)(2,1)S(1)} collective-permute-done((bf16[2,384,128]{2,1,0:T(8,128)(2,1)S(1)}, bf16[2,384,128]{2,1,0:T(8,128)(2,1)S(1)}, u32[]{:S(2)}, u32[]{:S(2)}) %collective-permute-start.4) | collective-permute-done | bytes 196640 | tf_op jit(solution)/shard_map/ppermute | solution.py:191
  82.2 5.2 %collective-permute-done.5.far4 = bf16[2,384,128]{2,1,0:T(8,128)(2,1)S(1)} collective-permute-done((bf16[2,384,128]{2,1,0:T(8,128)(2,1)S(1)}, bf16[2,384,128]{2,1,0:T(8,128)(2,1)S(1)}, u32[]{:S(2)}, u32[]{:S(2)}) %collective-permute-start.5) | collective-permute-done | bytes 196640 | tf_op jit(solution)/shard_map/ppermute | solution.py:191
  87.4 0.0 all-to-all-done.2.landed
  87.4 1.5 %place.1 = (bf16[128,16,128]{2,1,0:T(8,128)(2,1)}, f32[2,384,128]{2,1,0:T(8,128)S(1)}) custom-call(s32[32]{0:T(128)S(1)} %select_reduce_fusion.1.slots, bf16[4,512,128]{2,1,0:T(8,128)(2,1)S(1)} %all-to-all-done.2.landed, f32[2,384,128]{2,1,0:T(8,128)S(1)} %get-tuple-element.23.own, bf16[2,384,128]{2,1,0:T(8,128)(2,1)S(1)} %collective-permute-done.4.far2, ...), custom_call_target="tpu_custom_call" | custom-call | tf_op jit(solution)/shard_map/place/pallas_call | solution.py:147
  88.9 5.9 %all-to-all-start.3 = ((bf16[8,256,128]{2,1,0:T(8,128)(2,1)}), bf16[8,256,128]{2,1,0:T(8,128)(2,1)S(1)}, u32[]{:S(2)}, u32[]{:S(2)}) async-start(bf16[8,256,128]{2,1,0:T(8,128)(2,1)} %bitcast.5), calls=%async_computation.3 | async-start | bytes 1048576 | tf_op jit(solution)/shard_map/all_to_all | solution.py:181
  94.8 1.3 collective-permute-start.6
  96.1 1.3 collective-permute-start.7
  97.4 11.1 %collective-permute-done.6.far1 = bf16[2,384,128]{2,1,0:T(8,128)(2,1)S(1)} collective-permute-done((bf16[2,384,128]{2,1,0:T(8,128)(2,1)S(1)}, bf16[2,384,128]{2,1,0:T(8,128)(2,1)S(1)}, u32[]{:S(2)}, u32[]{:S(2)}) %collective-permute-start.6) | collective-permute-done | bytes 196640 | tf_op jit(solution)/shard_map/ppermute | solution.py:191
  108.4 0.2 collective-permute-done.7.far3
  108.6 0.8 column.1
  109.5 4.0 %all-to-all-start.4 = ((f32[16,16,128]{2,1,0:T(8,128)}), f32[16,16,128]{2,1,0:T(8,128)S(1)}, u32[]{:S(2)}, u32[]{:S(2)}) async-start(f32[16,16,128]{2,1,0:T(8,128)} %bitcast.8), calls=%async_computation.4 | async-start | bytes 262144 | tf_op jit(solution)/shard_map/all_to_all | solution.py:181
  113.5 4.5 %collective-permute-start.8 = (bf16[64,384]{1,0:T(8,128)(2,1)S(1)}, bf16[64,384]{1,0:T(8,128)(2,1)S(1)}, u32[]{:S(2)}, u32[]{:S(2)}) collective-permute-start(bf16[64,384]{1,0:T(8,128)(2,1)S(1)} %get-tuple-element.31), channel_id=1, source_target_pairs={{0,1},{1,0},{2,3},{3,2},{4,5},{5,4},{6,7},{7,6},{8,9},{9,8},{10,11... | collective-permute-start | bytes 147464 | tf_op jit(solution)/shard_map/ppermute | solution.py:195
  117.9 4.7 %collective-permute-start.9 = (bf16[64,384]{1,0:T(8,128)(2,1)S(1)}, bf16[64,384]{1,0:T(8,128)(2,1)S(1)}, u32[]{:S(2)}, u32[]{:S(2)}) collective-permute-start(bf16[64,384]{1,0:T(8,128)(2,1)S(1)} %get-tuple-element.32), channel_id=1, source_target_pairs={{0,2},{1,3},{2,0},{3,1},{4,6},{5,7},{6,4},{7,5},{8,10},{9,11},{10,... | collective-permute-start | bytes 147464 | tf_op jit(solution)/shard_map/ppermute | solution.py:195
  122.6 2.2 %collective-permute-start.10 = (bf16[64,384]{1,0:T(8,128)(2,1)S(1)}, bf16[64,384]{1,0:T(8,128)(2,1)S(1)}, u32[]{:S(2)}, u32[]{:S(2)}) collective-permute-start(bf16[64,384]{1,0:T(8,128)(2,1)S(1)} %get-tuple-element.33), channel_id=1, source_target_pairs={{0,3},{1,2},{2,1},{3,0},{4,7},{5,6},{6,5},{7,4},{8,11},{9,10},{10,... | collective-permute-start | bytes 147464 | tf_op jit(solution)/shard_map/ppermute | solution.py:195
  124.9 4.8 %collective-permute-done.10 = bf16[64,384]{1,0:T(8,128)(2,1)S(1)} collective-permute-done((bf16[64,384]{1,0:T(8,128)(2,1)S(1)}, bf16[64,384]{1,0:T(8,128)(2,1)S(1)}, u32[]{:S(2)}, u32[]{:S(2)}) %collective-permute-start.10) | collective-permute-done | bytes 49184 | tf_op jit(solution)/shard_map/ppermute | solution.py:195
  129.7 0.6 add_convert_fusion
  130.4 0.7 convert_element_type.28
  (18 shorter events, 0.1 us)
Async XLA Ops:
  2.1 27.3 %all-to-all-start = ((bf16[16,16,128]{2,1,0:T(8,128)(2,1)}), bf16[16,16,128]{2,1,0:T(8,128)(2,1)S(1)}, u32[]{:S(2)}, u32[]{:S(2)}) async-start(bf16[16,16,128]{2,1,0:T(8,128)(2,1)} %broadcast_in_dim.72), calls=%async_computation | async-start | bytes 131072 | tf_op jit(solution)/shard_map/all_to_all | solution.py:181
  17.8 0.8 copy-start.3
  17.9 0.7 copy-start.4
  30.3 18.5 %all-to-all-start.1 = ((bf16[8,256,128]{2,1,0:T(8,128)(2,1)}), bf16[8,256,128]{2,1,0:T(8,128)(2,1)S(1)}, u32[]{:S(2)}, u32[]{:S(2)}) async-start(bf16[8,256,128]{2,1,0:T(8,128)(2,1)} %get-tuple-element.19), calls=%async_computation.1 | async-start | bytes 1048576 | tf_op jit(solution)/shard_map/all_to_all | solution.py:181
  35.4 0.7 copy-start.5
  36.3 25.2 %collective-permute-start.3 = (bf16[2,128,384]{2,1,0:T(8,128)(2,1)S(1)}, bf16[2,128,384]{2,1,0:T(8,128)(2,1)S(1)}, u32[]{:S(2)}, u32[]{:S(2)}) collective-permute-start(bf16[2,128,384]{2,1,0:T(8,128)(2,1)S(1)} %get-tuple-element.20.near0), channel_id=1, source_target_pairs={{0,16},{4,20},{8,24},{12,28},{16,32},{20,36},{24,40},{28,44},{32,4... | collective-permute-start | bytes 589832 | tf_op jit(solution)/shard_map/ppermute | solution.py:191
  39.2 22.2 %collective-permute-start.2 = (bf16[2,128,384]{2,1,0:T(8,128)(2,1)S(1)}, bf16[2,128,384]{2,1,0:T(8,128)(2,1)S(1)}, u32[]{:S(2)}, u32[]{:S(2)}) collective-permute-start(bf16[2,128,384]{2,1,0:T(8,128)(2,1)S(1)} %get-tuple-element.20.near0), channel_id=1, source_target_pairs={{0,12},{4,16},{8,20},{12,24},{16,28},{20,32},{24,36},{28,40},{32,4... | collective-permute-start | bytes 589832 | tf_op jit(solution)/shard_map/ppermute | solution.py:191
  43.8 17.6 %collective-permute-start.1 = (bf16[2,128,384]{2,1,0:T(8,128)(2,1)S(1)}, bf16[2,128,384]{2,1,0:T(8,128)(2,1)S(1)}, u32[]{:S(2)}, u32[]{:S(2)}) collective-permute-start(bf16[2,128,384]{2,1,0:T(8,128)(2,1)S(1)} %get-tuple-element.20.near0), channel_id=1, source_target_pairs={{0,8},{4,12},{8,16},{12,20},{16,24},{20,28},{24,32},{28,36},{32,40... | collective-permute-start | bytes 589832 | tf_op jit(solution)/shard_map/ppermute | solution.py:191
  46.3 15.2 %collective-permute-start = (bf16[2,128,384]{2,1,0:T(8,128)(2,1)S(1)}, bf16[2,128,384]{2,1,0:T(8,128)(2,1)S(1)}, u32[]{:S(2)}, u32[]{:S(2)}) collective-permute-start(bf16[2,128,384]{2,1,0:T(8,128)(2,1)S(1)} %get-tuple-element.20.near0), channel_id=1, source_target_pairs={{0,4},{4,8},{8,12},{12,16},{16,20},{20,24},{24,28},{28,32},{32,36}... | collective-permute-start | bytes 589832 | tf_op jit(solution)/shard_map/ppermute | solution.py:191
  49.4 12.1 %copy-start = (bf16[384,128]{1,0:T(8,128)(2,1)S(1)}, bf16[384,128]{1,0:T(8,128)(2,1)}, u32[]{:S(2)}) copy-start(bf16[384,128]{1,0:T(8,128)(2,1)} %q.1) | copy-start | bytes 294916
  49.4 12.1 %copy-start.1 = (bf16[384,128]{1,0:T(8,128)(2,1)S(1)}, bf16[384,128]{1,0:T(8,128)(2,1)}, u32[]{:S(2)}) copy-start(bf16[384,128]{1,0:T(8,128)(2,1)} %o.1) | copy-start | bytes 294916
  49.4 12.1 %copy-start.2 = (bf16[384,128]{1,0:T(8,128)(2,1)S(1)}, bf16[384,128]{1,0:T(8,128)(2,1)}, u32[]{:S(2)}) copy-start(bf16[384,128]{1,0:T(8,128)(2,1)} %do.1) | copy-start | bytes 294916
  67.4 20.0 %all-to-all-start.2 = ((bf16[4,512,128]{2,1,0:T(8,128)(2,1)}), bf16[4,512,128]{2,1,0:T(8,128)(2,1)S(1)}, u32[]{:S(2)}, u32[]{:S(2)}) async-start(bf16[4,512,128]{2,1,0:T(8,128)(2,1)} %get-tuple-element.22), calls=%async_computation.2 | async-start | bytes 1048576 | tf_op jit(solution)/shard_map/all_to_all | solution.py:181
  71.2 11.0 %collective-permute-start.4 = (bf16[2,384,128]{2,1,0:T(8,128)(2,1)S(1)}, bf16[2,384,128]{2,1,0:T(8,128)(2,1)S(1)}, u32[]{:S(2)}, u32[]{:S(2)}) collective-permute-start(bf16[2,384,128]{2,1,0:T(8,128)(2,1)S(1)} %get-tuple-element.24), channel_id=1, source_target_pairs={{8,0},{12,4},{16,8},{20,12},{24,16},{28,20},{32,24},{36,28},{40,32... | collective-permute-start | bytes 589832 | tf_op jit(solution)/shard_map/ppermute | solution.py:191
  72.5 14.9 %collective-permute-start.5 = (bf16[2,384,128]{2,1,0:T(8,128)(2,1)S(1)}, bf16[2,384,128]{2,1,0:T(8,128)(2,1)S(1)}, u32[]{:S(2)}, u32[]{:S(2)}) collective-permute-start(bf16[2,384,128]{2,1,0:T(8,128)(2,1)S(1)} %get-tuple-element.25), channel_id=1, source_target_pairs={{16,0},{20,4},{24,8},{28,12},{32,16},{36,20},{40,24},{44,28},{48,3... | collective-permute-start | bytes 589832 | tf_op jit(solution)/shard_map/ppermute | solution.py:191
  88.9 19.7 %all-to-all-start.3 = ((bf16[8,256,128]{2,1,0:T(8,128)(2,1)}), bf16[8,256,128]{2,1,0:T(8,128)(2,1)S(1)}, u32[]{:S(2)}, u32[]{:S(2)}) async-start(bf16[8,256,128]{2,1,0:T(8,128)(2,1)} %bitcast.5), calls=%async_computation.3 | async-start | bytes 1048576 | tf_op jit(solution)/shard_map/all_to_all | solution.py:181
  94.8 13.6 %collective-permute-start.6 = (bf16[2,384,128]{2,1,0:T(8,128)(2,1)S(1)}, bf16[2,384,128]{2,1,0:T(8,128)(2,1)S(1)}, u32[]{:S(2)}, u32[]{:S(2)}) collective-permute-start(bf16[2,384,128]{2,1,0:T(8,128)(2,1)S(1)} %get-tuple-element.28), channel_id=1, source_target_pairs={{4,0},{8,4},{12,8},{16,12},{20,16},{24,20},{28,24},{32,28},{36,32}... | collective-permute-start | bytes 589832 | tf_op jit(solution)/shard_map/ppermute | solution.py:191
  96.1 12.5 %collective-permute-start.7 = (bf16[2,384,128]{2,1,0:T(8,128)(2,1)S(1)}, bf16[2,384,128]{2,1,0:T(8,128)(2,1)S(1)}, u32[]{:S(2)}, u32[]{:S(2)}) collective-permute-start(bf16[2,384,128]{2,1,0:T(8,128)(2,1)S(1)} %get-tuple-element.29), channel_id=1, source_target_pairs={{12,0},{16,4},{20,8},{24,12},{28,16},{32,20},{36,24},{40,28},{44,3... | collective-permute-start | bytes 589832 | tf_op jit(solution)/shard_map/ppermute | solution.py:191
  109.5 20.9 %all-to-all-start.4 = ((f32[16,16,128]{2,1,0:T(8,128)}), f32[16,16,128]{2,1,0:T(8,128)S(1)}, u32[]{:S(2)}, u32[]{:S(2)}) async-start(f32[16,16,128]{2,1,0:T(8,128)} %bitcast.8), calls=%async_computation.4 | async-start | bytes 262144 | tf_op jit(solution)/shard_map/all_to_all | solution.py:181
  113.5 11.4 %collective-permute-start.8 = (bf16[64,384]{1,0:T(8,128)(2,1)S(1)}, bf16[64,384]{1,0:T(8,128)(2,1)S(1)}, u32[]{:S(2)}, u32[]{:S(2)}) collective-permute-start(bf16[64,384]{1,0:T(8,128)(2,1)S(1)} %get-tuple-element.31), channel_id=1, source_target_pairs={{0,1},{1,0},{2,3},{3,2},{4,5},{5,4},{6,7},{7,6},{8,9},{9,8},{10,11... | collective-permute-start | bytes 147464 | tf_op jit(solution)/shard_map/ppermute | solution.py:195
  117.9 7.0 %collective-permute-start.9 = (bf16[64,384]{1,0:T(8,128)(2,1)S(1)}, bf16[64,384]{1,0:T(8,128)(2,1)S(1)}, u32[]{:S(2)}, u32[]{:S(2)}) collective-permute-start(bf16[64,384]{1,0:T(8,128)(2,1)S(1)} %get-tuple-element.32), channel_id=1, source_target_pairs={{0,2},{1,3},{2,0},{3,1},{4,6},{5,7},{6,4},{7,5},{8,10},{9,11},{10,... | collective-permute-start | bytes 147464 | tf_op jit(solution)/shard_map/ppermute | solution.py:195
  122.6 7.0 %collective-permute-start.10 = (bf16[64,384]{1,0:T(8,128)(2,1)S(1)}, bf16[64,384]{1,0:T(8,128)(2,1)S(1)}, u32[]{:S(2)}, u32[]{:S(2)}) collective-permute-start(bf16[64,384]{1,0:T(8,128)(2,1)S(1)} %get-tuple-element.33), channel_id=1, source_target_pairs={{0,3},{1,2},{2,1},{3,0},{4,7},{5,6},{6,5},{7,4},{8,11},{9,10},{10,... | collective-permute-start | bytes 147464 | tf_op jit(solution)/shard_map/ppermute | solution.py:195

commit v5 on v4

--- a/solution.py
+++ b/solution.py
@@ -7,8 +7,10 @@
 from jax.sharding import Mesh
 from jax.sharding import PartitionSpec as P
 
-XLO, Z, Y, HEADS = 2, 16, 4, 4
+XLO, Z, Y, XHI, CORES = 2, 16, 4, 2, 2
+HEADS = XHI * CORES
 DP = XLO * Z * Y
+COLUMNS = XLO * Y
 WIDTH = 128
 PART = WIDTH // HEADS
 PIECES = 32
@@ -38,7 +40,7 @@
 
 
 def fan_kernel(shares, own, fanned, near):
-    for column in range(XLO * Y):
+    for column in range(COLUMNS):
         fanned[column] = shares[...]
     near[...] = own[...]
 
@@ -48,46 +50,63 @@
         picked[piece * TILE : (piece + 1) * TILE] = pieces[slots[piece]]
 
 
-def place_kernel(slots, landed, own, far2, far4, spread, partial):
+def pair_kernel(place, kept, kept_near, landed, mine, other, own, far1, far23, far4, cut):
+    for xhi in range(XHI):
+        theirs = landed[xhi * PIECES * TILE : (xhi + 1) * PIECES * TILE]
+        cut[xhi] = kept[xhi].astype(jnp.float32) + theirs.astype(jnp.float32)
+    mine[...] = cut[place[1]]
+    other[...] = cut[1 - place[1]].astype(other.dtype)
+    for distance, (out, at) in enumerate(((own, 0), (far1, 0), (far23, 0), (far23, WIDTH), (far4, 0))):
+        for column in range(RROWS // WIDTH):
+            lanes = slice(column * WIDTH, (column + 1) * WIDTH)
+            theirs = landed[near_row(distance, column) : near_row(distance, column) + WIDTH]
+            out[at : at + WIDTH, lanes] = (kept_near[distance, :, lanes] + theirs.astype(jnp.float32)).astype(out.dtype)
+
+
+def place_kernel(slots, mine, theirs, own, far1, far23, far4, spread, partial, passed):
     spread[...] = jnp.zeros_like(spread)
-    total = landed[0].astype(jnp.float32)
-    for head in range(1, HEADS):
-        total = total + landed[head].astype(jnp.float32)
-    rounded = total.astype(jnp.bfloat16)
+    total = (mine[...] + theirs[...].astype(jnp.float32)).astype(jnp.bfloat16)
     for piece in range(PIECES):
-        spread[slots[piece]] = rounded[piece * TILE : (piece + 1) * TILE]
-    partial[...] = own[...] + far2[...].astype(jnp.float32) + far4[...].astype(jnp.float32)
-
-
-def column_kernel(place, landed, partial, far1, far3, column, mine, out1, out2, out3, slots):
+        spread[slots[piece]] = total[piece * TILE : (piece + 1) * TILE]
+    partial[...] = own[...] + far23[:WIDTH].astype(jnp.float32) + far4[...].astype(jnp.float32)
+    passed[...] = (far1[...].astype(jnp.float32) + far23[WIDTH:].astype(jnp.float32)).astype(passed.dtype)
+
+
+def near_row(distance, column):
+    return XHI * PIECES * TILE + (distance * (RROWS // WIDTH) + column) * WIDTH
+
+
+def column_kernel(place, landed, partial, passed, column, mine, other, cut):
     held = landed[0].astype(jnp.float32)
-    for sender in range(1, XLO * Y):
+    for sender in range(1, COLUMNS):
         held = held + landed[sender].astype(jnp.float32)
     column[...] = held
-    total = partial[...] + far1[...].astype(jnp.float32) + far3[...].astype(jnp.float32)
-    turned = [total[kind].T.astype(jnp.bfloat16) for kind in range(2)]
-    for head in range(HEADS):
+    total = partial[...] + passed[...].astype(jnp.float32)
+    for xhi in range(XHI):
         for kind in range(2):
-            slots[head, kind * PART : (kind + 1) * PART] = turned[kind][head * PART : (head + 1) * PART]
-    for step, out in enumerate((mine, out1, out2, out3)):
-        out[...] = slots[place[0] ^ step]
+            begin = (kind * XHI + xhi) * PART
+            cut[xhi, kind * PART : (kind + 1) * PART] = total[begin : begin + PART]
+    mine[...] = cut[place[1]]
+    other[...] = cut[1 - place[1]].astype(other.dtype)
 
 
 def attention_kernel(
-    q, o, do, start, gathered, near0, near1, near2, near3, near4, dq, close, own, far1, far2, far3, far4, exps, keys, values
+    place, q, o, do, start, gathered, near0, near1, near23, near4,
+    dq, kept, kept_near, sent, exps, keys, values, heads, turned,
 ):
     swap = swap_matrix()
-    packed = jnp.concatenate([gathered[c, : PIECES * TILE] for c in range(HEADS)], axis=1)
+    core = place[0]
+    packed = jnp.concatenate([gathered[c] for c in range(HEADS)], axis=1)
     columns = swapped(packed, swap)
     for quarter in range(HEADS):
         part = columns[:, quarter * WIDTH : (quarter + 1) * WIDTH].reshape(PIECES, 2, TILE // 2, WIDTH)
         rows = slice(quarter * QUARTER, (quarter + 1) * QUARTER)
         keys[rows] = part[:, 0].reshape(QUARTER, WIDTH).astype(jnp.bfloat16)
         values[rows] = part[:, 1].reshape(QUARTER, WIDTH).astype(jnp.bfloat16)
-    for distance, near in enumerate((near0, near1, near2, near3, near4)):
+    for distance, (near, at) in enumerate(((near0, 0), (near1, 0), (near23, 0), (near23, 2), (near4, 0))):
         rows = slice(PROMPT + distance * RROWS, PROMPT + (distance + 1) * RROWS)
-        keys[rows] = near[0].T
-        values[rows] = near[1].T
+        keys[rows] = near[at].T
+        values[rows] = near[at + 1].T
     chunks = [(i * QUARTER, QUARTER, None) for i in range(HEADS)]
     chunks += [(PROMPT + d * RROWS, RROWS, d) for d in range(HOPS + 1)]
     queries, dout = q[...], do[...]
@@ -132,12 +151,25 @@
             )
             prompt_sums.append(pair.reshape(PIECES * TILE, WIDTH).astype(jnp.bfloat16))
             continue
-        out = (own, far1, far2, far3, far4)[distance]
-        out[0] = dk.astype(out.dtype)
-        out[1] = dv.astype(out.dtype)
+        for kind, terms in enumerate((dk, dv)):
+            turned[distance, kind] = terms.T
+            for xhi in range(XHI):
+                rows = slice((kind * XHI + xhi) * PART, (kind * XHI + xhi + 1) * PART)
+                at = pl.multiple_of((xhi * CORES + core) * PART, PART)
+                kept_near[distance, rows] = turned[distance, kind, pl.ds(at, PART)]
+                at = pl.multiple_of((xhi * CORES + 1 - core) * PART, PART)
+                leaving = turned[distance, kind, pl.ds(at, PART)].astype(jnp.bfloat16)
+                for column in range(RROWS // WIDTH):
+                    first_row = near_row(distance, column)
+                    sent[first_row + rows.start : first_row + rows.stop] = leaving[
+                        :, column * WIDTH : (column + 1) * WIDTH
+                    ]
     split = swapped(jnp.concatenate(prompt_sums, axis=1), swap).astype(jnp.bfloat16)
     for head in range(HEADS):
-        close[head] = split[:, head * WIDTH : (head + 1) * WIDTH]
+        heads[head] = split[:, head * WIDTH : (head + 1) * WIDTH]
+    for xhi in range(XHI):
+        kept[xhi] = heads[xhi * CORES + core]
+        sent[xhi * PIECES * TILE : (xhi + 1) * PIECES * TILE] = heads[xhi * CORES + 1 - core]
     dq[...] = (dq_t.T * FACTOR).astype(jnp.bfloat16)
 
 
@@ -156,20 +188,25 @@
     )(*operands)
 
 
-def attention(q, o, do, start, gathered, near):
+def attention(place, q, o, do, start, gathered, near):
     half = jnp.bfloat16
     total = PROMPT + (HOPS + 1) * RROWS
-    block = (2, RROWS, WIDTH)
-    shapes = [((RROWS, WIDTH), half), ((HEADS, PIECES * TILE, WIDTH), half), (block, jnp.float32)]
     return local_call(
         attention_kernel,
         "attention",
-        shapes + [(block, half)] * HOPS,
-        (q, o, do, start, gathered, *near),
+        [
+            ((RROWS, WIDTH), half),
+            ((XHI, PIECES * TILE, WIDTH), half),
+            ((HOPS + 1, 2 * XHI * PART, RROWS), jnp.float32),
+            ((near_row(HOPS + 1, 0), WIDTH), half),
+        ],
+        (place, q, o, do, start, gathered, *near),
         [
             pltpu.VMEM((total, RROWS), jnp.float32),
             pltpu.VMEM((total, WIDTH), half),
             pltpu.VMEM((total, WIDTH), half),
+            pltpu.VMEM((HEADS, PIECES * TILE, WIDTH), half),
+            pltpu.VMEM((HOPS + 1, 2, WIDTH, RROWS), jnp.float32),
         ],
         pl.CostEstimate(
             flops=12 * total * RROWS * WIDTH, bytes_accessed=6_000_000, transcendentals=total * RROWS
@@ -191,8 +228,8 @@
     return lax.ppermute(array, ("xlo", "z", "y"), pairs)
 
 
-def swapped_heads(array, step):
-    return lax.ppermute(array, "head", [(i, i ^ step) for i in range(HEADS)])
+def traded(array, axis):
+    return lax.ppermute(array, axis, [(0, 1), (1, 0)])
 
 
 def body(prompt_kv, resp_kv, resp_query, resp_out, resp_dout, resp_lengths, prompt_owner):
@@ -201,18 +238,19 @@
     own_index = (xlo * Z + z) * Y + y
     own_group = own_index // PIECES
 
-    head = lax.axis_index("head")
-    place = head.reshape(1).astype(jnp.int32)
-    own = lax.all_gather(resp_kv.transpose(0, 2, 1), "head", axis=1, tiled=True)
+    place = jnp.stack([lax.axis_index("core"), lax.axis_index("xhi")]).astype(jnp.int32)
+    own = lax.all_gather(resp_kv.transpose(0, 2, 1), ("xhi", "core"), axis=1, tiled=True)
     along_z = given_to_all(prompt_kv.reshape(TILE, WIDTH), "z").reshape(Z * TILE, WIDTH)
     fanned, near = local_call(
         fan_kernel,
         "fan",
-        [((XLO * Y, Z * TILE, WIDTH), half), ((2, WIDTH, RROWS), half)],
+        [((COLUMNS, Z * TILE, WIDTH), half), ((2, WIDTH, RROWS), half)],
         (along_z, own),
     )
     pieces = exchanged(fanned, ("xlo", "y")).reshape(DP, TILE, WIDTH)
-    near = [near] + [shifted(near, distance) for distance in range(1, HOPS + 1)]
+    near1, near4 = shifted(near, 1), shifted(near, HOPS)
+    near23 = shifted(jnp.concatenate([near, near1], axis=0), 2)
+    near = [near, near1, near23, near4]
 
     holder = jnp.arange(DP, dtype=jnp.int32)
     slot = ((holder // (Z * Y)) * Y + holder % Y) * Z + (holder // Y) % Z
@@ -220,7 +258,7 @@
     owned = own_pieces[:, None] == prompt_owner[None, :]
     slots = jnp.sum(jnp.where(owned, slot[None, :], 0), axis=1).astype(jnp.int32)
     picked = local_call(select_kernel, "select", [((PIECES * TILE, WIDTH), half)], (slots, pieces))[0]
-    gathered = lax.all_gather(picked, "head", axis=0, tiled=False)
+    gathered = lax.all_gather(picked, ("xhi", "core"), axis=0, tiled=False)
 
     offset = (own_index % PIECES) * RROWS + jnp.arange(RROWS, dtype=jnp.int32)
     lengths = jnp.sum(
@@ -232,48 +270,53 @@
     begun = jnp.max(jnp.where(bounds[:, None] <= offset[None, :], bounds[:, None], 0), axis=0)
     start = (begun - (own_index % PIECES) * RROWS).astype(jnp.int32)[None, :]
 
-    query_grad, close, own_terms, *fars = attention(
-        resp_query, resp_out, resp_dout, start, gathered, near
-    )
-
-    landed = exchanged(close, "head")
-    fars = [shifted(far, -distance) for distance, far in enumerate(fars, 1)]
-    spread, partial = local_call(
+    query_grad, kept, kept_near, sent = attention(
+        place, resp_query, resp_out, resp_dout, start, gathered, near
+    )
+
+    pieces_shape, wide, narrow = (PIECES * TILE, WIDTH), (2 * XHI * PART, RROWS), (2 * PART, RROWS)
+    mine, other, own_terms, far1, far23, far4 = local_call(
+        pair_kernel,
+        "pair",
+        [(pieces_shape, jnp.float32), (pieces_shape, half), (wide, jnp.float32)]
+        + [(wide, half), ((2 * wide[0], RROWS), half), (wide, half)],
+        (place, kept, kept_near, traded(sent, "core")),
+        [pltpu.VMEM((XHI,) + pieces_shape, jnp.float32)],
+    )
+    theirs = traded(other, "xhi")
+    spread, partial, passed = local_call(
         place_kernel,
         "place",
-        [((DP, TILE, WIDTH), half), ((2, RROWS, WIDTH), jnp.float32)],
-        (slots, landed, own_terms, fars[1], fars[3]),
-    )
-    by_column = exchanged(spread.reshape(XLO * Y, Z * TILE, WIDTH), ("xlo", "y"))
-    cut = (2 * PART, RROWS)
-    column_sum, mine, *others = local_call(
+        [((DP, TILE, WIDTH), half), (wide, jnp.float32), (wide, half)],
+        (slots, mine, theirs, own_terms, far1, shifted(far23, -2), shifted(far4, -HOPS)),
+    )
+    by_column = exchanged(spread.reshape(COLUMNS, Z * TILE, WIDTH), ("xlo", "y"))
+    column_sum, mine, other = local_call(
         column_kernel,
         "column",
-        [((Z * TILE, WIDTH), jnp.float32)] + [(cut, half)] * HEADS,
-        (place, by_column, partial, fars[0], fars[2]),
-        [pltpu.VMEM((HEADS,) + cut, half)],
+        [((Z * TILE, WIDTH), jnp.float32), (narrow, jnp.float32), (narrow, half)],
+        (place, by_column, partial, shifted(passed, -1)),
+        [pltpu.VMEM((XHI,) + narrow, jnp.float32)],
     )
     by_z = exchanged(column_sum.reshape(Z, TILE, WIDTH), "z")
     prompt_grad = jnp.sum(by_z, axis=0).astype(half)
 
-    resp_total = mine.astype(jnp.float32)
-    for step, other in enumerate(others, 1):
-        resp_total = resp_total + swapped_heads(other, step).astype(jnp.float32)
+    resp_total = mine + traded(other, "xhi").astype(jnp.float32)
     resp_grad = resp_total.astype(half).reshape(2, PART, RROWS).transpose(0, 2, 1)
     return query_grad, resp_grad, prompt_grad.reshape(2, PROWS, PART)
 
 
 def solution(mesh):
-    fine = Mesh(np.asarray(mesh.devices).reshape(XLO, Z, Y, HEADS), ("xlo", "z", "y", "head"))
-    dp = ("xlo", "z", "y")
+    fine = Mesh(np.asarray(mesh.devices).reshape(XLO, Z, Y, XHI, CORES), ("xlo", "z", "y", "xhi", "core"))
+    dp, head = ("xlo", "z", "y"), ("xhi", "core")
     in_specs = (
-        P(None, dp, "head"),
-        P(None, dp, "head"),
-        P(dp, "head"),
-        P(dp, "head"),
-        P(dp, "head"),
+        P(None, dp, head),
+        P(None, dp, head),
+        P(dp, head),
+        P(dp, head),
+        P(dp, head),
         P(),
         P(),
     )
-    out_specs = (P(dp, "head"), P(None, dp, "head"), P(None, dp, "head"))
+    out_specs = (P(dp, head), P(None, dp, head), P(None, dp, head))
     return jax.shard_map(body, mesh=fine, in_specs=in_specs, out_specs=out_specs, check_vma=False)

time: 132 us -> 131 us (level)
  the two profiles are of different devices: /device:TPU:1 before, /device:TPU:24 now
where the time goes in v5:
time: 131 us; the launch traced here: 130 us
  starting transfers between devices  60.8 us (46%)
  waiting for transfers between devices  36.8 us (28%)
  blocking collectives  15.7 us (12%)
  Pallas kernels  11.2 us (9%)
  local copies, waits for them, and re-layouts  3.41 us (3%)
    all_to_all x4, starting transfers between devices, exchanged(): return lax.all_to_all(blocks, axes, split_axis=0, concat_axis=0, tiled=True)  35.7 us
    all_to_all x4, waiting for transfers between devices, exchanged(): return lax.all_to_all(blocks, axes, split_axis=0, concat_axis=0, tiled=True)  20.1 us
    ppermute x6, starting transfers between devices, shifted(): return lax.ppermute(array, ('xlo', 'z', 'y'), pairs)  14.7 us
    pallas_call x6, Pallas kernels, local_call(): pl.pallas_call(kernel, out_shape=[jax.ShapeDtypeStruct(shape, dtype) for...  11.2 us
    ppermute x6, waiting for transfers between devices, shifted(): return lax.ppermute(array, ('xlo', 'z', 'y'), pairs)  11.2 us
    ppermute x3, starting transfers between devices, traded(): return lax.ppermute(array, axis, [(0, 1), (1, 0)])  10.4 us
    all_gather x1, blocking collectives, body(): gathered = lax.all_gather(picked, ('xhi', 'core'), axis=0, tiled=False)  8.54 us
    all_gather x1, blocking collectives, body(): lax.all_gather(resp_kv.transpose(0, 2, 1), ('xhi', 'core'), axis=1, tiled...  7.11 us
  transfers between devices with their start and end apart: 13, of which 7 were waited for; matrix products, arithmetic and copies ran while one was open for 1% of the time, Pallas kernels for 0%

profile of v5, /device:TPU:24, one launch (start us, length us, event | category | flops | bytes accessed | tf_op | source)
XLA Modules:
  0.0 130.1 jit_solution(2534448246370069367)
XLA Ops:
  0.6 0.8 broadcast_in_dim.71
  1.4 0.6 broadcast_in_dim.72
  2.1 15.2 %all-to-all-start = ((bf16[16,16,128]{2,1,0:T(8,128)(2,1)}), bf16[16,16,128]{2,1,0:T(8,128)(2,1)S(1)}, u32[]{:S(2)}, u32[]{:S(2)}) async-start(bf16[16,16,128]{2,1,0:T(8,128)(2,1)} %broadcast_in_dim.72), calls=%async_computation | async-start | bytes 131072 | tf_op jit(solution)/shard_map/all_to_all | solution.py:218
  17.3 0.0 copy-start.3
  17.3 0.0 copy-start.4
  17.4 0.7 copy-done.4
  18.0 0.1 select_reduce_fusion.3
  18.1 0.1 select_reduce_fusion.2
  18.2 0.1 select_reduce_fusion
  18.4 7.1 %all_gather.9.own = bf16[2,128,384]{2,1,0:T(8,128)(2,1)S(1)} all-gather(bf16[2,32,384]{2,1,0:T(8,128)(2,1)S(1)} %bitcast.15), channel_id=1, replica_groups=mesh['xlo'=2,'z'=16,'y'=4,'xhi'=2,'core'=2] {'xhi','core'}, dimensions={1}, use_global_device_ids=true | all-gather | bytes 245760 | tf_op jit(solution)/shard_map/all_gather | solution.py:242
  25.5 4.5 %all-to-all-done = bf16[16,16,128]{2,1,0:T(8,128)(2,1)S(1)} async-done(((bf16[16,16,128]{2,1,0:T(8,128)(2,1)}), bf16[16,16,128]{2,1,0:T(8,128)(2,1)S(1)}, u32[]{:S(2)}, u32[]{:S(2)}) %all-to-all-start) | async-done | bytes 65568 | tf_op jit(solution)/shard_map/all_to_all | solution.py:218
  30.0 0.9 fan.1
  30.9 2.3 %collective-permute-start = (bf16[2,128,384]{2,1,0:T(8,128)(2,1)S(1)}, bf16[2,128,384]{2,1,0:T(8,128)(2,1)S(1)}, u32[]{:S(2)}, u32[]{:S(2)}) collective-permute-start(bf16[2,128,384]{2,1,0:T(8,128)(2,1)S(1)} %get-tuple-element.22.near0), channel_id=1, source_target_pairs={{0,4},{4,8},{8,12},{12,16},{16,20},{20,24},{24,28},{28,32},{32,36}... | collective-permute-start | bytes 589832 | tf_op jit(solution)/shard_map/ppermute | solution.py:228
  33.2 6.5 %all-to-all-start.1 = ((bf16[8,256,128]{2,1,0:T(8,128)(2,1)}), bf16[8,256,128]{2,1,0:T(8,128)(2,1)S(1)}, u32[]{:S(2)}, u32[]{:S(2)}) async-start(bf16[8,256,128]{2,1,0:T(8,128)(2,1)} %get-tuple-element.21), calls=%async_computation.1 | async-start | bytes 1048576 | tf_op jit(solution)/shard_map/all_to_all | solution.py:218
  39.8 3.5 %collective-permute-start.1 = (bf16[4,128,384]{2,1,0:T(8,128)(2,1)S(1)}, bf16[4,128,384]{2,1,0:T(8,128)(2,1)S(1)}, u32[]{:S(2)}, u32[]{:S(2)}) collective-permute-start(bf16[4,128,384]{2,1,0:T(8,128)(2,1)S(1)} %pad_maximum_fusion), channel_id=1, source_target_pairs={{0,8},{4,12},{8,16},{12,20},{16,24},{20,28},{24,32},{28,36},{32,40... | collective-permute-start | bytes 1179656 | tf_op jit(solution)/shard_map/ppermute | solution.py:228
  43.3 0.0 copy-start.5
  43.3 0.1 pad_add_fusion.place
  43.4 0.6 copy-done.5
  44.0 0.2 select_reduce_fusion.1.slots
  44.2 2.9 %collective-permute-start.2 = (bf16[2,128,384]{2,1,0:T(8,128)(2,1)S(1)}, bf16[2,128,384]{2,1,0:T(8,128)(2,1)S(1)}, u32[]{:S(2)}, u32[]{:S(2)}) collective-permute-start(bf16[2,128,384]{2,1,0:T(8,128)(2,1)S(1)} %get-tuple-element.22.near0), channel_id=1, source_target_pairs={{0,16},{4,20},{8,24},{12,28},{16,32},{20,36},{24,40},{28,44},{32,4... | collective-permute-start | bytes 589832 | tf_op jit(solution)/shard_map/ppermute | solution.py:228
  47.1 10.5 %all-to-all-done.1 = bf16[8,256,128]{2,1,0:T(8,128)(2,1)S(1)} async-done(((bf16[8,256,128]{2,1,0:T(8,128)(2,1)}), bf16[8,256,128]{2,1,0:T(8,128)(2,1)S(1)}, u32[]{:S(2)}, u32[]{:S(2)}) %all-to-all-start.1) | async-done | bytes 524320 | tf_op jit(solution)/shard_map/all_to_all | solution.py:218
  57.6 0.6 select.33
  58.2 0.0 copy-start
  58.2 0.0 copy-start.1
  58.2 0.0 copy-start.2
  58.2 8.5 %all-gather = bf16[2048,128]{1,0:T(8,128)(2,1)S(1)} all-gather(bf16[512,128]{1,0:T(8,128)(2,1)S(1)} %select.33), channel_id=2, replica_groups=mesh['xlo'=2,'z'=16,'y'=4,'xhi'=2,'core'=2] {'xhi','core'}, dimensions={0}, use_global_device_ids=true | all-gather | bytes 655360 | tf_op jit(solution)/shard_map/all_gather | solution.py:261
  66.7 0.0 collective-permute-done.2.near4
  66.7 0.0 collective-permute-done.1.near23
  66.8 6.3 %attention.1 = (bf16[384,128]{1,0:T(8,128)(2,1)}, bf16[2,512,128]{2,1,0:T(8,128)(2,1)S(1)}, f32[5,128,384]{2,1,0:T(8,128)S(1)}, bf16[2944,128]{1,0:T(8,128)(2,1)S(1)}) custom-call(s32[2]{0:T(128)S(1)} %pad_add_fusion.place, bf16[384,128]{1,0:T(8,128)(2,1)S(1)} %copy-done, bf16[384,128]{1,0:T(8,128)(2,1)S(1)} %copy-done.1, bf16[384,128]{1,0:T(8,128)(2,1)S(1)} %copy-done.2, ...), custom_call_target="tpu_custom_call" | custom-call | flops 1736441856 | bytes 6000000 | tf_op jit(solution)/shard_map/attention/pallas_call | solution.py:179
  73.1 2.2 %collective-permute-start.3 = (bf16[2944,128]{1,0:T(8,128)(2,1)S(1)}, bf16[2944,128]{1,0:T(8,128)(2,1)S(1)}, u32[]{:S(2)}, u32[]{:S(2)}) collective-permute-start(bf16[2944,128]{1,0:T(8,128)(2,1)S(1)} %get-tuple-element.26), channel_id=1, source_target_pairs={{0,1},{1,0},{2,3},{3,2},{4,5},{5,4},{6,7},{7,6},{8,9},{9,8},{10,11... | collective-permute-start | bytes 2261000 | tf_op jit(solution)/shard_map/ppermute | solution.py:232
  75.4 1.9 %collective-permute-done.3.landed = bf16[2944,128]{1,0:T(8,128)(2,1)S(1)} collective-permute-done((bf16[2944,128]{1,0:T(8,128)(2,1)S(1)}, bf16[2944,128]{1,0:T(8,128)(2,1)S(1)}, u32[]{:S(2)}, u32[]{:S(2)}) %collective-permute-start.3) | collective-permute-done | bytes 753696 | tf_op jit(solution)/shard_map/ppermute | solution.py:232
  77.2 0.7 pair.1
  78.0 1.9 %collective-permute-start.5 = (bf16[256,384]{1,0:T(8,128)(2,1)S(1)}, bf16[256,384]{1,0:T(8,128)(2,1)S(1)}, u32[]{:S(2)}, u32[]{:S(2)}) collective-permute-start(bf16[256,384]{1,0:T(8,128)(2,1)S(1)} %get-tuple-element.31), channel_id=1, source_target_pairs={{8,0},{12,4},{16,8},{20,12},{24,16},{28,20},{32,24},{36,28},{40,32... | collective-permute-start | bytes 589832 | tf_op jit(solution)/shard_map/ppermute | solution.py:228
  79.9 4.2 %collective-permute-start.4 = (bf16[512,128]{1,0:T(8,128)(2,1)S(1)}, bf16[512,128]{1,0:T(8,128)(2,1)S(1)}, u32[]{:S(2)}, u32[]{:S(2)}) collective-permute-start(bf16[512,128]{1,0:T(8,128)(2,1)S(1)} %get-tuple-element.28), channel_id=1, source_target_pairs={{0,2},{2,0},{1,3},{3,1},{4,6},{6,4},{5,7},{7,5},{8,10},{10,8},{9,1... | collective-permute-start | bytes 393224 | tf_op jit(solution)/shard_map/ppermute | solution.py:232
  84.2 1.3 collective-permute-start.6
  85.5 5.4 %collective-permute-done.6.far4 = bf16[128,384]{1,0:T(8,128)(2,1)S(1)} collective-permute-done((bf16[128,384]{1,0:T(8,128)(2,1)S(1)}, bf16[128,384]{1,0:T(8,128)(2,1)S(1)}, u32[]{:S(2)}, u32[]{:S(2)}) %collective-permute-start.6) | collective-permute-done | bytes 98336 | tf_op jit(solution)/shard_map/ppermute | solution.py:228
  90.8 0.0 collective-permute-done.4.theirs
  90.8 1.4 %place.1 = (bf16[128,16,128]{2,1,0:T(8,128)(2,1)}, f32[128,384]{1,0:T(8,128)S(1)}, bf16[128,384]{1,0:T(8,128)(2,1)S(1)}) custom-call(s32[32]{0:T(128)S(1)} %select_reduce_fusion.1.slots, f32[512,128]{1,0:T(8,128)S(1)} %get-tuple-element.27.mine, bf16[512,128]{1,0:T(8,128)(2,1)S(1)} %collective-permute-done.4.theirs, f32[128,384]{1,0:T(8,128)S(1)} %get-tuple-element.29.own, ...), custom_call_target="tpu_custom_call" | custom-call | tf_op jit(solution)/shard_map/place/pallas_call | solution.py:179
  92.3 7.8 %all-to-all-start.2 = ((bf16[8,256,128]{2,1,0:T(8,128)(2,1)}), bf16[8,256,128]{2,1,0:T(8,128)(2,1)S(1)}, u32[]{:S(2)}, u32[]{:S(2)}) async-start(bf16[8,256,128]{2,1,0:T(8,128)(2,1)} %bitcast.6), calls=%async_computation.2 | async-start | bytes 1048576 | tf_op jit(solution)/shard_map/all_to_all | solution.py:218
  100.1 2.8 %collective-permute-start.7 = (bf16[128,384]{1,0:T(8,128)(2,1)S(1)}, bf16[128,384]{1,0:T(8,128)(2,1)S(1)}, u32[]{:S(2)}, u32[]{:S(2)}) collective-permute-start(bf16[128,384]{1,0:T(8,128)(2,1)S(1)} %get-tuple-element.35), channel_id=1, source_target_pairs={{4,0},{8,4},{12,8},{16,12},{20,16},{24,20},{28,24},{32,28},{36,32}... | collective-permute-start | bytes 294920 | tf_op jit(solution)/shard_map/ppermute | solution.py:228
  102.8 5.8 %collective-permute-done.7.passed = bf16[128,384]{1,0:T(8,128)(2,1)S(1)} collective-permute-done((bf16[128,384]{1,0:T(8,128)(2,1)S(1)}, bf16[128,384]{1,0:T(8,128)(2,1)S(1)}, u32[]{:S(2)}, u32[]{:S(2)}) %collective-permute-start.7) | collective-permute-done | bytes 98336 | tf_op jit(solution)/shard_map/ppermute | solution.py:228
  108.7 1.3 column.1
  110.0 6.2 %all-to-all-start.3 = ((f32[16,16,128]{2,1,0:T(8,128)}), f32[16,16,128]{2,1,0:T(8,128)S(1)}, u32[]{:S(2)}, u32[]{:S(2)}) async-start(f32[16,16,128]{2,1,0:T(8,128)} %bitcast.9), calls=%async_computation.3 | async-start | bytes 262144 | tf_op jit(solution)/shard_map/all_to_all | solution.py:218
  116.2 3.9 %collective-permute-start.8 = (bf16[64,384]{1,0:T(8,128)(2,1)S(1)}, bf16[64,384]{1,0:T(8,128)(2,1)S(1)}, u32[]{:S(2)}, u32[]{:S(2)}) collective-permute-start(bf16[64,384]{1,0:T(8,128)(2,1)S(1)} %get-tuple-element.37), channel_id=1, source_target_pairs={{0,2},{2,0},{1,3},{3,1},{4,6},{6,4},{5,7},{7,5},{8,10},{10,8},{9,1... | collective-permute-start | bytes 147464 | tf_op jit(solution)/shard_map/ppermute | solution.py:232
  120.1 3.6 %collective-permute-done.8 = bf16[64,384]{1,0:T(8,128)(2,1)S(1)} collective-permute-done((bf16[64,384]{1,0:T(8,128)(2,1)S(1)}, bf16[64,384]{1,0:T(8,128)(2,1)S(1)}, u32[]{:S(2)}, u32[]{:S(2)}) %collective-permute-start.8) | collective-permute-done | bytes 49184 | tf_op jit(solution)/shard_map/ppermute | solution.py:232
  123.7 0.6 add_convert_fusion
  124.3 5.1 %all-to-all-done.3 = f32[16,16,128]{2,1,0:T(8,128)S(1)} async-done(((f32[16,16,128]{2,1,0:T(8,128)}), f32[16,16,128]{2,1,0:T(8,128)S(1)}, u32[]{:S(2)}, u32[]{:S(2)}) %all-to-all-start.3) | async-done | bytes 131104 | tf_op jit(solution)/shard_map/all_to_all | solution.py:218
  129.4 0.7 convert_element_type.16
  (15 shorter events, 0.1 us)
Async XLA Ops:
  2.1 27.9 %all-to-all-start = ((bf16[16,16,128]{2,1,0:T(8,128)(2,1)}), bf16[16,16,128]{2,1,0:T(8,128)(2,1)S(1)}, u32[]{:S(2)}, u32[]{:S(2)}) async-start(bf16[16,16,128]{2,1,0:T(8,128)(2,1)} %broadcast_in_dim.72), calls=%async_computation | async-start | bytes 131072 | tf_op jit(solution)/shard_map/all_to_all | solution.py:218
  17.3 1.1 copy-start.3
  17.3 0.7 copy-start.4
  30.9 8.8 %collective-permute-start = (bf16[2,128,384]{2,1,0:T(8,128)(2,1)S(1)}, bf16[2,128,384]{2,1,0:T(8,128)(2,1)S(1)}, u32[]{:S(2)}, u32[]{:S(2)}) collective-permute-start(bf16[2,128,384]{2,1,0:T(8,128)(2,1)S(1)} %get-tuple-element.22.near0), channel_id=1, source_target_pairs={{0,4},{4,8},{8,12},{12,16},{16,20},{20,24},{24,28},{28,32},{32,36}... | collective-permute-start | bytes 589832 | tf_op jit(solution)/shard_map/ppermute | solution.py:228
  33.2 24.4 %all-to-all-start.1 = ((bf16[8,256,128]{2,1,0:T(8,128)(2,1)}), bf16[8,256,128]{2,1,0:T(8,128)(2,1)S(1)}, u32[]{:S(2)}, u32[]{:S(2)}) async-start(bf16[8,256,128]{2,1,0:T(8,128)(2,1)} %get-tuple-element.21), calls=%async_computation.1 | async-start | bytes 1048576 | tf_op jit(solution)/shard_map/all_to_all | solution.py:218
  39.8 27.0 %collective-permute-start.1 = (bf16[4,128,384]{2,1,0:T(8,128)(2,1)S(1)}, bf16[4,128,384]{2,1,0:T(8,128)(2,1)S(1)}, u32[]{:S(2)}, u32[]{:S(2)}) collective-permute-start(bf16[4,128,384]{2,1,0:T(8,128)(2,1)S(1)} %pad_maximum_fusion), channel_id=1, source_target_pairs={{0,8},{4,12},{8,16},{12,20},{16,24},{20,28},{24,32},{28,36},{32,40... | collective-permute-start | bytes 1179656 | tf_op jit(solution)/shard_map/ppermute | solution.py:228
  43.3 0.7 copy-start.5
  44.2 22.6 %collective-permute-start.2 = (bf16[2,128,384]{2,1,0:T(8,128)(2,1)S(1)}, bf16[2,128,384]{2,1,0:T(8,128)(2,1)S(1)}, u32[]{:S(2)}, u32[]{:S(2)}) collective-permute-start(bf16[2,128,384]{2,1,0:T(8,128)(2,1)S(1)} %get-tuple-element.22.near0), channel_id=1, source_target_pairs={{0,16},{4,20},{8,24},{12,28},{16,32},{20,36},{24,40},{28,44},{32,4... | collective-permute-start | bytes 589832 | tf_op jit(solution)/shard_map/ppermute | solution.py:228
  58.2 8.6 %copy-start = (bf16[384,128]{1,0:T(8,128)(2,1)S(1)}, bf16[384,128]{1,0:T(8,128)(2,1)}, u32[]{:S(2)}) copy-start(bf16[384,128]{1,0:T(8,128)(2,1)} %q.1) | copy-start | bytes 294916
  58.2 8.6 %copy-start.1 = (bf16[384,128]{1,0:T(8,128)(2,1)S(1)}, bf16[384,128]{1,0:T(8,128)(2,1)}, u32[]{:S(2)}) copy-start(bf16[384,128]{1,0:T(8,128)(2,1)} %o.1) | copy-start | bytes 294916
  58.2 8.6 %copy-start.2 = (bf16[384,128]{1,0:T(8,128)(2,1)S(1)}, bf16[384,128]{1,0:T(8,128)(2,1)}, u32[]{:S(2)}) copy-start(bf16[384,128]{1,0:T(8,128)(2,1)} %do.1) | copy-start | bytes 294916
  73.1 4.1 %collective-permute-start.3 = (bf16[2944,128]{1,0:T(8,128)(2,1)S(1)}, bf16[2944,128]{1,0:T(8,128)(2,1)S(1)}, u32[]{:S(2)}, u32[]{:S(2)}) collective-permute-start(bf16[2944,128]{1,0:T(8,128)(2,1)S(1)} %get-tuple-element.26), channel_id=1, source_target_pairs={{0,1},{1,0},{2,3},{3,2},{4,5},{5,4},{6,7},{7,6},{8,9},{9,8},{10,11... | collective-permute-start | bytes 2261000 | tf_op jit(solution)/shard_map/ppermute | solution.py:232
  78.0 12.8 %collective-permute-start.5 = (bf16[256,384]{1,0:T(8,128)(2,1)S(1)}, bf16[256,384]{1,0:T(8,128)(2,1)S(1)}, u32[]{:S(2)}, u32[]{:S(2)}) collective-permute-start(bf16[256,384]{1,0:T(8,128)(2,1)S(1)} %get-tuple-element.31), channel_id=1, source_target_pairs={{8,0},{12,4},{16,8},{20,12},{24,16},{28,20},{32,24},{36,28},{40,32... | collective-permute-start | bytes 589832 | tf_op jit(solution)/shard_map/ppermute | solution.py:228
  79.9 10.9 %collective-permute-start.4 = (bf16[512,128]{1,0:T(8,128)(2,1)S(1)}, bf16[512,128]{1,0:T(8,128)(2,1)S(1)}, u32[]{:S(2)}, u32[]{:S(2)}) collective-permute-start(bf16[512,128]{1,0:T(8,128)(2,1)S(1)} %get-tuple-element.28), channel_id=1, source_target_pairs={{0,2},{2,0},{1,3},{3,1},{4,6},{6,4},{5,7},{7,5},{8,10},{10,8},{9,1... | collective-permute-start | bytes 393224 | tf_op jit(solution)/shard_map/ppermute | solution.py:232
  84.2 6.7 %collective-permute-start.6 = (bf16[128,384]{1,0:T(8,128)(2,1)S(1)}, bf16[128,384]{1,0:T(8,128)(2,1)S(1)}, u32[]{:S(2)}, u32[]{:S(2)}) collective-permute-start(bf16[128,384]{1,0:T(8,128)(2,1)S(1)} %get-tuple-element.32), channel_id=1, source_target_pairs={{16,0},{20,4},{24,8},{28,12},{32,16},{36,20},{40,24},{44,28},{48,3... | collective-permute-start | bytes 294920 | tf_op jit(solution)/shard_map/ppermute | solution.py:228
  92.3 16.4 %all-to-all-start.2 = ((bf16[8,256,128]{2,1,0:T(8,128)(2,1)}), bf16[8,256,128]{2,1,0:T(8,128)(2,1)S(1)}, u32[]{:S(2)}, u32[]{:S(2)}) async-start(bf16[8,256,128]{2,1,0:T(8,128)(2,1)} %bitcast.6), calls=%async_computation.2 | async-start | bytes 1048576 | tf_op jit(solution)/shard_map/all_to_all | solution.py:218
  100.1 8.6 %collective-permute-start.7 = (bf16[128,384]{1,0:T(8,128)(2,1)S(1)}, bf16[128,384]{1,0:T(8,128)(2,1)S(1)}, u32[]{:S(2)}, u32[]{:S(2)}) collective-permute-start(bf16[128,384]{1,0:T(8,128)(2,1)S(1)} %get-tuple-element.35), channel_id=1, source_target_pairs={{4,0},{8,4},{12,8},{16,12},{20,16},{24,20},{28,24},{32,28},{36,32}... | collective-permute-start | bytes 294920 | tf_op jit(solution)/shard_map/ppermute | solution.py:228
  110.0 19.4 %all-to-all-start.3 = ((f32[16,16,128]{2,1,0:T(8,128)}), f32[16,16,128]{2,1,0:T(8,128)S(1)}, u32[]{:S(2)}, u32[]{:S(2)}) async-start(f32[16,16,128]{2,1,0:T(8,128)} %bitcast.9), calls=%async_computation.3 | async-start | bytes 262144 | tf_op jit(solution)/shard_map/all_to_all | solution.py:218
  116.2 7.5 %collective-permute-start.8 = (bf16[64,384]{1,0:T(8,128)(2,1)S(1)}, bf16[64,384]{1,0:T(8,128)(2,1)S(1)}, u32[]{:S(2)}, u32[]{:S(2)}) collective-permute-start(bf16[64,384]{1,0:T(8,128)(2,1)S(1)} %get-tuple-element.37), channel_id=1, source_target_pairs={{0,2},{2,0},{1,3},{3,1},{4,6},{6,4},{5,7},{7,5},{8,10},{10,8},{9,1... | collective-permute-start | bytes 147464 | tf_op jit(solution)/shard_map/ppermute | solution.py:232

commit v6 on v5

--- a/solution.py
+++ b/solution.py
@@ -91,7 +91,7 @@
 
 
 def attention_kernel(
-    place, q, o, do, start, gathered, near0, near1, near23, near4,
+    place, q, o, do, start, gathered, near0, near1, near2, near3, near4,
     dq, kept, kept_near, sent, exps, keys, values, heads, turned,
 ):
     swap = swap_matrix()
@@ -103,10 +103,10 @@
         rows = slice(quarter * QUARTER, (quarter + 1) * QUARTER)
         keys[rows] = part[:, 0].reshape(QUARTER, WIDTH).astype(jnp.bfloat16)
         values[rows] = part[:, 1].reshape(QUARTER, WIDTH).astype(jnp.bfloat16)
-    for distance, (near, at) in enumerate(((near0, 0), (near1, 0), (near23, 0), (near23, 2), (near4, 0))):
+    for distance, near in enumerate((near0, near1, near2, near3, near4)):
         rows = slice(PROMPT + distance * RROWS, PROMPT + (distance + 1) * RROWS)
-        keys[rows] = near[at].T
-        values[rows] = near[at + 1].T
+        keys[rows] = near[0].T
+        values[rows] = near[1].T
     chunks = [(i * QUARTER, QUARTER, None) for i in range(HEADS)]
     chunks += [(PROMPT + d * RROWS, RROWS, d) for d in range(HOPS + 1)]
     queries, dout = q[...], do[...]
@@ -224,7 +224,7 @@
 
 
 def shifted(array, by):
-    pairs = [(i, i + by) for i in range(DP) if 0 <= i + by < DP]
+    pairs = [(i, i + by) for i in range(DP) if i // PIECES == (i + by) // PIECES]
     return lax.ppermute(array, ("xlo", "z", "y"), pairs)
 
 
@@ -248,9 +248,7 @@
         (along_z, own),
     )
     pieces = exchanged(fanned, ("xlo", "y")).reshape(DP, TILE, WIDTH)
-    near1, near4 = shifted(near, 1), shifted(near, HOPS)
-    near23 = shifted(jnp.concatenate([near, near1], axis=0), 2)
-    near = [near, near1, near23, near4]
+    near = [near] + [shifted(near, distance) for distance in range(1, HOPS + 1)]
 
     holder = jnp.arange(DP, dtype=jnp.int32)
     slot = ((holder // (Z * Y)) * Y + holder % Y) * Z + (holder // Y) % Z

time: 131 us -> 124 us (0.947)
  waiting for transfers between devices: 36.8 us -> 26.1 us
  starting transfers between devices: 60.8 us -> 64.8 us
    all_to_all x4, waiting for transfers between devices: 20.1 us -> 9.59 us  [exchanged(): return lax.all_to_all(blocks, axes, split_axis=0, concat_axis=0, tiled=True)]
    ppermute x6 -> x7, starting transfers between devices: 14.7 us -> 20.9 us  [shifted(): return lax.ppermute(array, ('xlo', 'z', 'y'), pairs)]
    all_to_all x4, starting transfers between devices: 35.7 us -> 33.5 us  [exchanged(): return lax.all_to_all(blocks, axes, split_axis=0, concat_axis=0, tiled=True)]
    ppermute x6 -> x7, waiting for transfers between devices: 11.2 us -> 11.1 us  [shifted(): return lax.ppermute(array, ('xlo', 'z', 'y'), pairs)]
  transfers between devices with their start and end apart: 13 -> 14, of which waited for: 7 -> 6; matrix products, arithmetic and copies ran while one was open for 1% -> 1% of each run, Pallas kernels for 0% -> 0%
where the time goes in v6:
time: 124 us; the launch traced here: 123 us
  starting transfers between devices  64.8 us (52%)
  waiting for transfers between devices  26.1 us (21%)
  blocking collectives  15.6 us (13%)
  Pallas kernels  11.2 us (9%)
  local copies, waits for them, and re-layouts  3.4 us (3%)
    all_to_all x4, starting transfers between devices, exchanged(): return lax.all_to_all(blocks, axes, split_axis=0, concat_axis=0, tiled=True)  33.5 us
    ppermute x7, starting transfers between devices, shifted(): return lax.ppermute(array, ('xlo', 'z', 'y'), pairs)  20.9 us
    pallas_call x6, Pallas kernels, local_call(): pl.pallas_call(kernel, out_shape=[jax.ShapeDtypeStruct(shape, dtype) for...  11.2 us
    ppermute x7, waiting for transfers between devices, shifted(): return lax.ppermute(array, ('xlo', 'z', 'y'), pairs)  11.1 us
    ppermute x3, starting transfers between devices, traded(): return lax.ppermute(array, axis, [(0, 1), (1, 0)])  10.4 us
    all_to_all x4, waiting for transfers between devices, exchanged(): return lax.all_to_all(blocks, axes, split_axis=0, concat_axis=0, tiled=True)  9.59 us
    all_gather x1, blocking collectives, body(): gathered = lax.all_gather(picked, ('xhi', 'core'), axis=0, tiled=False)  8.54 us
    all_gather x1, blocking collectives, body(): lax.all_gather(resp_kv.transpose(0, 2, 1), ('xhi', 'core'), axis=1, tiled...  7.11 us
  transfers between devices with their start and end apart: 14, of which 6 were waited for; matrix products, arithmetic and copies ran while one was open for 1% of the time, Pallas kernels for 0%

profile of v6, /device:TPU:24, one launch (start us, length us, event | category | flops | bytes accessed | tf_op | source)
XLA Modules:
  0.0 123.3 jit_solution(5845034700183491147)
XLA Ops:
  0.6 0.8 broadcast_in_dim.71
  1.4 0.6 broadcast_in_dim.72
  2.1 15.2 %all-to-all-start = ((bf16[16,16,128]{2,1,0:T(8,128)(2,1)}), bf16[16,16,128]{2,1,0:T(8,128)(2,1)S(1)}, u32[]{:S(2)}, u32[]{:S(2)}) async-start(bf16[16,16,128]{2,1,0:T(8,128)(2,1)} %broadcast_in_dim.72), calls=%async_computation | async-start | bytes 131072 | tf_op jit(solution)/shard_map/all_to_all | solution.py:218
  17.3 0.0 copy-start.3
  17.3 0.0 copy-start.4
  17.4 0.7 copy-done.4
  18.0 0.1 select_reduce_fusion.3
  18.1 7.1 %all_gather.9.own = bf16[2,128,384]{2,1,0:T(8,128)(2,1)S(1)} all-gather(bf16[2,32,384]{2,1,0:T(8,128)(2,1)S(1)} %bitcast.15), channel_id=1, replica_groups=mesh['xlo'=2,'z'=16,'y'=4,'xhi'=2,'core'=2] {'xhi','core'}, dimensions={1}, use_global_device_ids=true | all-gather | bytes 245760 | tf_op jit(solution)/shard_map/all_gather | solution.py:242
  25.2 0.1 select_reduce_fusion.2
  25.3 0.1 select_reduce_fusion
  25.4 4.6 %all-to-all-done = bf16[16,16,128]{2,1,0:T(8,128)(2,1)S(1)} async-done(((bf16[16,16,128]{2,1,0:T(8,128)(2,1)}), bf16[16,16,128]{2,1,0:T(8,128)(2,1)S(1)}, u32[]{:S(2)}, u32[]{:S(2)}) %all-to-all-start) | async-done | bytes 65568 | tf_op jit(solution)/shard_map/all_to_all | solution.py:218
  30.0 0.9 fan.1
  30.9 5.6 %all-to-all-start.1 = ((bf16[8,256,128]{2,1,0:T(8,128)(2,1)}), bf16[8,256,128]{2,1,0:T(8,128)(2,1)S(1)}, u32[]{:S(2)}, u32[]{:S(2)}) async-start(bf16[8,256,128]{2,1,0:T(8,128)(2,1)} %get-tuple-element.21), calls=%async_computation.1 | async-start | bytes 1048576 | tf_op jit(solution)/shard_map/all_to_all | solution.py:218
  36.5 0.0 copy-start.5
  36.5 0.1 pad_add_fusion.place
  36.6 0.6 copy-done.5
  37.2 0.2 select_reduce_fusion.1.slots
  37.4 2.6 %collective-permute-start.3 = (bf16[2,128,384]{2,1,0:T(8,128)(2,1)S(1)}, bf16[2,128,384]{2,1,0:T(8,128)(2,1)S(1)}, u32[]{:S(2)}, u32[]{:S(2)}) collective-permute-start(bf16[2,128,384]{2,1,0:T(8,128)(2,1)S(1)} %get-tuple-element.22.near0), channel_id=1, source_target_pairs={{0,16},{4,20},{8,24},{12,28},{16,32},{20,36},{24,40},{28,44},{32,4... | collective-permute-start | bytes 589832 | tf_op jit(solution)/shard_map/ppermute | solution.py:228
  40.0 3.2 %collective-permute-start.2 = (bf16[2,128,384]{2,1,0:T(8,128)(2,1)S(1)}, bf16[2,128,384]{2,1,0:T(8,128)(2,1)S(1)}, u32[]{:S(2)}, u32[]{:S(2)}) collective-permute-start(bf16[2,128,384]{2,1,0:T(8,128)(2,1)S(1)} %get-tuple-element.22.near0), channel_id=1, source_target_pairs={{0,12},{4,16},{8,20},{12,24},{16,28},{20,32},{24,36},{28,40},{32,4... | collective-permute-start | bytes 589832 | tf_op jit(solution)/shard_map/ppermute | solution.py:228
  43.2 2.6 %collective-permute-start.1 = (bf16[2,128,384]{2,1,0:T(8,128)(2,1)S(1)}, bf16[2,128,384]{2,1,0:T(8,128)(2,1)S(1)}, u32[]{:S(2)}, u32[]{:S(2)}) collective-permute-start(bf16[2,128,384]{2,1,0:T(8,128)(2,1)S(1)} %get-tuple-element.22.near0), channel_id=1, source_target_pairs={{0,8},{4,12},{8,16},{12,20},{16,24},{20,28},{24,32},{28,36},{32,40... | collective-permute-start | bytes 589832 | tf_op jit(solution)/shard_map/ppermute | solution.py:228
  45.8 4.5 %collective-permute-start = (bf16[2,128,384]{2,1,0:T(8,128)(2,1)S(1)}, bf16[2,128,384]{2,1,0:T(8,128)(2,1)S(1)}, u32[]{:S(2)}, u32[]{:S(2)}) collective-permute-start(bf16[2,128,384]{2,1,0:T(8,128)(2,1)S(1)} %get-tuple-element.22.near0), channel_id=1, source_target_pairs={{0,4},{4,8},{8,12},{12,16},{16,20},{20,24},{24,28},{28,32},{32,36}... | collective-permute-start | bytes 589832 | tf_op jit(solution)/shard_map/ppermute | solution.py:228
  50.4 0.6 select.33
  51.0 0.0 copy-start
  51.0 0.0 copy-start.1
  51.0 0.0 copy-start.2
  51.0 8.5 %all-gather = bf16[2048,128]{1,0:T(8,128)(2,1)S(1)} all-gather(bf16[512,128]{1,0:T(8,128)(2,1)S(1)} %select.33), channel_id=2, replica_groups=mesh['xlo'=2,'z'=16,'y'=4,'xhi'=2,'core'=2] {'xhi','core'}, dimensions={0}, use_global_device_ids=true | all-gather | bytes 655360 | tf_op jit(solution)/shard_map/all_gather | solution.py:259
  59.5 0.0 collective-permute-done.3.near4
  59.5 0.0 collective-permute-done.2.near3
  59.5 0.0 collective-permute-done.1.near2
  59.6 6.3 %attention.1 = (bf16[384,128]{1,0:T(8,128)(2,1)}, bf16[2,512,128]{2,1,0:T(8,128)(2,1)S(1)}, f32[5,128,384]{2,1,0:T(8,128)S(1)}, bf16[2944,128]{1,0:T(8,128)(2,1)S(1)}) custom-call(s32[2]{0:T(128)S(1)} %pad_add_fusion.place, bf16[384,128]{1,0:T(8,128)(2,1)S(1)} %copy-done, bf16[384,128]{1,0:T(8,128)(2,1)S(1)} %copy-done.1, bf16[384,128]{1,0:T(8,128)(2,1)S(1)} %copy-done.2, ...), custom_call_target="tpu_custom_call" | custom-call | flops 1736441856 | bytes 6000000 | tf_op jit(solution)/shard_map/attention/pallas_call | solution.py:179
  65.9 2.2 %collective-permute-start.4 = (bf16[2944,128]{1,0:T(8,128)(2,1)S(1)}, bf16[2944,128]{1,0:T(8,128)(2,1)S(1)}, u32[]{:S(2)}, u32[]{:S(2)}) collective-permute-start(bf16[2944,128]{1,0:T(8,128)(2,1)S(1)} %get-tuple-element.26), channel_id=1, source_target_pairs={{0,1},{1,0},{2,3},{3,2},{4,5},{5,4},{6,7},{7,6},{8,9},{9,8},{10,11... | collective-permute-start | bytes 2261000 | tf_op jit(solution)/shard_map/ppermute | solution.py:232
  68.2 1.9 %collective-permute-done.4.landed = bf16[2944,128]{1,0:T(8,128)(2,1)S(1)} collective-permute-done((bf16[2944,128]{1,0:T(8,128)(2,1)S(1)}, bf16[2944,128]{1,0:T(8,128)(2,1)S(1)}, u32[]{:S(2)}, u32[]{:S(2)}) %collective-permute-start.4) | collective-permute-done | bytes 753696 | tf_op jit(solution)/shard_map/ppermute | solution.py:232
  70.0 0.7 pair.1
  70.8 3.9 %collective-permute-start.6 = (bf16[256,384]{1,0:T(8,128)(2,1)S(1)}, bf16[256,384]{1,0:T(8,128)(2,1)S(1)}, u32[]{:S(2)}, u32[]{:S(2)}) collective-permute-start(bf16[256,384]{1,0:T(8,128)(2,1)S(1)} %get-tuple-element.31), channel_id=1, source_target_pairs={{8,0},{12,4},{16,8},{20,12},{24,16},{28,20},{32,24},{36,28},{40,32... | collective-permute-start | bytes 589832 | tf_op jit(solution)/shard_map/ppermute | solution.py:228
  74.7 4.2 %collective-permute-start.5 = (bf16[512,128]{1,0:T(8,128)(2,1)S(1)}, bf16[512,128]{1,0:T(8,128)(2,1)S(1)}, u32[]{:S(2)}, u32[]{:S(2)}) collective-permute-start(bf16[512,128]{1,0:T(8,128)(2,1)S(1)} %get-tuple-element.28), channel_id=1, source_target_pairs={{0,2},{2,0},{1,3},{3,1},{4,6},{6,4},{5,7},{7,5},{8,10},{10,8},{9,1... | collective-permute-start | bytes 393224 | tf_op jit(solution)/shard_map/ppermute | solution.py:232
  79.0 1.3 %collective-permute-start.7 = (bf16[128,384]{1,0:T(8,128)(2,1)S(1)}, bf16[128,384]{1,0:T(8,128)(2,1)S(1)}, u32[]{:S(2)}, u32[]{:S(2)}) collective-permute-start(bf16[128,384]{1,0:T(8,128)(2,1)S(1)} %get-tuple-element.32), channel_id=1, source_target_pairs={{16,0},{20,4},{24,8},{28,12},{32,16},{36,20},{40,24},{44,28},{48,3... | collective-permute-start | bytes 294920 | tf_op jit(solution)/shard_map/ppermute | solution.py:228
  80.3 5.2 %collective-permute-done.7.far4 = bf16[128,384]{1,0:T(8,128)(2,1)S(1)} collective-permute-done((bf16[128,384]{1,0:T(8,128)(2,1)S(1)}, bf16[128,384]{1,0:T(8,128)(2,1)S(1)}, u32[]{:S(2)}, u32[]{:S(2)}) %collective-permute-start.7) | collective-permute-done | bytes 98336 | tf_op jit(solution)/shard_map/ppermute | solution.py:228
  85.5 1.4 %place.1 = (bf16[128,16,128]{2,1,0:T(8,128)(2,1)}, f32[128,384]{1,0:T(8,128)S(1)}, bf16[128,384]{1,0:T(8,128)(2,1)S(1)}) custom-call(s32[32]{0:T(128)S(1)} %select_reduce_fusion.1.slots, f32[512,128]{1,0:T(8,128)S(1)} %get-tuple-element.27.mine, bf16[512,128]{1,0:T(8,128)(2,1)S(1)} %collective-permute-done.5.theirs, f32[128,384]{1,0:T(8,128)S(1)} %get-tuple-element.29.own, ...), custom_call_target="tpu_custom_call" | custom-call | tf_op jit(solution)/shard_map/place/pallas_call | solution.py:179
  86.9 4.8 %all-to-all-start.2 = ((bf16[8,256,128]{2,1,0:T(8,128)(2,1)}), bf16[8,256,128]{2,1,0:T(8,128)(2,1)S(1)}, u32[]{:S(2)}, u32[]{:S(2)}) async-start(bf16[8,256,128]{2,1,0:T(8,128)(2,1)} %bitcast.6), calls=%async_computation.2 | async-start | bytes 1048576 | tf_op jit(solution)/shard_map/all_to_all | solution.py:218
  91.7 2.8 %collective-permute-start.8 = (bf16[128,384]{1,0:T(8,128)(2,1)S(1)}, bf16[128,384]{1,0:T(8,128)(2,1)S(1)}, u32[]{:S(2)}, u32[]{:S(2)}) collective-permute-start(bf16[128,384]{1,0:T(8,128)(2,1)S(1)} %get-tuple-element.35), channel_id=1, source_target_pairs={{4,0},{8,4},{12,8},{16,12},{20,16},{24,20},{28,24},{32,28},{36,32}... | collective-permute-start | bytes 294920 | tf_op jit(solution)/shard_map/ppermute | solution.py:228
  94.5 5.8 %collective-permute-done.8.passed = bf16[128,384]{1,0:T(8,128)(2,1)S(1)} collective-permute-done((bf16[128,384]{1,0:T(8,128)(2,1)S(1)}, bf16[128,384]{1,0:T(8,128)(2,1)S(1)}, u32[]{:S(2)}, u32[]{:S(2)}) %collective-permute-start.8) | collective-permute-done | bytes 98336 | tf_op jit(solution)/shard_map/ppermute | solution.py:228
  100.3 1.3 %column.1 = (f32[256,128]{1,0:T(8,128)}, f32[64,384]{1,0:T(8,128)S(1)}, bf16[64,384]{1,0:T(8,128)(2,1)S(1)}) custom-call(s32[2]{0:T(128)S(1)} %pad_add_fusion.place, bf16[8,256,128]{2,1,0:T(8,128)(2,1)S(1)} %all-to-all-done.2.landed, f32[128,384]{1,0:T(8,128)S(1)} %get-tuple-element.34.partial, bf16[128,384]{1,0:T(8,128)(2,1)S(1)} %collective-permute-done.8.passed), custom_call_target="tpu_custom_call" | custom-call | tf_op jit(solution)/shard_map/column/pallas_call | solution.py:179
  101.6 7.9 %all-to-all-start.3 = ((f32[16,16,128]{2,1,0:T(8,128)}), f32[16,16,128]{2,1,0:T(8,128)S(1)}, u32[]{:S(2)}, u32[]{:S(2)}) async-start(f32[16,16,128]{2,1,0:T(8,128)} %bitcast.9), calls=%async_computation.3 | async-start | bytes 262144 | tf_op jit(solution)/shard_map/all_to_all | solution.py:218
  109.5 3.9 %collective-permute-start.9 = (bf16[64,384]{1,0:T(8,128)(2,1)S(1)}, bf16[64,384]{1,0:T(8,128)(2,1)S(1)}, u32[]{:S(2)}, u32[]{:S(2)}) collective-permute-start(bf16[64,384]{1,0:T(8,128)(2,1)S(1)} %get-tuple-element.37), channel_id=1, source_target_pairs={{0,2},{2,0},{1,3},{3,1},{4,6},{6,4},{5,7},{7,5},{8,10},{10,8},{9,1... | collective-permute-start | bytes 147464 | tf_op jit(solution)/shard_map/ppermute | solution.py:232
  113.4 3.6 %collective-permute-done.9 = bf16[64,384]{1,0:T(8,128)(2,1)S(1)} collective-permute-done((bf16[64,384]{1,0:T(8,128)(2,1)S(1)}, bf16[64,384]{1,0:T(8,128)(2,1)S(1)}, u32[]{:S(2)}, u32[]{:S(2)}) %collective-permute-start.9) | collective-permute-done | bytes 49184 | tf_op jit(solution)/shard_map/ppermute | solution.py:232
  116.9 0.6 add_convert_fusion
  117.6 5.0 %all-to-all-done.3 = f32[16,16,128]{2,1,0:T(8,128)S(1)} async-done(((f32[16,16,128]{2,1,0:T(8,128)}), f32[16,16,128]{2,1,0:T(8,128)S(1)}, u32[]{:S(2)}, u32[]{:S(2)}) %all-to-all-start.3) | async-done | bytes 131104 | tf_op jit(solution)/shard_map/all_to_all | solution.py:218
  122.6 0.7 convert_element_type.16
  (16 shorter events, 0.1 us)
Async XLA Ops:
  2.1 27.9 %all-to-all-start = ((bf16[16,16,128]{2,1,0:T(8,128)(2,1)}), bf16[16,16,128]{2,1,0:T(8,128)(2,1)S(1)}, u32[]{:S(2)}, u32[]{:S(2)}) async-start(bf16[16,16,128]{2,1,0:T(8,128)(2,1)} %broadcast_in_dim.72), calls=%async_computation | async-start | bytes 131072 | tf_op jit(solution)/shard_map/all_to_all | solution.py:218
  17.3 0.8 copy-start.3
  17.3 0.7 copy-start.4
  30.9 19.5 %all-to-all-start.1 = ((bf16[8,256,128]{2,1,0:T(8,128)(2,1)}), bf16[8,256,128]{2,1,0:T(8,128)(2,1)S(1)}, u32[]{:S(2)}, u32[]{:S(2)}) async-start(bf16[8,256,128]{2,1,0:T(8,128)(2,1)} %get-tuple-element.21), calls=%async_computation.1 | async-start | bytes 1048576 | tf_op jit(solution)/shard_map/all_to_all | solution.py:218
  36.5 0.7 copy-start.5
  37.4 22.2 %collective-permute-start.3 = (bf16[2,128,384]{2,1,0:T(8,128)(2,1)S(1)}, bf16[2,128,384]{2,1,0:T(8,128)(2,1)S(1)}, u32[]{:S(2)}, u32[]{:S(2)}) collective-permute-start(bf16[2,128,384]{2,1,0:T(8,128)(2,1)S(1)} %get-tuple-element.22.near0), channel_id=1, source_target_pairs={{0,16},{4,20},{8,24},{12,28},{16,32},{20,36},{24,40},{28,44},{32,4... | collective-permute-start | bytes 589832 | tf_op jit(solution)/shard_map/ppermute | solution.py:228
  40.0 19.5 %collective-permute-start.2 = (bf16[2,128,384]{2,1,0:T(8,128)(2,1)S(1)}, bf16[2,128,384]{2,1,0:T(8,128)(2,1)S(1)}, u32[]{:S(2)}, u32[]{:S(2)}) collective-permute-start(bf16[2,128,384]{2,1,0:T(8,128)(2,1)S(1)} %get-tuple-element.22.near0), channel_id=1, source_target_pairs={{0,12},{4,16},{8,20},{12,24},{16,28},{20,32},{24,36},{28,40},{32,4... | collective-permute-start | bytes 589832 | tf_op jit(solution)/shard_map/ppermute | solution.py:228
  43.2 16.3 %collective-permute-start.1 = (bf16[2,128,384]{2,1,0:T(8,128)(2,1)S(1)}, bf16[2,128,384]{2,1,0:T(8,128)(2,1)S(1)}, u32[]{:S(2)}, u32[]{:S(2)}) collective-permute-start(bf16[2,128,384]{2,1,0:T(8,128)(2,1)S(1)} %get-tuple-element.22.near0), channel_id=1, source_target_pairs={{0,8},{4,12},{8,16},{12,20},{16,24},{20,28},{24,32},{28,36},{32,40... | collective-permute-start | bytes 589832 | tf_op jit(solution)/shard_map/ppermute | solution.py:228
  45.8 13.7 %collective-permute-start = (bf16[2,128,384]{2,1,0:T(8,128)(2,1)S(1)}, bf16[2,128,384]{2,1,0:T(8,128)(2,1)S(1)}, u32[]{:S(2)}, u32[]{:S(2)}) collective-permute-start(bf16[2,128,384]{2,1,0:T(8,128)(2,1)S(1)} %get-tuple-element.22.near0), channel_id=1, source_target_pairs={{0,4},{4,8},{8,12},{12,16},{16,20},{20,24},{24,28},{28,32},{32,36}... | collective-permute-start | bytes 589832 | tf_op jit(solution)/shard_map/ppermute | solution.py:228
  51.0 8.6 %copy-start = (bf16[384,128]{1,0:T(8,128)(2,1)S(1)}, bf16[384,128]{1,0:T(8,128)(2,1)}, u32[]{:S(2)}) copy-start(bf16[384,128]{1,0:T(8,128)(2,1)} %q.1) | copy-start | bytes 294916
  51.0 8.6 %copy-start.1 = (bf16[384,128]{1,0:T(8,128)(2,1)S(1)}, bf16[384,128]{1,0:T(8,128)(2,1)}, u32[]{:S(2)}) copy-start(bf16[384,128]{1,0:T(8,128)(2,1)} %o.1) | copy-start | bytes 294916
  51.0 8.6 %copy-start.2 = (bf16[384,128]{1,0:T(8,128)(2,1)S(1)}, bf16[384,128]{1,0:T(8,128)(2,1)}, u32[]{:S(2)}) copy-start(bf16[384,128]{1,0:T(8,128)(2,1)} %do.1) | copy-start | bytes 294916
  65.9 4.1 %collective-permute-start.4 = (bf16[2944,128]{1,0:T(8,128)(2,1)S(1)}, bf16[2944,128]{1,0:T(8,128)(2,1)S(1)}, u32[]{:S(2)}, u32[]{:S(2)}) collective-permute-start(bf16[2944,128]{1,0:T(8,128)(2,1)S(1)} %get-tuple-element.26), channel_id=1, source_target_pairs={{0,1},{1,0},{2,3},{3,2},{4,5},{5,4},{6,7},{7,6},{8,9},{9,8},{10,11... | collective-permute-start | bytes 2261000 | tf_op jit(solution)/shard_map/ppermute | solution.py:232
  70.8 14.7 %collective-permute-start.6 = (bf16[256,384]{1,0:T(8,128)(2,1)S(1)}, bf16[256,384]{1,0:T(8,128)(2,1)S(1)}, u32[]{:S(2)}, u32[]{:S(2)}) collective-permute-start(bf16[256,384]{1,0:T(8,128)(2,1)S(1)} %get-tuple-element.31), channel_id=1, source_target_pairs={{8,0},{12,4},{16,8},{20,12},{24,16},{28,20},{32,24},{36,28},{40,32... | collective-permute-start | bytes 589832 | tf_op jit(solution)/shard_map/ppermute | solution.py:228
  74.7 10.8 %collective-permute-start.5 = (bf16[512,128]{1,0:T(8,128)(2,1)S(1)}, bf16[512,128]{1,0:T(8,128)(2,1)S(1)}, u32[]{:S(2)}, u32[]{:S(2)}) collective-permute-start(bf16[512,128]{1,0:T(8,128)(2,1)S(1)} %get-tuple-element.28), channel_id=1, source_target_pairs={{0,2},{2,0},{1,3},{3,1},{4,6},{6,4},{5,7},{7,5},{8,10},{10,8},{9,1... | collective-permute-start | bytes 393224 | tf_op jit(solution)/shard_map/ppermute | solution.py:232
  79.0 6.5 %collective-permute-start.7 = (bf16[128,384]{1,0:T(8,128)(2,1)S(1)}, bf16[128,384]{1,0:T(8,128)(2,1)S(1)}, u32[]{:S(2)}, u32[]{:S(2)}) collective-permute-start(bf16[128,384]{1,0:T(8,128)(2,1)S(1)} %get-tuple-element.32), channel_id=1, source_target_pairs={{16,0},{20,4},{24,8},{28,12},{32,16},{36,20},{40,24},{44,28},{48,3... | collective-permute-start | bytes 294920 | tf_op jit(solution)/shard_map/ppermute | solution.py:228
  86.9 13.4 %all-to-all-start.2 = ((bf16[8,256,128]{2,1,0:T(8,128)(2,1)}), bf16[8,256,128]{2,1,0:T(8,128)(2,1)S(1)}, u32[]{:S(2)}, u32[]{:S(2)}) async-start(bf16[8,256,128]{2,1,0:T(8,128)(2,1)} %bitcast.6), calls=%async_computation.2 | async-start | bytes 1048576 | tf_op jit(solution)/shard_map/all_to_all | solution.py:218
  91.7 8.6 %collective-permute-start.8 = (bf16[128,384]{1,0:T(8,128)(2,1)S(1)}, bf16[128,384]{1,0:T(8,128)(2,1)S(1)}, u32[]{:S(2)}, u32[]{:S(2)}) collective-permute-start(bf16[128,384]{1,0:T(8,128)(2,1)S(1)} %get-tuple-element.35), channel_id=1, source_target_pairs={{4,0},{8,4},{12,8},{16,12},{20,16},{24,20},{28,24},{32,28},{36,32}... | collective-permute-start | bytes 294920 | tf_op jit(solution)/shard_map/ppermute | solution.py:228
  101.6 21.0 %all-to-all-start.3 = ((f32[16,16,128]{2,1,0:T(8,128)}), f32[16,16,128]{2,1,0:T(8,128)S(1)}, u32[]{:S(2)}, u32[]{:S(2)}) async-start(f32[16,16,128]{2,1,0:T(8,128)} %bitcast.9), calls=%async_computation.3 | async-start | bytes 262144 | tf_op jit(solution)/shard_map/all_to_all | solution.py:218
  109.5 7.5 %collective-permute-start.9 = (bf16[64,384]{1,0:T(8,128)(2,1)S(1)}, bf16[64,384]{1,0:T(8,128)(2,1)S(1)}, u32[]{:S(2)}, u32[]{:S(2)}) collective-permute-start(bf16[64,384]{1,0:T(8,128)(2,1)S(1)} %get-tuple-element.37), channel_id=1, source_target_pairs={{0,2},{2,0},{1,3},{3,1},{4,6},{6,4},{5,7},{7,5},{8,10},{10,8},{9,1... | collective-permute-start | bytes 147464 | tf_op jit(solution)/shard_map/ppermute | solution.py:232

commit v7 on v6

--- a/solution.py
+++ b/solution.py
@@ -63,12 +63,12 @@
             out[at : at + WIDTH, lanes] = (kept_near[distance, :, lanes] + theirs.astype(jnp.float32)).astype(out.dtype)
 
 
-def place_kernel(slots, mine, theirs, own, far1, far23, far4, spread, partial, passed):
+def place_kernel(slots, mine, theirs, own, far1, far23, spread, partial, passed):
     spread[...] = jnp.zeros_like(spread)
     total = (mine[...] + theirs[...].astype(jnp.float32)).astype(jnp.bfloat16)
     for piece in range(PIECES):
         spread[slots[piece]] = total[piece * TILE : (piece + 1) * TILE]
-    partial[...] = own[...] + far23[:WIDTH].astype(jnp.float32) + far4[...].astype(jnp.float32)
+    partial[...] = own[...] + far23[:WIDTH].astype(jnp.float32)
     passed[...] = (far1[...].astype(jnp.float32) + far23[WIDTH:].astype(jnp.float32)).astype(passed.dtype)
 
 
@@ -76,12 +76,12 @@
     return XHI * PIECES * TILE + (distance * (RROWS // WIDTH) + column) * WIDTH
 
 
-def column_kernel(place, landed, partial, passed, column, mine, other, cut):
+def column_kernel(place, landed, partial, passed, far4, column, mine, other, cut):
     held = landed[0].astype(jnp.float32)
     for sender in range(1, COLUMNS):
         held = held + landed[sender].astype(jnp.float32)
     column[...] = held
-    total = partial[...] + passed[...].astype(jnp.float32)
+    total = partial[...] + passed[...].astype(jnp.float32) + far4[...].astype(jnp.float32)
     for xhi in range(XHI):
         for kind in range(2):
             begin = (kind * XHI + xhi) * PART
@@ -286,14 +286,14 @@
         place_kernel,
         "place",
         [((DP, TILE, WIDTH), half), (wide, jnp.float32), (wide, half)],
-        (slots, mine, theirs, own_terms, far1, shifted(far23, -2), shifted(far4, -HOPS)),
+        (slots, mine, theirs, own_terms, far1, shifted(far23, -2)),
     )
     by_column = exchanged(spread.reshape(COLUMNS, Z * TILE, WIDTH), ("xlo", "y"))
     column_sum, mine, other = local_call(
         column_kernel,
         "column",
         [((Z * TILE, WIDTH), jnp.float32), (narrow, jnp.float32), (narrow, half)],
-        (place, by_column, partial, shifted(passed, -1)),
+        (place, by_column, partial, shifted(passed, -1), shifted(far4, -HOPS)),
         [pltpu.VMEM((XHI,) + narrow, jnp.float32)],
     )
     by_z = exchanged(column_sum.reshape(Z, TILE, WIDTH), "z")

time: 124 us -> 124 us (level)
  starting transfers between devices: 64.8 us -> 66.4 us
  waiting for transfers between devices: 26.1 us -> 24.8 us
    ppermute x7, waiting for transfers between devices: 11.1 us -> 5.86 us  [shifted(): return lax.ppermute(array, ('xlo', 'z', 'y'), pairs)]
    ppermute x3, waiting for transfers between devices: 5.43 us -> 9.34 us  [traded(): return lax.ppermute(array, axis, [(0, 1), (1, 0)])]
  transfers between devices with their start and end apart: 14 -> 14, of which waited for: 6 -> 7; matrix products, arithmetic and copies ran while one was open for 1% -> 1% of each run, Pallas kernels for 0% -> 0%
where the time goes in v7:
time: 124 us
  starting transfers between devices  66.4 us (54%)
  waiting for transfers between devices  24.8 us (20%)
  blocking collectives  15.6 us (13%)
  Pallas kernels  11.2 us (9%)
  local copies, waits for them, and re-layouts  3.4 us (3%)
    all_to_all x4, starting transfers between devices, exchanged(): return lax.all_to_all(blocks, axes, split_axis=0, concat_axis=0, tiled=True)  34.3 us
    ppermute x7, starting transfers between devices, shifted(): return lax.ppermute(array, ('xlo', 'z', 'y'), pairs)  20.9 us
    pallas_call x6, Pallas kernels, local_call(): pl.pallas_call(kernel, out_shape=[jax.ShapeDtypeStruct(shape, dtype) for...  11.2 us
    ppermute x3, starting transfers between devices, traded(): return lax.ppermute(array, axis, [(0, 1), (1, 0)])  11.1 us
    all_to_all x4, waiting for transfers between devices, exchanged(): return lax.all_to_all(blocks, axes, split_axis=0, concat_axis=0, tiled=True)  9.58 us
    ppermute x3, waiting for transfers between devices, traded(): return lax.ppermute(array, axis, [(0, 1), (1, 0)])  9.34 us
    all_gather x1, blocking collectives, body(): gathered = lax.all_gather(picked, ('xhi', 'core'), axis=0, tiled=False)  8.54 us
    all_gather x1, blocking collectives, body(): lax.all_gather(resp_kv.transpose(0, 2, 1), ('xhi', 'core'), axis=1, tiled...  7.11 us
  transfers between devices with their start and end apart: 14, of which 7 were waited for; matrix products, arithmetic and copies ran while one was open for 1% of the time, Pallas kernels for 0%

profile of v7, /device:TPU:24, one launch (start us, length us, event | category | flops | bytes accessed | tf_op | source)
XLA Modules:
  0.0 123.5 jit_solution(13769382296192982446)
XLA Ops:
  0.6 0.8 broadcast_in_dim.71
  1.4 0.6 broadcast_in_dim.72
  2.1 15.2 %all-to-all-start = ((bf16[16,16,128]{2,1,0:T(8,128)(2,1)}), bf16[16,16,128]{2,1,0:T(8,128)(2,1)S(1)}, u32[]{:S(2)}, u32[]{:S(2)}) async-start(bf16[16,16,128]{2,1,0:T(8,128)(2,1)} %broadcast_in_dim.72), calls=%async_computation | async-start | bytes 131072 | tf_op jit(solution)/shard_map/all_to_all | solution.py:218
  17.3 0.0 copy-start.3
  17.3 0.0 copy-start.4
  17.4 0.7 copy-done.4
  18.0 0.1 select_reduce_fusion.3
  18.1 7.1 %all_gather.9.own = bf16[2,128,384]{2,1,0:T(8,128)(2,1)S(1)} all-gather(bf16[2,32,384]{2,1,0:T(8,128)(2,1)S(1)} %bitcast.15), channel_id=1, replica_groups=mesh['xlo'=2,'z'=16,'y'=4,'xhi'=2,'core'=2] {'xhi','core'}, dimensions={1}, use_global_device_ids=true | all-gather | bytes 245760 | tf_op jit(solution)/shard_map/all_gather | solution.py:242
  25.2 0.1 select_reduce_fusion.2
  25.3 0.1 select_reduce_fusion
  25.4 4.6 %all-to-all-done = bf16[16,16,128]{2,1,0:T(8,128)(2,1)S(1)} async-done(((bf16[16,16,128]{2,1,0:T(8,128)(2,1)}), bf16[16,16,128]{2,1,0:T(8,128)(2,1)S(1)}, u32[]{:S(2)}, u32[]{:S(2)}) %all-to-all-start) | async-done | bytes 65568 | tf_op jit(solution)/shard_map/all_to_all | solution.py:218
  30.0 0.9 fan.1
  30.9 5.6 %all-to-all-start.1 = ((bf16[8,256,128]{2,1,0:T(8,128)(2,1)}), bf16[8,256,128]{2,1,0:T(8,128)(2,1)S(1)}, u32[]{:S(2)}, u32[]{:S(2)}) async-start(bf16[8,256,128]{2,1,0:T(8,128)(2,1)} %get-tuple-element.21), calls=%async_computation.1 | async-start | bytes 1048576 | tf_op jit(solution)/shard_map/all_to_all | solution.py:218
  36.5 0.0 copy-start.5
  36.5 0.1 pad_add_fusion.place
  36.6 0.6 copy-done.5
  37.2 0.2 select_reduce_fusion.1.slots
  37.4 2.6 %collective-permute-start.3 = (bf16[2,128,384]{2,1,0:T(8,128)(2,1)S(1)}, bf16[2,128,384]{2,1,0:T(8,128)(2,1)S(1)}, u32[]{:S(2)}, u32[]{:S(2)}) collective-permute-start(bf16[2,128,384]{2,1,0:T(8,128)(2,1)S(1)} %get-tuple-element.22.near0), channel_id=1, source_target_pairs={{0,16},{4,20},{8,24},{12,28},{16,32},{20,36},{24,40},{28,44},{32,4... | collective-permute-start | bytes 589832 | tf_op jit(solution)/shard_map/ppermute | solution.py:228
  40.0 3.2 %collective-permute-start.2 = (bf16[2,128,384]{2,1,0:T(8,128)(2,1)S(1)}, bf16[2,128,384]{2,1,0:T(8,128)(2,1)S(1)}, u32[]{:S(2)}, u32[]{:S(2)}) collective-permute-start(bf16[2,128,384]{2,1,0:T(8,128)(2,1)S(1)} %get-tuple-element.22.near0), channel_id=1, source_target_pairs={{0,12},{4,16},{8,20},{12,24},{16,28},{20,32},{24,36},{28,40},{32,4... | collective-permute-start | bytes 589832 | tf_op jit(solution)/shard_map/ppermute | solution.py:228
  43.2 2.6 %collective-permute-start.1 = (bf16[2,128,384]{2,1,0:T(8,128)(2,1)S(1)}, bf16[2,128,384]{2,1,0:T(8,128)(2,1)S(1)}, u32[]{:S(2)}, u32[]{:S(2)}) collective-permute-start(bf16[2,128,384]{2,1,0:T(8,128)(2,1)S(1)} %get-tuple-element.22.near0), channel_id=1, source_target_pairs={{0,8},{4,12},{8,16},{12,20},{16,24},{20,28},{24,32},{28,36},{32,40... | collective-permute-start | bytes 589832 | tf_op jit(solution)/shard_map/ppermute | solution.py:228
  45.8 4.5 %collective-permute-start = (bf16[2,128,384]{2,1,0:T(8,128)(2,1)S(1)}, bf16[2,128,384]{2,1,0:T(8,128)(2,1)S(1)}, u32[]{:S(2)}, u32[]{:S(2)}) collective-permute-start(bf16[2,128,384]{2,1,0:T(8,128)(2,1)S(1)} %get-tuple-element.22.near0), channel_id=1, source_target_pairs={{0,4},{4,8},{8,12},{12,16},{16,20},{20,24},{24,28},{28,32},{32,36}... | collective-permute-start | bytes 589832 | tf_op jit(solution)/shard_map/ppermute | solution.py:228
  50.4 0.0 all-to-all-done.1
  50.4 0.6 select.33
  51.0 0.0 copy-start
  51.0 0.0 copy-start.1
  51.0 0.0 copy-start.2
  51.0 8.5 %all-gather = bf16[2048,128]{1,0:T(8,128)(2,1)S(1)} all-gather(bf16[512,128]{1,0:T(8,128)(2,1)S(1)} %select.33), channel_id=2, replica_groups=mesh['xlo'=2,'z'=16,'y'=4,'xhi'=2,'core'=2] {'xhi','core'}, dimensions={0}, use_global_device_ids=true | all-gather | bytes 655360 | tf_op jit(solution)/shard_map/all_gather | solution.py:259
  59.5 0.0 collective-permute-done.near1
  59.6 6.3 %attention.1 = (bf16[384,128]{1,0:T(8,128)(2,1)}, bf16[2,512,128]{2,1,0:T(8,128)(2,1)S(1)}, f32[5,128,384]{2,1,0:T(8,128)S(1)}, bf16[2944,128]{1,0:T(8,128)(2,1)S(1)}) custom-call(s32[2]{0:T(128)S(1)} %pad_add_fusion.place, bf16[384,128]{1,0:T(8,128)(2,1)S(1)} %copy-done, bf16[384,128]{1,0:T(8,128)(2,1)S(1)} %copy-done.1, bf16[384,128]{1,0:T(8,128)(2,1)S(1)} %copy-done.2, ...), custom_call_target="tpu_custom_call" | custom-call | flops 1736441856 | bytes 6000000 | tf_op jit(solution)/shard_map/attention/pallas_call | solution.py:179
  65.9 2.2 %collective-permute-start.4 = (bf16[2944,128]{1,0:T(8,128)(2,1)S(1)}, bf16[2944,128]{1,0:T(8,128)(2,1)S(1)}, u32[]{:S(2)}, u32[]{:S(2)}) collective-permute-start(bf16[2944,128]{1,0:T(8,128)(2,1)S(1)} %get-tuple-element.26), channel_id=1, source_target_pairs={{0,1},{1,0},{2,3},{3,2},{4,5},{5,4},{6,7},{7,6},{8,9},{9,8},{10,11... | collective-permute-start | bytes 2261000 | tf_op jit(solution)/shard_map/ppermute | solution.py:232
  68.2 1.9 %collective-permute-done.4.landed = bf16[2944,128]{1,0:T(8,128)(2,1)S(1)} collective-permute-done((bf16[2944,128]{1,0:T(8,128)(2,1)S(1)}, bf16[2944,128]{1,0:T(8,128)(2,1)S(1)}, u32[]{:S(2)}, u32[]{:S(2)}) %collective-permute-start.4) | collective-permute-done | bytes 753696 | tf_op jit(solution)/shard_map/ppermute | solution.py:232
  70.0 0.7 pair.1
  70.8 3.9 %collective-permute-start.6 = (bf16[256,384]{1,0:T(8,128)(2,1)S(1)}, bf16[256,384]{1,0:T(8,128)(2,1)S(1)}, u32[]{:S(2)}, u32[]{:S(2)}) collective-permute-start(bf16[256,384]{1,0:T(8,128)(2,1)S(1)} %get-tuple-element.31), channel_id=1, source_target_pairs={{8,0},{12,4},{16,8},{20,12},{24,16},{28,20},{32,24},{36,28},{40,32... | collective-permute-start | bytes 589832 | tf_op jit(solution)/shard_map/ppermute | solution.py:228
  74.7 4.2 %collective-permute-start.5 = (bf16[512,128]{1,0:T(8,128)(2,1)S(1)}, bf16[512,128]{1,0:T(8,128)(2,1)S(1)}, u32[]{:S(2)}, u32[]{:S(2)}) collective-permute-start(bf16[512,128]{1,0:T(8,128)(2,1)S(1)} %get-tuple-element.28), channel_id=1, source_target_pairs={{0,2},{2,0},{1,3},{3,1},{4,6},{6,4},{5,7},{7,5},{8,10},{10,8},{9,1... | collective-permute-start | bytes 393224 | tf_op jit(solution)/shard_map/ppermute | solution.py:232
  78.9 4.6 %collective-permute-done.5.theirs = bf16[512,128]{1,0:T(8,128)(2,1)S(1)} collective-permute-done((bf16[512,128]{1,0:T(8,128)(2,1)S(1)}, bf16[512,128]{1,0:T(8,128)(2,1)S(1)}, u32[]{:S(2)}, u32[]{:S(2)}) %collective-permute-start.5) | collective-permute-done | bytes 131104 | tf_op jit(solution)/shard_map/ppermute | solution.py:232
  83.6 1.4 %place.1 = (bf16[128,16,128]{2,1,0:T(8,128)(2,1)}, f32[128,384]{1,0:T(8,128)S(1)}, bf16[128,384]{1,0:T(8,128)(2,1)S(1)}) custom-call(s32[32]{0:T(128)S(1)} %select_reduce_fusion.1.slots, f32[512,128]{1,0:T(8,128)S(1)} %get-tuple-element.27.mine, bf16[512,128]{1,0:T(8,128)(2,1)S(1)} %collective-permute-done.5.theirs, f32[128,384]{1,0:T(8,128)S(1)} %get-tuple-element.29.own, ...), custom_call_target="tpu_custom_call" | custom-call | tf_op jit(solution)/shard_map/place/pallas_call | solution.py:179
  85.0 5.0 %all-to-all-start.2 = ((bf16[8,256,128]{2,1,0:T(8,128)(2,1)}), bf16[8,256,128]{2,1,0:T(8,128)(2,1)S(1)}, u32[]{:S(2)}, u32[]{:S(2)}) async-start(bf16[8,256,128]{2,1,0:T(8,128)(2,1)} %bitcast.6), calls=%async_computation.2 | async-start | bytes 1048576 | tf_op jit(solution)/shard_map/all_to_all | solution.py:218
  90.0 1.3 %collective-permute-start.8 = (bf16[128,384]{1,0:T(8,128)(2,1)S(1)}, bf16[128,384]{1,0:T(8,128)(2,1)S(1)}, u32[]{:S(2)}, u32[]{:S(2)}) collective-permute-start(bf16[128,384]{1,0:T(8,128)(2,1)S(1)} %get-tuple-element.35), channel_id=1, source_target_pairs={{16,0},{20,4},{24,8},{28,12},{32,16},{36,20},{40,24},{44,28},{48,3... | collective-permute-start | bytes 294920 | tf_op jit(solution)/shard_map/ppermute | solution.py:228
  91.3 2.8 %collective-permute-start.7 = (bf16[128,384]{1,0:T(8,128)(2,1)S(1)}, bf16[128,384]{1,0:T(8,128)(2,1)S(1)}, u32[]{:S(2)}, u32[]{:S(2)}) collective-permute-start(bf16[128,384]{1,0:T(8,128)(2,1)S(1)} %get-tuple-element.34), channel_id=1, source_target_pairs={{4,0},{8,4},{12,8},{16,12},{20,16},{24,20},{28,24},{32,28},{36,32}... | collective-permute-start | bytes 294920 | tf_op jit(solution)/shard_map/ppermute | solution.py:228
  94.1 2.4 %collective-permute-done.8.far4 = bf16[128,384]{1,0:T(8,128)(2,1)S(1)} collective-permute-done((bf16[128,384]{1,0:T(8,128)(2,1)S(1)}, bf16[128,384]{1,0:T(8,128)(2,1)S(1)}, u32[]{:S(2)}, u32[]{:S(2)}) %collective-permute-start.8) | collective-permute-done | bytes 98336 | tf_op jit(solution)/shard_map/ppermute | solution.py:228
  96.5 3.4 %collective-permute-done.7.passed = bf16[128,384]{1,0:T(8,128)(2,1)S(1)} collective-permute-done((bf16[128,384]{1,0:T(8,128)(2,1)S(1)}, bf16[128,384]{1,0:T(8,128)(2,1)S(1)}, u32[]{:S(2)}, u32[]{:S(2)}) %collective-permute-start.7) | collective-permute-done | bytes 98336 | tf_op jit(solution)/shard_map/ppermute | solution.py:228
  99.9 1.3 %column.1 = (f32[256,128]{1,0:T(8,128)}, f32[64,384]{1,0:T(8,128)S(1)}, bf16[64,384]{1,0:T(8,128)(2,1)S(1)}) custom-call(s32[2]{0:T(128)S(1)} %pad_add_fusion.place, bf16[8,256,128]{2,1,0:T(8,128)(2,1)S(1)} %all-to-all-done.2.landed, f32[128,384]{1,0:T(8,128)S(1)} %get-tuple-element.33.partial, bf16[128,384]{1,0:T(8,128)(2,1)S(1)} %collective-permute-done.7.passed, ...), custom_call_target="tpu_custom_call" | custom-call | tf_op jit(solution)/shard_map/column/pallas_call | solution.py:179
  101.2 8.5 %all-to-all-start.3 = ((f32[16,16,128]{2,1,0:T(8,128)}), f32[16,16,128]{2,1,0:T(8,128)S(1)}, u32[]{:S(2)}, u32[]{:S(2)}) async-start(f32[16,16,128]{2,1,0:T(8,128)} %bitcast.9), calls=%async_computation.3 | async-start | bytes 262144 | tf_op jit(solution)/shard_map/all_to_all | solution.py:218
  109.7 4.6 %collective-permute-start.9 = (bf16[64,384]{1,0:T(8,128)(2,1)S(1)}, bf16[64,384]{1,0:T(8,128)(2,1)S(1)}, u32[]{:S(2)}, u32[]{:S(2)}) collective-permute-start(bf16[64,384]{1,0:T(8,128)(2,1)S(1)} %get-tuple-element.37), channel_id=1, source_target_pairs={{0,2},{2,0},{1,3},{3,1},{4,6},{6,4},{5,7},{7,5},{8,10},{10,8},{9,1... | collective-permute-start | bytes 147464 | tf_op jit(solution)/shard_map/ppermute | solution.py:232
  114.3 2.8 %collective-permute-done.9 = bf16[64,384]{1,0:T(8,128)(2,1)S(1)} collective-permute-done((bf16[64,384]{1,0:T(8,128)(2,1)S(1)}, bf16[64,384]{1,0:T(8,128)(2,1)S(1)}, u32[]{:S(2)}, u32[]{:S(2)}) %collective-permute-start.9) | collective-permute-done | bytes 49184 | tf_op jit(solution)/shard_map/ppermute | solution.py:232
  117.2 0.6 add_convert_fusion
  117.8 5.0 %all-to-all-done.3 = f32[16,16,128]{2,1,0:T(8,128)S(1)} async-done(((f32[16,16,128]{2,1,0:T(8,128)}), f32[16,16,128]{2,1,0:T(8,128)S(1)}, u32[]{:S(2)}, u32[]{:S(2)}) %all-to-all-start.3) | async-done | bytes 131104 | tf_op jit(solution)/shard_map/all_to_all | solution.py:218
  122.8 0.7 convert_element_type.16
  (16 shorter events, 0.1 us)
Async XLA Ops:
  2.1 27.9 %all-to-all-start = ((bf16[16,16,128]{2,1,0:T(8,128)(2,1)}), bf16[16,16,128]{2,1,0:T(8,128)(2,1)S(1)}, u32[]{:S(2)}, u32[]{:S(2)}) async-start(bf16[16,16,128]{2,1,0:T(8,128)(2,1)} %broadcast_in_dim.72), calls=%async_computation | async-start | bytes 131072 | tf_op jit(solution)/shard_map/all_to_all | solution.py:218
  17.3 0.8 copy-start.3
  17.3 0.7 copy-start.4
  30.9 19.5 %all-to-all-start.1 = ((bf16[8,256,128]{2,1,0:T(8,128)(2,1)}), bf16[8,256,128]{2,1,0:T(8,128)(2,1)S(1)}, u32[]{:S(2)}, u32[]{:S(2)}) async-start(bf16[8,256,128]{2,1,0:T(8,128)(2,1)} %get-tuple-element.21), calls=%async_computation.1 | async-start | bytes 1048576 | tf_op jit(solution)/shard_map/all_to_all | solution.py:218
  36.5 0.7 copy-start.5
  37.4 22.2 %collective-permute-start.3 = (bf16[2,128,384]{2,1,0:T(8,128)(2,1)S(1)}, bf16[2,128,384]{2,1,0:T(8,128)(2,1)S(1)}, u32[]{:S(2)}, u32[]{:S(2)}) collective-permute-start(bf16[2,128,384]{2,1,0:T(8,128)(2,1)S(1)} %get-tuple-element.22.near0), channel_id=1, source_target_pairs={{0,16},{4,20},{8,24},{12,28},{16,32},{20,36},{24,40},{28,44},{32,4... | collective-permute-start | bytes 589832 | tf_op jit(solution)/shard_map/ppermute | solution.py:228
  40.0 19.5 %collective-permute-start.2 = (bf16[2,128,384]{2,1,0:T(8,128)(2,1)S(1)}, bf16[2,128,384]{2,1,0:T(8,128)(2,1)S(1)}, u32[]{:S(2)}, u32[]{:S(2)}) collective-permute-start(bf16[2,128,384]{2,1,0:T(8,128)(2,1)S(1)} %get-tuple-element.22.near0), channel_id=1, source_target_pairs={{0,12},{4,16},{8,20},{12,24},{16,28},{20,32},{24,36},{28,40},{32,4... | collective-permute-start | bytes 589832 | tf_op jit(solution)/shard_map/ppermute | solution.py:228
  43.2 16.3 %collective-permute-start.1 = (bf16[2,128,384]{2,1,0:T(8,128)(2,1)S(1)}, bf16[2,128,384]{2,1,0:T(8,128)(2,1)S(1)}, u32[]{:S(2)}, u32[]{:S(2)}) collective-permute-start(bf16[2,128,384]{2,1,0:T(8,128)(2,1)S(1)} %get-tuple-element.22.near0), channel_id=1, source_target_pairs={{0,8},{4,12},{8,16},{12,20},{16,24},{20,28},{24,32},{28,36},{32,40... | collective-permute-start | bytes 589832 | tf_op jit(solution)/shard_map/ppermute | solution.py:228
  45.8 13.7 %collective-permute-start = (bf16[2,128,384]{2,1,0:T(8,128)(2,1)S(1)}, bf16[2,128,384]{2,1,0:T(8,128)(2,1)S(1)}, u32[]{:S(2)}, u32[]{:S(2)}) collective-permute-start(bf16[2,128,384]{2,1,0:T(8,128)(2,1)S(1)} %get-tuple-element.22.near0), channel_id=1, source_target_pairs={{0,4},{4,8},{8,12},{12,16},{16,20},{20,24},{24,28},{28,32},{32,36}... | collective-permute-start | bytes 589832 | tf_op jit(solution)/shard_map/ppermute | solution.py:228
  51.0 8.6 %copy-start = (bf16[384,128]{1,0:T(8,128)(2,1)S(1)}, bf16[384,128]{1,0:T(8,128)(2,1)}, u32[]{:S(2)}) copy-start(bf16[384,128]{1,0:T(8,128)(2,1)} %q.1) | copy-start | bytes 294916
  51.0 8.6 %copy-start.1 = (bf16[384,128]{1,0:T(8,128)(2,1)S(1)}, bf16[384,128]{1,0:T(8,128)(2,1)}, u32[]{:S(2)}) copy-start(bf16[384,128]{1,0:T(8,128)(2,1)} %o.1) | copy-start | bytes 294916
  51.0 8.6 %copy-start.2 = (bf16[384,128]{1,0:T(8,128)(2,1)S(1)}, bf16[384,128]{1,0:T(8,128)(2,1)}, u32[]{:S(2)}) copy-start(bf16[384,128]{1,0:T(8,128)(2,1)} %do.1) | copy-start | bytes 294916
  65.9 4.1 %collective-permute-start.4 = (bf16[2944,128]{1,0:T(8,128)(2,1)S(1)}, bf16[2944,128]{1,0:T(8,128)(2,1)S(1)}, u32[]{:S(2)}, u32[]{:S(2)}) collective-permute-start(bf16[2944,128]{1,0:T(8,128)(2,1)S(1)} %get-tuple-element.26), channel_id=1, source_target_pairs={{0,1},{1,0},{2,3},{3,2},{4,5},{5,4},{6,7},{7,6},{8,9},{9,8},{10,11... | collective-permute-start | bytes 2261000 | tf_op jit(solution)/shard_map/ppermute | solution.py:232
  70.8 12.8 %collective-permute-start.6 = (bf16[256,384]{1,0:T(8,128)(2,1)S(1)}, bf16[256,384]{1,0:T(8,128)(2,1)S(1)}, u32[]{:S(2)}, u32[]{:S(2)}) collective-permute-start(bf16[256,384]{1,0:T(8,128)(2,1)S(1)} %get-tuple-element.31), channel_id=1, source_target_pairs={{8,0},{12,4},{16,8},{20,12},{24,16},{28,20},{32,24},{36,28},{40,32... | collective-permute-start | bytes 589832 | tf_op jit(solution)/shard_map/ppermute | solution.py:228
  74.7 8.9 %collective-permute-start.5 = (bf16[512,128]{1,0:T(8,128)(2,1)S(1)}, bf16[512,128]{1,0:T(8,128)(2,1)S(1)}, u32[]{:S(2)}, u32[]{:S(2)}) collective-permute-start(bf16[512,128]{1,0:T(8,128)(2,1)S(1)} %get-tuple-element.28), channel_id=1, source_target_pairs={{0,2},{2,0},{1,3},{3,1},{4,6},{6,4},{5,7},{7,5},{8,10},{10,8},{9,1... | collective-permute-start | bytes 393224 | tf_op jit(solution)/shard_map/ppermute | solution.py:232
  85.0 14.9 %all-to-all-start.2 = ((bf16[8,256,128]{2,1,0:T(8,128)(2,1)}), bf16[8,256,128]{2,1,0:T(8,128)(2,1)S(1)}, u32[]{:S(2)}, u32[]{:S(2)}) async-start(bf16[8,256,128]{2,1,0:T(8,128)(2,1)} %bitcast.6), calls=%async_computation.2 | async-start | bytes 1048576 | tf_op jit(solution)/shard_map/all_to_all | solution.py:218
  90.0 6.5 %collective-permute-start.8 = (bf16[128,384]{1,0:T(8,128)(2,1)S(1)}, bf16[128,384]{1,0:T(8,128)(2,1)S(1)}, u32[]{:S(2)}, u32[]{:S(2)}) collective-permute-start(bf16[128,384]{1,0:T(8,128)(2,1)S(1)} %get-tuple-element.35), channel_id=1, source_target_pairs={{16,0},{20,4},{24,8},{28,12},{32,16},{36,20},{40,24},{44,28},{48,3... | collective-permute-start | bytes 294920 | tf_op jit(solution)/shard_map/ppermute | solution.py:228
  91.3 8.6 %collective-permute-start.7 = (bf16[128,384]{1,0:T(8,128)(2,1)S(1)}, bf16[128,384]{1,0:T(8,128)(2,1)S(1)}, u32[]{:S(2)}, u32[]{:S(2)}) collective-permute-start(bf16[128,384]{1,0:T(8,128)(2,1)S(1)} %get-tuple-element.34), channel_id=1, source_target_pairs={{4,0},{8,4},{12,8},{16,12},{20,16},{24,20},{28,24},{32,28},{36,32}... | collective-permute-start | bytes 294920 | tf_op jit(solution)/shard_map/ppermute | solution.py:228
  101.2 21.6 %all-to-all-start.3 = ((f32[16,16,128]{2,1,0:T(8,128)}), f32[16,16,128]{2,1,0:T(8,128)S(1)}, u32[]{:S(2)}, u32[]{:S(2)}) async-start(f32[16,16,128]{2,1,0:T(8,128)} %bitcast.9), calls=%async_computation.3 | async-start | bytes 262144 | tf_op jit(solution)/shard_map/all_to_all | solution.py:218
  109.7 7.5 %collective-permute-start.9 = (bf16[64,384]{1,0:T(8,128)(2,1)S(1)}, bf16[64,384]{1,0:T(8,128)(2,1)S(1)}, u32[]{:S(2)}, u32[]{:S(2)}) collective-permute-start(bf16[64,384]{1,0:T(8,128)(2,1)S(1)} %get-tuple-element.37), channel_id=1, source_target_pairs={{0,2},{2,0},{1,3},{3,1},{4,6},{6,4},{5,7},{7,5},{8,10},{10,8},{9,1... | collective-permute-start | bytes 147464 | tf_op jit(solution)/shard_map/ppermute | solution.py:232
